TPU v7x, 256 devices: a whole 4x4x8 slice. The times are simulated.
256 devices in a mesh: seq: 32 (over x_hi, z, core), tp: 8 (over y, x_lo).
Axes of the slice: x: 4 (x_hi: 2, x_lo: 2; x = x_hi * 2 + x_lo), y: 4, z: 8, core: 2. Of those that a mesh axis runs over, the one named last changes fastest.
Arguments:
- projected: bfloat16 [3, 4096, 8192], P(None, 'tp', 'seq'), may hold values from -12 to 12
- filter_taps: bfloat16 [4096, 8192], P('tp', 'seq'), may hold values from -2.5 to 2.5
- short_weight: float32 [3, 4096, 3], P(None, 'tp'), may hold values from -3 to 3
- skip_bias: float32 [4096], P('tp'), may hold values from -3 to 3
- norm_gain: float32 [4096], replicated, may hold values from 0.1 to 1.9
- gate_weight: bfloat16 [5632, 4096], P(('seq', 'tp')), may hold values from -0.09375 to 0.09375
- up_weight: bfloat16 [5632, 4096], P(('seq', 'tp')), may hold values from -0.09375 to 0.09375
- down_weight: bfloat16 [5632, 4096], P(('seq', 'tp')), may hold values from -0.078125 to 0.078125
Outputs:
- mixed: bfloat16 [4096, 8192], P('tp', 'seq')
All inputs are finite; a program needn't handle non-finite values.
Results may differ from a plain program's by a relative error of at most 0.018.
Values may be sent and summed in bfloat16 or wider, within the bound.
No kernel may reach another device: no remote copies, remote signals or barrier semaphores. Data moves between devices by JAX's collectives and lax.ppermute only.
A program may use at most 128 MiB of HBM per device.

v0:
```python
import jax
import jax.numpy as jnp
from jax import lax
from jax.experimental import pallas as pl
from jax.experimental.pallas import tpu as pltpu
from jax.sharding import Mesh
from jax.sharding import PartitionSpec as P

EPSILON = 1e-06
LANES = 128
SEQ = ("xh", "z", "core")
TP = ("y", "xl")


def short_filter(signal, weights, leading):
    extent = signal.shape[2]
    padded = jnp.concatenate([leading, signal], axis=2)
    return (
        weights[:, :, 0:1] * padded[:, :, 2:]
        + weights[:, :, 1:2] * padded[:, :, 1 : extent + 1]
        + weights[:, :, 2:3] * padded[:, :, 0:extent]
    )


def build_table(taps_ref, channel, table_ref):
    seq_len = taps_ref.shape[2]
    base = jnp.broadcast_to(taps_ref[channel].astype(jnp.float32), (8, seq_len))
    base = pltpu.roll(base, 0, 1, stride=1, stride_axis=0)
    lane = lax.broadcasted_iota(jnp.int32, (8, seq_len), 1)
    row = lax.broadcasted_iota(jnp.int32, (8, seq_len), 0)
    base = jnp.where(lane >= row, base, 0.0)
    for pair in range(LANES // 16):
        parts = []
        for shift in (16 * pair, 16 * pair + 8):
            moved = pltpu.roll(base, shift, 1) if shift else base
            parts.append(jnp.where(lane >= shift, moved, 0.0) if shift else moved)
        table_ref[16 * pair : 16 * pair + 16, :] = jnp.concatenate(parts, axis=0).astype(jnp.bfloat16)

def apply_table(gated_ref, bias_ref, channel, table_ref, out_ref):
    rows = gated_ref.shape[1]
    gated = gated_ref[channel].astype(jnp.float32)
    tiles = rows // 8
    left = []
    for skip in range(tiles):
        keep = rows - 8 * skip
        left.append(jnp.concatenate([gated[:keep, :LANES], gated[:keep, LANES:]], axis=0).astype(jnp.bfloat16))
    zero = jnp.zeros((8, LANES), jnp.float32)
    total = [[zero] * tiles, [zero] * tiles]
    row = lax.broadcasted_iota(jnp.int32, (rows, LANES), 0)
    carried = [zero] * tiles
    for rho in range(8):
        sums = [carried, [zero] * tiles]
        carried = [zero] * tiles
        for skip in range(tiles):
            step = 8 * skip + rho
            keep = rows - 8 * skip
            part = jnp.dot(left[skip], table_ref[:, 2 * LANES * step : 2 * LANES * (step + 1)], preferred_element_type=jnp.float32)
            for lane_half in range(2):
                for row_half in range(2):
                    move = (2 * step + lane_half + row_half) // 2
                    if move >= rows: continue
                    side = (lane_half + row_half) % 2
                    target = sums[side] if move == step else carried
                    first = move // 8
                    for tile in range(tiles - first):
                        start = row_half * keep + 8 * tile
                        target[tile + first] = target[tile + first] + part[start:start + 8, lane_half * LANES:(lane_half + 1) * LANES]
        for side in range(2):
            if rho == 0:
                moved = sums[side]
            else:
                moved = jnp.concatenate(sums[side], axis=0)
                moved = jnp.where(row >= rho, pltpu.roll(moved, rho, 0), 0.0)
                moved = [moved[8*t:8*t+8] for t in range(tiles)]
            total[side] = [a + b for a, b in zip(total[side], moved)]
    total[0] = [a + b for a, b in zip(total[0], carried)]
    whole = jnp.concatenate([jnp.concatenate(total[0], axis=0), jnp.concatenate(total[1], axis=0)], axis=1)
    out_ref[channel] = (whole + bias_ref[channel] * gated).astype(jnp.bfloat16)

def conv_kernel(bias_ref, gated_ref, taps_ref, out_ref, even_ref, odd_ref):
    channels = gated_ref.shape[0]
    build_table(taps_ref, 0, even_ref)
    def body(step, carry):
        channel = 2 * step
        build_table(taps_ref, channel + 1, odd_ref)
        apply_table(gated_ref, bias_ref, channel, even_ref, out_ref)
        build_table(taps_ref, lax.rem(channel + 2, channels), even_ref)
        apply_table(gated_ref, bias_ref, channel + 1, odd_ref, out_ref)
        return carry
    lax.fori_loop(0, channels // 2, body, 0)

def long_mixing(gated, taps, bias):
    channels, rows, width = gated.shape
    seq_len = rows * width
    return pl.pallas_call(conv_kernel,
        out_shape=jax.ShapeDtypeStruct(gated.shape, jnp.bfloat16),
        in_specs=[pl.BlockSpec(memory_space=pltpu.SMEM), pl.BlockSpec(memory_space=pltpu.VMEM), pl.BlockSpec(memory_space=pltpu.VMEM)],
        out_specs=pl.BlockSpec(memory_space=pltpu.VMEM),
        scratch_shapes=[pltpu.VMEM((LANES, seq_len), jnp.bfloat16)]*2,
        compiler_params=pltpu.CompilerParams(vmem_limit_bytes=24*1024*1024),
        cost_estimate=pl.CostEstimate(flops=2*channels*seq_len*seq_len, bytes_accessed=6*channels*seq_len, transcendentals=0),
        name="long_mixing")(bias, gated, taps.reshape(channels, 1, seq_len))


def padded_rows(weight):
    rows = weight.shape[0]
    return jnp.pad(weight, ((0, -rows % 8), (0, 0)))


def swap(values, axis):
    return lax.ppermute(values, axis, [(0, 1), (1, 0)])


def spread_part(own, part, parts):
    size = own.shape[0] // (2 * parts)
    core = lax.axis_index("core")
    return lax.dynamic_slice_in_dim(own, (core * parts + part) * size, size, 0)


def down_product(weight, hidden):
    return lax.dot_general(
        weight, hidden, (((0,), (0,)), ((), ())), preferred_element_type=jnp.float32
    )


def per_device(
    projected, filter_taps, short_weight, skip_bias, norm_gain, gate_weight, up_weight, down_weight
):
    groups = lax.axis_size(SEQ)
    members = lax.axis_size(TP)
    local_width, block_len = filter_taps.shape
    per_group = local_width // groups
    seq_len = groups * block_len
    offset = lax.axis_index(SEQ) * per_group
    bias_part = lax.dynamic_slice_in_dim(skip_bias, offset, per_group, 0)

    edge = lax.ppermute(
        projected[:, :, block_len - 2 :].transpose(0, 2, 1).reshape(6, local_width),
        SEQ,
        [(i, i + 1) for i in range(groups - 1)],
    )
    edge = edge.reshape(3, 2, local_width).transpose(0, 2, 1)
    shorts = short_filter(
        projected.astype(jnp.float32), short_weight, edge.astype(jnp.float32)
    )
    query = shorts[0]
    gated = (shorts[1] * shorts[2]).astype(jnp.bfloat16)
    sent = jnp.stack([gated, filter_taps]).reshape(2, groups, per_group, block_len)
    here = lax.all_to_all(
        sent.transpose(1, 0, 2, 3), SEQ, split_axis=0, concat_axis=0, tiled=True
    )

    own_pair = jnp.concatenate([padded_rows(gate_weight), padded_rows(up_weight)], axis=0)
    other_pair = swap(own_pair, "xh")
    down_own = lax.all_gather(padded_rows(down_weight), ("z", "core"), axis=0, tiled=True)
    here, own_pair, other_pair = lax.optimization_barrier((here, own_pair, other_pair))
    gate_up = lax.all_gather(
        jnp.concatenate([own_pair, other_pair], axis=0), ("z", "core"), axis=0, tiled=True
    )

    here = here.transpose(1, 2, 0, 3)
    mixed_term = long_mixing(here[0], here[1].reshape(per_group, seq_len), bias_part)
    returned = mixed_term.transpose(1, 0, 2)
    first, second = spread_part(down_own, 0, 2), spread_part(down_own, 1, 2)
    returned, first, second = lax.optimization_barrier((returned, first, second))
    near_first = swap(first, "xh")
    returned = lax.all_to_all(returned, SEQ, split_axis=0, concat_axis=0, tiled=True)
    hyena = (query * returned.reshape(local_width, block_len).astype(jnp.float32)).astype(
        jnp.bfloat16
    )

    hyena, near_first, second = lax.optimization_barrier((hyena, near_first, second))
    near_second = swap(second, "xh")
    copies = jnp.broadcast_to(hyena[None], (members, local_width, block_len))
    whole = lax.all_to_all(copies, TP, split_axis=0, concat_axis=0, tiled=True)
    whole = whole.reshape(members * local_width, block_len)
    wide = whole.astype(jnp.float32)
    mean_square = jnp.mean(wide * wide, axis=0)
    normed = (wide * lax.rsqrt(mean_square + EPSILON)[None, :] * norm_gain[:, None]).astype(
        jnp.bfloat16
    )
    sums = jnp.dot(gate_up, normed, preferred_element_type=jnp.float32)
    sums = sums.reshape(-1, 2, 2, own_pair.shape[0] // 2, block_len)
    hidden = (jax.nn.silu(sums[:, :, 0]) * sums[:, :, 1]).astype(jnp.bfloat16)
    hidden_own = hidden[:, 0].reshape(-1, block_len)
    hidden_other = hidden[:, 1].reshape(-1, block_len)
    partial_sum = down_product(down_own, hidden_own)
    core = lax.axis_index("core")
    for part, near in enumerate((near_first, near_second)):
        size = near.shape[0]
        for side, rows in ((core, near), (1 - core, swap(near, "core"))):
            chosen = lax.dynamic_slice_in_dim(hidden_other, (side * 2 + part) * size, size, 0)
            partial_sum += down_product(rows, chosen)
    partial_sum = partial_sum.astype(jnp.bfloat16)
    shares = lax.all_to_all(
        partial_sum.reshape(members, local_width, block_len),
        TP,
        split_axis=0,
        concat_axis=0,
        tiled=True,
    )
    feed_out = jnp.sum(shares.astype(jnp.float32), axis=0)
    return (hyena.astype(jnp.float32) + feed_out).astype(jnp.bfloat16)


def solution(mesh):
    fine = Mesh(mesh.devices.reshape(2, 8, 2, 4, 2), SEQ + TP)
    placed = (
        P(None, TP, SEQ),
        P(TP, SEQ),
        P(None, TP, None),
        P(TP),
        P(),
        P(SEQ + TP, None),
        P(SEQ + TP, None),
        P(SEQ + TP, None),
    )
    return jax.shard_map(
        per_device, mesh=fine, in_specs=placed, out_specs=P(TP, SEQ), check_vma=False
    )
```

profile of v0, /device:TPU:1, one launch (start us, length us, event | category | flops | bytes accessed | tf_op | source)
XLA Modules:
  0.0 206.1 jit_solution(11110737545386169026)
XLA Ops:
  6.5 1.7 pad.12
  8.3 1.2 slice_bitcast_fusion.3
  9.6 4.9 %collective-permute-start = (bf16[6,512]{1,0:T(8,128)(2,1)S(1)}, bf16[6,512]{1,0:T(8,128)(2,1)S(1)}, u32[]{:S(2)}, u32[]{:S(2)}) collective-permute-start(bf16[6,512]{1,0:T(8,128)(2,1)S(1)} %reshape.37), channel_id=1, source_target_pairs={{0,8},{8,16},{16,24},{24,32},{32,40},{40,48},{48,56},{56,64},{64,7... | collective-permute-start | bytes 18440 | tf_op jit(solution)/shard_map/ppermute | solution.py:137
  14.6 0.9 fusion.29
  15.7 1.2 copy.18
  16.8 3.0 %fusion.8 = f32[3,512,256]{2,1,0:T(8,128)S(1)} fusion(f32[3,512,2]{2,1,0:T(8,128)} %copy.18, f32[3,512,256]{2,1,0:T(8,128)S(1)} %convert_element_type.55, f32[3,512]{1,0:T(4,128)S(1)} %get-tuple-element.32, f32[3,512]{1,0:T(4,128)S(1)} %get-tuple-element.33, f32[3,512]{1,0:T(4,128)S(1)} %bitcast.72), kind=kLoop, calls=%fused_computation.16 | loop fusion | flops 2752512 | bytes 3176448 | tf_op jit(solution)/shard_map/add | solution.py:19
  20.0 0.9 copy.19
  20.9 12.8 %all-to-all-start = ((bf16[32,2,16,256]{3,2,1,0:T(8,128)(2,1)}), bf16[32,2,16,256]{3,2,1,0:T(8,128)(2,1)S(1)}, u32[]{:S(2)}, u32[]{:S(2)}) async-start(bf16[32,2,16,256]{3,2,1,0:T(8,128)(2,1)} %copy.19), calls=%async_computation | async-start | bytes 1048576 | tf_op jit(solution)/shard_map/all_to_all | solution.py:149
  33.7 3.0 %collective-permute-start.1 = (bf16[48,4096]{1,0:T(8,128)(2,1)S(1)}, bf16[48,4096]{1,0:T(8,128)(2,1)S(1)}, u32[]{:S(2)}, u32[]{:S(2)}) collective-permute-start(bf16[48,4096]{1,0:T(8,128)(2,1)S(1)} %fusion.17), channel_id=1, source_target_pairs={{0,128},{128,0},{1,129},{129,1},{2,130},{130,2},{3,131},{131,3},{4... | collective-permute-start | bytes 1179656 | tf_op jit(solution)/shard_map/ppermute | solution.py:111
  36.7 12.8 %collective-permute-done.1 = bf16[48,4096]{1,0:T(8,128)(2,1)S(1)} collective-permute-done((bf16[48,4096]{1,0:T(8,128)(2,1)S(1)}, bf16[48,4096]{1,0:T(8,128)(2,1)S(1)}, u32[]{:S(2)}, u32[]{:S(2)}) %collective-permute-start.1) | collective-permute-done | bytes 393248 | tf_op jit(solution)/shard_map/ppermute | solution.py:111
  49.5 7.8 %all-to-all-done = bf16[32,2,16,256]{3,2,1,0:T(8,128)(2,1)S(1)} async-done(((bf16[32,2,16,256]{3,2,1,0:T(8,128)(2,1)}), bf16[32,2,16,256]{3,2,1,0:T(8,128)(2,1)S(1)}, u32[]{:S(2)}, u32[]{:S(2)}) %all-to-all-start) | async-done | bytes 524320 | tf_op jit(solution)/shard_map/all_to_all | solution.py:149
  57.3 1.0 pad_maximum_fusion.1
  58.3 0.8 dynamic_slice.21.bias_ref
  59.5 14.4 %long_mixing.1 = bf16[16,32,256]{2,1,0:T(8,128)(2,1)S(1)} custom-call(f32[16]{0:T(128)S(1)} %dynamic_slice.21.bias_ref, bf16[16,32,256]{2,1,0:T(8,128)(2,1)S(1)} %get-tuple-element.26.gated_ref, bf16[16,1,8192]{2,1,0:T(2,128)(2,1)S(1)} %reshape_reshape_squeeze.4.taps_ref), custom_call_target="tpu_custom_call" | custom-call | flops 2147483648 | bytes 786432 | tf_op jit(solution)/shard_map/long_mixing/pallas_call | solution.py:95
  74.0 2.4 %constant_dynamic-slice_fusion = (bf16[96,4096]{1,0:T(8,128)(2,1)}, bf16[96,4096]{1,0:T(8,128)(2,1)S(1)}) fusion(bf16[384,4096]{1,0:T(8,128)(2,1)} %all-gather.3.cloned.1.call-done, s32[]{:T(128)S(6)} %select_n.19, s32[]{:T(128)S(6)} %select_n.18), kind=kLoop, calls=%fused_computation.51 | loop fusion | bytes 3145736 | tf_op jit(solution)/shard_map/dynamic_slice | solution.py:117
  76.9 23.2 %all_to_all.20 = bf16[32,16,256]{2,1,0:T(8,128)(2,1)S(1)} all-to-all(bf16[32,16,256]{2,1,0:T(8,128)(2,1)S(1)} %copy.22), channel_id=1, replica_groups=mesh['xh'=2,'z'=8,'core'=2,'y'=4,'xl'=2] {'xh','z','core'}, dimensions={0} | all-to-all | bytes 524288 | tf_op jit(solution)/shard_map/all_to_all | solution.py:167
  100.2 1.4 broadcast_in_dim.2
  101.7 5.0 %all-to-all-start.2 = ((bf16[8,512,256]{2,1,0:T(8,128)(2,1)}), bf16[8,512,256]{2,1,0:T(8,128)(2,1)S(1)}, u32[]{:S(2)}, u32[]{:S(2)}) async-start(bf16[8,512,256]{2,1,0:T(8,128)(2,1)} %broadcast_in_dim.2), calls=%async_computation.2 | async-start | bytes 4194304 | tf_op jit(solution)/shard_map/all_to_all | solution.py:175
  106.7 0.9 collective-permute-start.4
  107.6 1.1 collective-permute-start.3
  108.6 39.1 %collective-permute-done.4 = bf16[96,4096]{1,0:T(8,128)(2,1)} collective-permute-done((bf16[96,4096]{1,0:T(8,128)(2,1)}, bf16[96,4096]{1,0:T(8,128)(2,1)}, u32[]{:S(2)}, u32[]{:S(2)}) %collective-permute-start.4) | collective-permute-done | bytes 786464 | tf_op jit(solution)/shard_map/ppermute | solution.py:111
  147.8 1.4 collective-permute-start.5
  149.2 0.6 fusion.2
  149.7 1.7 fusion.4
  151.4 7.2 %fusion.30 = f32[16,2,2,24,256]{4,3,2,1,0:T(8,128)S(1)} fusion(bf16[16,2,2,24,4096]{4,3,2,1,0:T(8,128)(2,1)} %bitcast.73, bf16[4096,256,1,1,1]{1,0,4,3,2:T(8,128)(2,1)} %bitcast.62), kind=kOutput, calls=%fused_computation.57 | convolution fusion | flops 3221225472 | bytes 16252928 | tf_op jit(solution)/shard_map/dot_general | solution.py:182
  158.9 1.3 fusion.31
  160.2 0.8 convolution_add_fusion.2
  161.0 1.9 fusion.19
  162.9 1.9 fusion
  164.9 1.9 fusion.1
  166.8 31.4 %all_to_all.21 = bf16[8,512,256]{2,1,0:T(8,128)(2,1)S(1)} all-to-all(bf16[8,512,256]{2,1,0:T(8,128)(2,1)S(1)} %bitcast.61), channel_id=1, replica_groups=mesh['xh'=2,'z'=8,'core'=2,'y'=4,'xl'=2] {'y','xl'}, dimensions={0} | all-to-all | bytes 4194304 | tf_op jit(solution)/shard_map/all_to_all | solution.py:195
  198.5 0.8 add_convert_fusion
  (43 shorter events, 2.2 us)
Async XLA Ops:
  6.5 8.9 %copy-start.1 = (bf16[3,512,256]{2,1,0:T(8,128)(2,1)S(1)}, bf16[3,512,256]{2,1,0:T(8,128)(2,1)}, u32[]{:S(2)}) copy-start(bf16[3,512,256]{2,1,0:T(8,128)(2,1)} %param.8) | copy-start | bytes 2359300
  6.5 67.5 %all-gather.3.cloned.1.call-start = ((), (), s32[]{:S(2)}) async-start(), calls=%async_computation.4 | async-start | bytes 3342336 | tf_op jit(solution)/shard_map/all_gather | solution.py:155
  9.6 6.0 %collective-permute-start = (bf16[6,512]{1,0:T(8,128)(2,1)S(1)}, bf16[6,512]{1,0:T(8,128)(2,1)S(1)}, u32[]{:S(2)}, u32[]{:S(2)}) collective-permute-start(bf16[6,512]{1,0:T(8,128)(2,1)S(1)} %reshape.37), channel_id=1, source_target_pairs={{0,8},{8,16},{16,24},{24,32},{32,40},{40,48},{48,56},{56,64},{64,7... | collective-permute-start | bytes 18440 | tf_op jit(solution)/shard_map/ppermute | solution.py:137
  16.8 3.1 %copy-start.2 = (bf16[512,256]{1,0:T(8,128)(2,1)S(1)}, bf16[512,256]{1,0:T(8,128)(2,1)}, u32[]{:S(2)}) copy-start(bf16[512,256]{1,0:T(8,128)(2,1)} %param.9) | copy-start | bytes 786436
  19.8 13.8 %copy-start.3 = (bf16[22,4096]{1,0:T(8,128)(2,1)S(1)}, bf16[22,4096]{1,0:T(8,128)(2,1)}, u32[]{:S(2)}) copy-start(bf16[22,4096]{1,0:T(8,128)(2,1)} %param.14) | copy-start | bytes 540676
  19.9 13.8 %copy-start.4 = (bf16[22,4096]{1,0:T(8,128)(2,1)S(1)}, bf16[22,4096]{1,0:T(8,128)(2,1)}, u32[]{:S(2)}) copy-start(bf16[22,4096]{1,0:T(8,128)(2,1)} %param.13) | copy-start | bytes 540676
  20.9 36.4 %all-to-all-start = ((bf16[32,2,16,256]{3,2,1,0:T(8,128)(2,1)}), bf16[32,2,16,256]{3,2,1,0:T(8,128)(2,1)S(1)}, u32[]{:S(2)}, u32[]{:S(2)}) async-start(bf16[32,2,16,256]{3,2,1,0:T(8,128)(2,1)} %copy.19), calls=%async_computation | async-start | bytes 1048576 | tf_op jit(solution)/shard_map/all_to_all | solution.py:149
  33.6 117.8 %all-gather.5.cloned.1.call-start = ((), (), s32[]{:S(2)}) async-start(), calls=%async_computation.5 | async-start | bytes 13369344 | tf_op jit(solution)/shard_map/all_gather | solution.py:157
  33.7 15.8 %collective-permute-start.1 = (bf16[48,4096]{1,0:T(8,128)(2,1)S(1)}, bf16[48,4096]{1,0:T(8,128)(2,1)S(1)}, u32[]{:S(2)}, u32[]{:S(2)}) collective-permute-start(bf16[48,4096]{1,0:T(8,128)(2,1)S(1)} %fusion.17), channel_id=1, source_target_pairs={{0,128},{128,0},{1,129},{129,1},{2,130},{130,2},{3,131},{131,3},{4... | collective-permute-start | bytes 1179656 | tf_op jit(solution)/shard_map/ppermute | solution.py:111
  76.4 23.8 %collective-permute-start.2 = (bf16[96,4096]{1,0:T(8,128)(2,1)S(1)}, bf16[96,4096]{1,0:T(8,128)(2,1)S(1)}, u32[]{:S(2)}, u32[]{:S(2)}) collective-permute-start(bf16[96,4096]{1,0:T(8,128)(2,1)S(1)} %get-tuple-element.16), channel_id=1, source_target_pairs={{0,128},{128,0},{1,129},{129,1},{2,130},{130,2},{3,131},{131,3},{4... | collective-permute-start | bytes 2359304 | tf_op jit(solution)/shard_map/ppermute | solution.py:111
  101.7 5.9 %copy-start.5 = (f32[4096]{0:T(1024)S(1)}, f32[4096]{0:T(1024)}, u32[]{:S(2)}) copy-start(f32[4096]{0:T(1024)} %param.12) | copy-start | bytes 49156
  101.7 47.5 %all-to-all-start.2 = ((bf16[8,512,256]{2,1,0:T(8,128)(2,1)}), bf16[8,512,256]{2,1,0:T(8,128)(2,1)S(1)}, u32[]{:S(2)}, u32[]{:S(2)}) async-start(bf16[8,512,256]{2,1,0:T(8,128)(2,1)} %broadcast_in_dim.2), calls=%async_computation.2 | async-start | bytes 4194304 | tf_op jit(solution)/shard_map/all_to_all | solution.py:175
  106.7 41.1 %collective-permute-start.4 = (bf16[96,4096]{1,0:T(8,128)(2,1)}, bf16[96,4096]{1,0:T(8,128)(2,1)}, u32[]{:S(2)}, u32[]{:S(2)}) collective-permute-start(bf16[96,4096]{1,0:T(8,128)(2,1)} %get-tuple-element.22), channel_id=1, source_target_pairs={{0,128},{128,0},{1,129},{129,1},{2,130},{130,2},{3,131},{131,3},{4... | collective-permute-start | bytes 2359304 | tf_op jit(solution)/shard_map/ppermute | solution.py:111
  107.6 55.4 %collective-permute-start.3 = (bf16[96,4096]{1,0:T(8,128)(2,1)S(1)}, bf16[96,4096]{1,0:T(8,128)(2,1)}, u32[]{:S(2)}, u32[]{:S(2)}) collective-permute-start(bf16[96,4096]{1,0:T(8,128)(2,1)S(1)} %collective-permute-done.2), channel_id=1, source_target_pairs={{0,8},{8,0},{1,9},{9,1},{2,10},{10,2},{3,11},{11,3},{4,12},{12,4},... | collective-permute-start | bytes 2359304 | tf_op jit(solution)/shard_map/ppermute | solution.py:111
  147.8 17.1 %collective-permute-start.5 = (bf16[96,4096]{1,0:T(8,128)(2,1)}, bf16[96,4096]{1,0:T(8,128)(2,1)}, u32[]{:S(2)}, u32[]{:S(2)}) collective-permute-start(bf16[96,4096]{1,0:T(8,128)(2,1)} %collective-permute-done.4), channel_id=1, source_target_pairs={{0,8},{8,0},{1,9},{9,1},{2,10},{10,2},{3,11},{11,3},{4,12},{12,4},... | collective-permute-start | bytes 2359304 | tf_op jit(solution)/shard_map/ppermute | solution.py:111
  151.4 7.5 %copy-start = (bf16[384,4096]{1,0:T(8,128)(2,1)S(1)}, bf16[384,4096]{1,0:T(8,128)(2,1)}, u32[]{:S(2)}) copy-start(bf16[384,4096]{1,0:T(8,128)(2,1)} %all-gather.3.cloned.1.call-done) | copy-start | bytes 9437188
Sparse Core Ops, SparseCore 0:
  9.2 52.1 all-gather.2
  63.3 80.0 all-gather.4
where the time goes:
time: 207 us; the launch traced here: 206 us
  waiting for transfers between devices  59.8 us (29%)
  blocking collectives  54.7 us (26%)
  starting transfers between devices  29.4 us (14%)
  matrix products  15 us (7%)
  Pallas kernels  14.4 us (7%)
  between operations  13.7 us (7%)
  local copies, waits for them, and re-layouts  11.3 us (5%)
  other arithmetic  7.84 us (4%)
    ppermute x5, waiting for transfers between devices, swap(): return lax.ppermute(values, axis, [(0, 1), (1, 0)])  51.9 us
    all_to_all x1, blocking collectives, per_device(): lax.all_to_all(partial_sum.reshape(members, local_width, block_len), TP,...  31.4 us
    all_to_all x1, blocking collectives, per_device(): lax.all_to_all(returned, SEQ, split_axis=0, concat_axis=0, tiled=True)  23.2 us
    pallas_call x1, Pallas kernels, long_mixing(): pl.pallas_call(conv_kernel, out_shape=jax.ShapeDtypeStruct(gated.shape, j...  14.4 us
    all_to_all x1, starting transfers between devices, per_device(): lax.all_to_all(sent.transpose(1, 0, 2, 3), SEQ, split_axis=0, concat_axis...  12.8 us
    dot_general x5, matrix products, down_product(): lax.dot_general(weight, hidden, (((0,), (0,)), ((), ())), preferred_eleme...  7.8 us
    all_to_all x1, waiting for transfers between devices, per_device(): lax.all_to_all(sent.transpose(1, 0, 2, 3), SEQ, split_axis=0, concat_axis...  7.78 us
    dot_general x1, matrix products, per_device(): sums = jnp.dot(gate_up, normed, preferred_element_type=jnp.float32)  7.21 us
  transfers between devices with their start and end apart: 10, of which 3 were waited for; matrix products, arithmetic and copies ran while one was open for 14% of the time, Pallas kernels for 7%

commit v1 on v0

--- a/solution.py
+++ b/solution.py
@@ -98,8 +98,150 @@
         out_specs=pl.BlockSpec(memory_space=pltpu.VMEM),
         scratch_shapes=[pltpu.VMEM((LANES, seq_len), jnp.bfloat16)]*2,
         compiler_params=pltpu.CompilerParams(vmem_limit_bytes=24*1024*1024),
-        cost_estimate=pl.CostEstimate(flops=2*channels*seq_len*seq_len, bytes_accessed=6*channels*seq_len, transcendentals=0),
+        cost_estimate=pl.CostEstimate(flops=8 * channels * seq_len * seq_len, bytes_accessed=6*channels*seq_len, transcendentals=0),
         name="long_mixing")(bias, gated, taps.reshape(channels, 1, seq_len))
+
+
+def pack_kernel(gate_ref, up_ref, other_ref, out_ref):
+    parts = [gate_ref[...], up_ref[...], other_ref[...]]
+    whole = jnp.concatenate([part.astype(jnp.float32) for part in parts], axis=0)
+    out_ref[...] = whole.astype(out_ref.dtype)
+
+
+def pack_rows(gate, up, other):
+    rows = gate.shape[0] + up.shape[0] + other.shape[0]
+    return pl.pallas_call(
+        pack_kernel,
+        out_shape=jax.ShapeDtypeStruct((rows, gate.shape[1]), gate.dtype),
+        name="pack_rows",
+    )(gate, up, other)
+
+
+def payload_kernel(query_ref, mixed_ref, gain_ref, hyena_ref, out_ref):
+    rows = query_ref.shape[0]
+    hyena = (query_ref[...] * mixed_ref[...].astype(jnp.float32)).astype(jnp.bfloat16)
+    hyena_ref[...] = hyena
+    wide = hyena.astype(jnp.float32)
+    scaled = (wide * gain_ref[...]).astype(jnp.bfloat16)
+    rest = jnp.sum(wide * wide, axis=0, keepdims=True)
+    place = lax.broadcasted_iota(jnp.int32, (out_ref.shape[1] - rows, wide.shape[1]), 0)
+    extra = jnp.zeros(place.shape, jnp.float32)
+    for index in range(3):
+        part = rest.astype(jnp.bfloat16).astype(jnp.float32)
+        extra = jnp.where(place == index, part, extra)
+        rest = rest - part
+    for member in range(out_ref.shape[0]):
+        out_ref[member, :rows, :] = scaled
+        out_ref[member, rows:, :] = extra.astype(jnp.bfloat16)
+
+
+def make_payload(query, mixed, gain, members):
+    rows, width = query.shape
+    return pl.pallas_call(
+        payload_kernel,
+        out_shape=(
+            jax.ShapeDtypeStruct((rows, width), jnp.bfloat16),
+            jax.ShapeDtypeStruct((members, rows + 16, width), jnp.bfloat16),
+        ),
+        name="make_payload",
+    )(query, mixed, gain.reshape(rows, 1))
+
+
+def feed_kernel(
+    core_ref, sent_ref, weight_ref, own_ref, near_ref, far_ref, out_ref, x_ref, scale_ref, hidden_ref
+):
+    step = pl.program_id(0)
+    first_steps = pl.num_programs(0) - sent_ref.shape[0] // out_ref.shape[0]
+    members, rows = sent_ref.shape[0], out_ref.shape[2]
+    block = own_ref.shape[0] // (weight_ref.shape[0] * first_steps)
+    half = near_ref.shape[0]
+
+    @pl.when(step == 0)
+    def _():
+        squares = jnp.zeros((1, x_ref.shape[1]), jnp.float32)
+        for member in range(members):
+            x_ref[member * rows : (member + 1) * rows, :] = sent_ref[member, :rows, :]
+            extra = sent_ref[member, rows:, :].astype(jnp.float32)
+            squares = squares + (extra[0:1] + extra[1:2] + extra[2:3])
+        scale = lax.rsqrt(squares / (members * rows) + EPSILON)
+        scale_ref[...] = jnp.broadcast_to(scale, scale_ref.shape)
+
+    @pl.when(step < first_steps)
+    def _():
+        scale = scale_ref[0:1, :]
+        for index in range(weight_ref.shape[0]):
+            sums = jnp.dot(weight_ref[index], x_ref[...], preferred_element_type=jnp.float32)
+            sums = sums * scale
+            units = sums.shape[0] // 4
+            for side in range(2):
+                gate = sums[2 * side * units : (2 * side + 1) * units]
+                up = sums[(2 * side + 1) * units : (2 * side + 2) * units]
+                value = gate / (1.0 + jnp.exp(-gate)) * up
+                blank = jnp.zeros((block - units, value.shape[1]), jnp.float32)
+                start = pl.multiple_of((step * weight_ref.shape[0] + index) * block, 8)
+                hidden_ref[side, pl.ds(start, block), :] = jnp.concatenate([value, blank], axis=0)
+
+    @pl.when(step >= first_steps)
+    def _():
+        core = core_ref[0]
+        near_start = pl.multiple_of(core * half, 8)
+        far_start = pl.multiple_of((1 - core) * half, 8)
+        pieces = (
+            (hidden_ref[0], own_ref),
+            (hidden_ref[1, pl.ds(near_start, half), :], near_ref),
+            (hidden_ref[1, pl.ds(far_start, half), :], far_ref),
+        )
+        total = None
+        for hidden, ref in pieces:
+            part = lax.dot_general(
+                hidden.astype(jnp.bfloat16),
+                ref[...],
+                (((0,), (0,)), ((), ())),
+                preferred_element_type=jnp.float32,
+            )
+            total = part if total is None else total + part
+        for member in range(out_ref.shape[0]):
+            out_ref[member] = total[:, member * rows : (member + 1) * rows].astype(jnp.bfloat16)
+
+
+def feed_forward(sent, weights, own, near, far, core):
+    members, padded, width = sent.shape
+    blocks, block_rows, channels = weights.shape
+    rows = channels // members
+    per_step, out_step = 2, 2
+    first_steps = blocks // per_step
+
+    def down_spec(rows_here):
+        return pl.BlockSpec(
+            (rows_here, out_step * rows), lambda i: (0, jnp.maximum(i - first_steps, 0))
+        )
+
+    return pl.pallas_call(
+        feed_kernel,
+        grid=(first_steps + members // out_step,),
+        out_shape=jax.ShapeDtypeStruct((members, width, rows), jnp.bfloat16),
+        in_specs=[
+            pl.BlockSpec(memory_space=pltpu.SMEM),
+            pl.BlockSpec(memory_space=pltpu.VMEM),
+            pl.BlockSpec(
+                (per_step, block_rows, channels), lambda i: (jnp.minimum(i, first_steps - 1), 0, 0)
+            ),
+            down_spec(own.shape[0]),
+            down_spec(near.shape[0]),
+            down_spec(far.shape[0]),
+        ],
+        out_specs=pl.BlockSpec(
+            (out_step, width, rows), lambda i: (jnp.maximum(i - first_steps, 0), 0, 0)
+        ),
+        scratch_shapes=[
+            pltpu.VMEM((channels, width), jnp.bfloat16),
+            pltpu.VMEM((8, width), jnp.float32),
+            pltpu.VMEM((2, own.shape[0], width), jnp.float32),
+        ],
+        compiler_params=pltpu.CompilerParams(vmem_limit_bytes=48 * 1024 * 1024),
+        cost_estimate=pl.CostEstimate(flops=10**10, bytes_accessed=3 * 10**7, transcendentals=0),
+        name="feed_forward",
+    )(core, sent, weights, own, near, far)
 
 
 def padded_rows(weight):
@@ -109,18 +251,6 @@
 
 def swap(values, axis):
     return lax.ppermute(values, axis, [(0, 1), (1, 0)])
-
-
-def spread_part(own, part, parts):
-    size = own.shape[0] // (2 * parts)
-    core = lax.axis_index("core")
-    return lax.dynamic_slice_in_dim(own, (core * parts + part) * size, size, 0)
-
-
-def down_product(weight, hidden):
-    return lax.dot_general(
-        weight, hidden, (((0,), (0,)), ((), ())), preferred_element_type=jnp.float32
-    )
 
 
 def per_device(
@@ -150,56 +280,33 @@
         sent.transpose(1, 0, 2, 3), SEQ, split_axis=0, concat_axis=0, tiled=True
     )
 
-    own_pair = jnp.concatenate([padded_rows(gate_weight), padded_rows(up_weight)], axis=0)
-    other_pair = swap(own_pair, "xh")
+    core = lax.axis_index("core")
     down_own = lax.all_gather(padded_rows(down_weight), ("z", "core"), axis=0, tiled=True)
-    here, own_pair, other_pair = lax.optimization_barrier((here, own_pair, other_pair))
+    other_pair = swap(jnp.concatenate([gate_weight, up_weight], axis=0), "xh")
+    here, other_pair = lax.optimization_barrier((here, other_pair))
     gate_up = lax.all_gather(
-        jnp.concatenate([own_pair, other_pair], axis=0), ("z", "core"), axis=0, tiled=True
-    )
-
+        pack_rows(gate_weight, up_weight, other_pair)[None], ("z", "core"), axis=0, tiled=True
+    )
+
+    half = down_own.shape[0] // 2
+    down_half = lax.dynamic_slice_in_dim(down_own, core * half, half, 0)
+    here, down_half = lax.optimization_barrier((here, down_half))
+    down_near = swap(down_half, "xh")
     here = here.transpose(1, 2, 0, 3)
     mixed_term = long_mixing(here[0], here[1].reshape(per_group, seq_len), bias_part)
-    returned = mixed_term.transpose(1, 0, 2)
-    first, second = spread_part(down_own, 0, 2), spread_part(down_own, 1, 2)
-    returned, first, second = lax.optimization_barrier((returned, first, second))
-    near_first = swap(first, "xh")
-    returned = lax.all_to_all(returned, SEQ, split_axis=0, concat_axis=0, tiled=True)
-    hyena = (query * returned.reshape(local_width, block_len).astype(jnp.float32)).astype(
-        jnp.bfloat16
-    )
-
-    hyena, near_first, second = lax.optimization_barrier((hyena, near_first, second))
-    near_second = swap(second, "xh")
-    copies = jnp.broadcast_to(hyena[None], (members, local_width, block_len))
-    whole = lax.all_to_all(copies, TP, split_axis=0, concat_axis=0, tiled=True)
-    whole = whole.reshape(members * local_width, block_len)
-    wide = whole.astype(jnp.float32)
-    mean_square = jnp.mean(wide * wide, axis=0)
-    normed = (wide * lax.rsqrt(mean_square + EPSILON)[None, :] * norm_gain[:, None]).astype(
-        jnp.bfloat16
-    )
-    sums = jnp.dot(gate_up, normed, preferred_element_type=jnp.float32)
-    sums = sums.reshape(-1, 2, 2, own_pair.shape[0] // 2, block_len)
-    hidden = (jax.nn.silu(sums[:, :, 0]) * sums[:, :, 1]).astype(jnp.bfloat16)
-    hidden_own = hidden[:, 0].reshape(-1, block_len)
-    hidden_other = hidden[:, 1].reshape(-1, block_len)
-    partial_sum = down_product(down_own, hidden_own)
-    core = lax.axis_index("core")
-    for part, near in enumerate((near_first, near_second)):
-        size = near.shape[0]
-        for side, rows in ((core, near), (1 - core, swap(near, "core"))):
-            chosen = lax.dynamic_slice_in_dim(hidden_other, (side * 2 + part) * size, size, 0)
-            partial_sum += down_product(rows, chosen)
-    partial_sum = partial_sum.astype(jnp.bfloat16)
-    shares = lax.all_to_all(
-        partial_sum.reshape(members, local_width, block_len),
-        TP,
-        split_axis=0,
-        concat_axis=0,
-        tiled=True,
-    )
-    feed_out = jnp.sum(shares.astype(jnp.float32), axis=0)
+    returned = lax.all_to_all(
+        mixed_term.transpose(1, 0, 2), SEQ, split_axis=0, concat_axis=0, tiled=True
+    )
+    gain = lax.dynamic_slice_in_dim(
+        norm_gain, lax.axis_index(TP) * local_width, local_width, 0
+    )
+    hyena, payload = make_payload(query, returned.reshape(local_width, block_len), gain, members)
+    payload, down_near = lax.optimization_barrier((payload, down_near))
+    down_far = swap(down_near, "core")
+    sent = lax.all_to_all(payload, TP, split_axis=0, concat_axis=0, tiled=True)
+    partial_sum = feed_forward(sent, gate_up, down_own, down_near, down_far, core.reshape(1))
+    shares = lax.all_to_all(partial_sum, TP, split_axis=0, concat_axis=0, tiled=True)
+    feed_out = jnp.sum(shares.astype(jnp.float32), axis=0).T
     return (hyena.astype(jnp.float32) + feed_out).astype(jnp.bfloat16)
 
 

time: 207 us -> 197 us (0.952)
  blocking collectives: 54.7 us -> 30.4 us
  Pallas kernels: 14.4 us -> 34.6 us
  matrix products: 15 us -> 0 us
  starting transfers between devices: 29.4 us -> 35.4 us
  other arithmetic: 7.84 us -> 4.02 us
  local copies, waits for them, and re-layouts: 11.3 us -> 14.7 us
  waiting for transfers between devices: 59.8 us -> 62.7 us
    ppermute x5 -> x3, waiting for transfers between devices: 51.9 us -> 16.1 us  [swap(): return lax.ppermute(values, axis, [(0, 1), (1, 0)])]
    all_to_all x1 -> x2, waiting for transfers between devices: 0.01 us -> 35 us  [the longest x1 20.5 us: per_device(): sent = lax.all_to_all(payload, TP, split_axis=0, concat_axis=0, tiled=True)]
    all_to_all x2 -> x1, blocking collectives: 54.7 us -> 30.4 us  [per_device(): lax.all_to_all(partial_sum, TP, split_axis=0, concat_axis=0, tiled=True)]
    pallas_call x0 -> x3, Pallas kernels: none -> 20.1 us  [the longest x1 15 us: feed_forward(): pl.pallas_call(feed_kernel, grid=(first_steps + members // out_step,), ou...]
    dot_general x6 -> x0, matrix products: 15 us -> none  [the longest x5 7.8 us: down_product(): lax.dot_general(weight, hidden, (((0,), (0,)), ((), ())), preferred_eleme...]
    all_to_all x1 -> x2, starting transfers between devices: 5.02 us -> 10.2 us  [the longest x1 5.8 us: per_device(): lax.all_to_all(mixed_term.transpose(1, 0, 2), SEQ, split_axis=0, concat_a...]
    unnamed x14 -> x22, local copies, waits for them, and re-layouts: 0.04 us -> 3.78 us
    all_gather x1, waiting for transfers between devices: 0.02 us -> 3.24 us  [per_device(): lax.all_gather(padded_rows(down_weight), ('z', 'core'), axis=0, tiled=True)]
  transfers between devices with their start and end apart: 10 -> 9, of which waited for: 3 -> 7; matrix products, arithmetic and copies ran while one was open for 14% -> 6% of each run, Pallas kernels for 7% -> 10%
where the time goes in v1:
time: 197 us; the launch traced here: 195 us
  waiting for transfers between devices  62.7 us (32%)
  starting transfers between devices  35.4 us (18%)
  Pallas kernels  34.6 us (18%)
  blocking collectives  30.4 us (15%)
  local copies, waits for them, and re-layouts  14.7 us (7%)
  between operations  13.6 us (7%)
  other arithmetic  4.02 us (2%)
    all_to_all x1, blocking collectives, per_device(): lax.all_to_all(partial_sum, TP, split_axis=0, concat_axis=0, tiled=True)  30.4 us
    all_to_all x1, waiting for transfers between devices, per_device(): sent = lax.all_to_all(payload, TP, split_axis=0, concat_axis=0, tiled=True)  20.5 us
    ppermute x3, waiting for transfers between devices, swap(): return lax.ppermute(values, axis, [(0, 1), (1, 0)])  16.1 us
    pallas_call x1, Pallas kernels, feed_forward(): pl.pallas_call(feed_kernel, grid=(first_steps + members // out_step,), ou...  15 us
    all_to_all x1, waiting for transfers between devices, per_device(): lax.all_to_all(mixed_term.transpose(1, 0, 2), SEQ, split_axis=0, concat_a...  14.5 us
    pallas_call x1, Pallas kernels, long_mixing(): pl.pallas_call(conv_kernel, out_shape=jax.ShapeDtypeStruct(gated.shape, j...  14.4 us
    all_to_all x1, starting transfers between devices, per_device(): lax.all_to_all(sent.transpose(1, 0, 2, 3), SEQ, split_axis=0, concat_axis...  13.1 us
    all_to_all x1, waiting for transfers between devices, per_device(): lax.all_to_all(sent.transpose(1, 0, 2, 3), SEQ, split_axis=0, concat_axis...  7.76 us
  transfers between devices with their start and end apart: 9, of which 7 were waited for; matrix products, arithmetic and copies ran while one was open for 6% of the time, Pallas kernels for 10%

profile of v1, /device:TPU:1, one launch (start us, length us, event | category | flops | bytes accessed | tf_op | source)
XLA Modules:
  0.0 195.4 jit_solution(16908058581120506298)
XLA Ops:
  6.5 1.7 pad.4
  8.3 1.2 slice_bitcast_fusion.1
  9.6 4.9 %collective-permute-start = (bf16[6,512]{1,0:T(8,128)(2,1)S(1)}, bf16[6,512]{1,0:T(8,128)(2,1)S(1)}, u32[]{:S(2)}, u32[]{:S(2)}) collective-permute-start(bf16[6,512]{1,0:T(8,128)(2,1)S(1)} %reshape.19), channel_id=1, source_target_pairs={{0,8},{8,16},{16,24},{24,32},{32,40},{40,48},{48,56},{56,64},{64,7... | collective-permute-start | bytes 18440 | tf_op jit(solution)/shard_map/ppermute | solution.py:267
  15.7 1.8 fusion.3
  17.5 0.9 fusion.5
  18.5 0.9 copy.20
  19.4 13.1 %all-to-all-start = ((bf16[32,2,16,256]{3,2,1,0:T(8,128)(2,1)}), bf16[32,2,16,256]{3,2,1,0:T(8,128)(2,1)S(1)}, u32[]{:S(2)}, u32[]{:S(2)}) async-start(bf16[32,2,16,256]{3,2,1,0:T(8,128)(2,1)} %copy.20), calls=%async_computation | async-start | bytes 1048576 | tf_op jit(solution)/shard_map/all_to_all | solution.py:279
  32.6 3.0 %collective-permute-start.1 = (bf16[44,4096]{1,0:T(8,128)(2,1)S(1)}, bf16[44,4096]{1,0:T(8,128)(2,1)S(1)}, u32[]{:S(2)}, u32[]{:S(2)}) collective-permute-start(bf16[44,4096]{1,0:T(8,128)(2,1)S(1)} %pad_maximum_fusion.1), channel_id=1, source_target_pairs={{0,128},{128,0},{1,129},{129,1},{2,130},{130,2},{3,131},{131,3},{4... | collective-permute-start | bytes 1081352 | tf_op jit(solution)/shard_map/ppermute | solution.py:253
  35.6 12.9 %collective-permute-done.1.other_ref = bf16[44,4096]{1,0:T(8,128)(2,1)S(1)} collective-permute-done((bf16[44,4096]{1,0:T(8,128)(2,1)S(1)}, bf16[44,4096]{1,0:T(8,128)(2,1)S(1)}, u32[]{:S(2)}, u32[]{:S(2)}) %collective-permute-start.1) | collective-permute-done | bytes 360480 | tf_op jit(solution)/shard_map/ppermute | solution.py:253
  48.5 7.8 %all-to-all-done = bf16[32,2,16,256]{3,2,1,0:T(8,128)(2,1)S(1)} async-done(((bf16[32,2,16,256]{3,2,1,0:T(8,128)(2,1)}), bf16[32,2,16,256]{3,2,1,0:T(8,128)(2,1)S(1)}, u32[]{:S(2)}, u32[]{:S(2)}) %all-to-all-start) | async-done | bytes 524320 | tf_op jit(solution)/shard_map/all_to_all | solution.py:279
  56.3 2.2 %pack_rows.1 = bf16[88,4096]{1,0:T(8,128)(2,1)} custom-call(bf16[22,4096]{1,0:T(8,128)(2,1)} %gate_ref.1, bf16[22,4096]{1,0:T(8,128)(2,1)} %up_ref.1, bf16[44,4096]{1,0:T(8,128)(2,1)} %copy-done.6), custom_call_target="tpu_custom_call" | custom-call | tf_op jit(solution)/shard_map/pack_rows/pallas_call | solution.py:113
  58.5 3.2 %all-gather.4.cloned.1.call-done.own_ref = bf16[384,4096]{1,0:T(8,128)(2,1)} async-done(((bf16[24,4096]{1,0:T(8,128)(2,1)}), bf16[384,4096]{1,0:T(8,128)(2,1)}) %all-gather.4.cloned.1.call-update) | async-done | bytes 3145744 | tf_op jit(solution)/shard_map/all_gather | solution.py:284
  61.8 2.7 %constant_dynamic-slice_fusion = bf16[192,4096]{1,0:T(8,128)(2,1)} fusion(bf16[384,4096]{1,0:T(8,128)(2,1)} %all-gather.4.cloned.1.call-done.own_ref, s32[]{:T(128)S(6)} %select_n.10), kind=kLoop, calls=%fused_computation.22 | loop fusion | bytes 3145732 | tf_op jit(solution)/shard_map/dynamic_slice | solution.py:292
  64.5 2.8 %collective-permute-start.2 = (bf16[192,4096]{1,0:T(8,128)(2,1)}, bf16[192,4096]{1,0:T(8,128)(2,1)S(1)}, u32[]{:S(2)}, u32[]{:S(2)}) collective-permute-start(bf16[192,4096]{1,0:T(8,128)(2,1)} %constant_dynamic-slice_fusion), channel_id=1, source_target_pairs={{0,128},{128,0},{1,129},{129,1},{2,130},{130,2},{3,131},{131,3},{4... | collective-permute-start | bytes 4718600 | tf_op jit(solution)/shard_map/ppermute | solution.py:253
  67.3 0.8 dynamic_slice.9.bias_ref
  68.5 14.4 %long_mixing.1 = bf16[16,32,256]{2,1,0:T(8,128)(2,1)S(1)} custom-call(f32[16]{0:T(128)S(1)} %dynamic_slice.9.bias_ref, bf16[16,32,256]{2,1,0:T(8,128)(2,1)S(1)} %get-tuple-element.24.gated_ref, bf16[16,1,8192]{2,1,0:T(2,128)(2,1)S(1)} %reshape_reshape_squeeze.4.taps_ref), custom_call_target="tpu_custom_call" | custom-call | flops 8589934592 | bytes 786432 | tf_op jit(solution)/shard_map/long_mixing/pallas_call | solution.py:95
  82.9 0.9 copy.23
  83.8 5.8 %all-to-all-start.1 = ((bf16[32,16,256]{2,1,0:T(8,128)(2,1)}), bf16[32,16,256]{2,1,0:T(8,128)(2,1)S(1)}, u32[]{:S(2)}, u32[]{:S(2)}) async-start(bf16[32,16,256]{2,1,0:T(8,128)(2,1)} %copy.23), calls=%async_computation.1 | async-start | bytes 524288 | tf_op jit(solution)/shard_map/all_to_all | solution.py:297
  89.6 0.8 dynamic_slice.11
  90.4 0.9 copy.24.gain_ref
  91.2 14.5 %all-to-all-done.1 = bf16[32,16,256]{2,1,0:T(8,128)(2,1)S(1)} async-done(((bf16[32,16,256]{2,1,0:T(8,128)(2,1)}), bf16[32,16,256]{2,1,0:T(8,128)(2,1)S(1)}, u32[]{:S(2)}, u32[]{:S(2)}) %all-to-all-start.1) | async-done | bytes 262176 | tf_op jit(solution)/shard_map/all_to_all | solution.py:297
  105.7 0.7 copy-done.3
  106.4 2.9 %make_payload.1 = (bf16[512,256]{1,0:T(8,128)(2,1)}, bf16[8,528,256]{2,1,0:T(8,128)(2,1)}) custom-call(f32[512,256]{1,0:T(8,128)} %get-tuple-element.22.query_ref, bf16[512,256]{1,0:T(8,128)(2,1)} %bitcast.36, f32[512,1]{1,0:T(8,128)} %copy.24.gain_ref), custom_call_target="tpu_custom_call" | custom-call | tf_op jit(solution)/shard_map/make_payload/pallas_call | solution.py:140
  109.3 4.4 %all-to-all-start.2 = ((bf16[8,528,256]{2,1,0:T(8,128)(2,1)}), bf16[8,528,256]{2,1,0:T(8,128)(2,1)}, u32[]{:S(2)}, u32[]{:S(2)}) async-start(bf16[8,528,256]{2,1,0:T(8,128)(2,1)} %get-tuple-element.18), calls=%async_computation.2 | async-start | bytes 4325376 | tf_op jit(solution)/shard_map/all_to_all | solution.py:306
  113.7 1.5 collective-permute-start.3
  115.2 3.2 %collective-permute-done.3.far_ref = bf16[192,4096]{1,0:T(8,128)(2,1)S(1)} collective-permute-done((bf16[192,4096]{1,0:T(8,128)(2,1)S(1)}, bf16[192,4096]{1,0:T(8,128)(2,1)S(1)}, u32[]{:S(2)}, u32[]{:S(2)}) %collective-permute-start.3) | collective-permute-done | bytes 1572896 | tf_op jit(solution)/shard_map/ppermute | solution.py:253
  118.3 1.1 copy-done
  119.5 20.5 %all-to-all-done.2.sent_ref = bf16[8,528,256]{2,1,0:T(8,128)(2,1)} async-done(((bf16[8,528,256]{2,1,0:T(8,128)(2,1)}), bf16[8,528,256]{2,1,0:T(8,128)(2,1)}, u32[]{:S(2)}, u32[]{:S(2)}) %all-to-all-start.2) | async-done | bytes 2162720 | tf_op jit(solution)/shard_map/all_to_all | solution.py:306
  140.0 1.4 copy-done.1
  141.4 15.0 %feed_forward.1 = bf16[8,256,512]{2,1,0:T(8,128)(2,1)S(1)} custom-call(s32[1]{0:T(128)} %bitcast.11.core_ref, bf16[8,528,256]{2,1,0:T(8,128)(2,1)} %all-to-all-done.2.sent_ref, bf16[16,88,4096]{2,1,0:T(8,128)(2,1)} %bitcast.40, bf16[384,4096]{1,0:T(8,128)(2,1)} %all-gather.4.cloned.1.call-done.own_ref, ...), custom_call_target="tpu_custom_call" | custom-call | flops 10000000000 | bytes 30000000 | tf_op jit(solution)/shard_map/feed_forward/pallas_call | solution.py:219
  156.4 30.4 %all_to_all.20 = bf16[8,256,512]{2,1,0:T(8,128)(2,1)S(1)} all-to-all(bf16[8,256,512]{2,1,0:T(8,128)(2,1)S(1)} %feed_forward.1), channel_id=1, replica_groups=mesh['xh'=2,'z'=8,'core'=2,'y'=4,'xl'=2] {'y','xl'}, dimensions={0} | all-to-all | bytes 4194304 | tf_op jit(solution)/shard_map/all_to_all | solution.py:308
  187.8 0.8 fusion.6
  (39 shorter events, 2.9 us)
Async XLA Ops:
  6.5 8.1 %copy-start.2 = (bf16[3,512,256]{2,1,0:T(8,128)(2,1)S(1)}, bf16[3,512,256]{2,1,0:T(8,128)(2,1)}, u32[]{:S(2)}) copy-start(bf16[3,512,256]{2,1,0:T(8,128)(2,1)} %param.8) | copy-start | bytes 2359300
  6.5 8.1 %copy-start.9 = (f32[3,512,3]{1,2,0:T(4,128)S(1)}, f32[3,512,3]{1,2,0:T(4,128)}, u32[]{:S(2)}) copy-start(f32[3,512,3]{1,2,0:T(4,128)} %param.10) | copy-start | bytes 55300
  6.5 55.2 %all-gather.4.cloned.1.call-start = ((), (), s32[]{:S(2)}) async-start(), calls=%async_computation.4 | async-start | bytes 3342336 | tf_op jit(solution)/shard_map/all_gather | solution.py:284
  9.6 5.7 %collective-permute-start = (bf16[6,512]{1,0:T(8,128)(2,1)S(1)}, bf16[6,512]{1,0:T(8,128)(2,1)S(1)}, u32[]{:S(2)}, u32[]{:S(2)}) collective-permute-start(bf16[6,512]{1,0:T(8,128)(2,1)S(1)} %reshape.19), channel_id=1, source_target_pairs={{0,8},{8,16},{16,24},{24,32},{32,40},{40,48},{48,56},{56,64},{64,7... | collective-permute-start | bytes 18440 | tf_op jit(solution)/shard_map/ppermute | solution.py:267
  17.5 1.0 copy-start.7
  18.5 14.0 %copy-start.4 = (bf16[22,4096]{1,0:T(8,128)(2,1)S(1)}, bf16[22,4096]{1,0:T(8,128)(2,1)}, u32[]{:S(2)}) copy-start(bf16[22,4096]{1,0:T(8,128)(2,1)} %gate_ref.1) | copy-start | bytes 540676
  18.5 14.0 %copy-start.5 = (bf16[22,4096]{1,0:T(8,128)(2,1)S(1)}, bf16[22,4096]{1,0:T(8,128)(2,1)}, u32[]{:S(2)}) copy-start(bf16[22,4096]{1,0:T(8,128)(2,1)} %up_ref.1) | copy-start | bytes 540676
  19.4 36.9 %all-to-all-start = ((bf16[32,2,16,256]{3,2,1,0:T(8,128)(2,1)}), bf16[32,2,16,256]{3,2,1,0:T(8,128)(2,1)S(1)}, u32[]{:S(2)}, u32[]{:S(2)}) async-start(bf16[32,2,16,256]{3,2,1,0:T(8,128)(2,1)} %copy.20), calls=%async_computation | async-start | bytes 1048576 | tf_op jit(solution)/shard_map/all_to_all | solution.py:279
  32.5 107.5 %all-gather.6.cloned.1.call-start = ((), (), s32[]{:S(2)}) async-start(), calls=%async_computation.5 | async-start | bytes 12255232 | tf_op jit(solution)/shard_map/all_gather | solution.py:287
  32.6 15.9 %collective-permute-start.1 = (bf16[44,4096]{1,0:T(8,128)(2,1)S(1)}, bf16[44,4096]{1,0:T(8,128)(2,1)S(1)}, u32[]{:S(2)}, u32[]{:S(2)}) collective-permute-start(bf16[44,4096]{1,0:T(8,128)(2,1)S(1)} %pad_maximum_fusion.1), channel_id=1, source_target_pairs={{0,128},{128,0},{1,129},{129,1},{2,130},{130,2},{3,131},{131,3},{4... | collective-permute-start | bytes 1081352 | tf_op jit(solution)/shard_map/ppermute | solution.py:253
  48.5 7.8 %copy-start.6 = (bf16[44,4096]{1,0:T(8,128)(2,1)}, bf16[44,4096]{1,0:T(8,128)(2,1)S(1)}, u32[]{:S(2)}) copy-start(bf16[44,4096]{1,0:T(8,128)(2,1)S(1)} %collective-permute-done.1.other_ref) | copy-start | bytes 1081348
  64.5 44.8 %collective-permute-start.2 = (bf16[192,4096]{1,0:T(8,128)(2,1)}, bf16[192,4096]{1,0:T(8,128)(2,1)S(1)}, u32[]{:S(2)}, u32[]{:S(2)}) collective-permute-start(bf16[192,4096]{1,0:T(8,128)(2,1)} %constant_dynamic-slice_fusion), channel_id=1, source_target_pairs={{0,128},{128,0},{1,129},{129,1},{2,130},{130,2},{3,131},{131,3},{4... | collective-permute-start | bytes 4718600 | tf_op jit(solution)/shard_map/ppermute | solution.py:253
  83.8 21.9 %all-to-all-start.1 = ((bf16[32,16,256]{2,1,0:T(8,128)(2,1)}), bf16[32,16,256]{2,1,0:T(8,128)(2,1)S(1)}, u32[]{:S(2)}, u32[]{:S(2)}) async-start(bf16[32,16,256]{2,1,0:T(8,128)(2,1)} %copy.23), calls=%async_computation.1 | async-start | bytes 524288 | tf_op jit(solution)/shard_map/all_to_all | solution.py:297
  105.7 0.7 copy-start.3
  109.3 30.7 %all-to-all-start.2 = ((bf16[8,528,256]{2,1,0:T(8,128)(2,1)}), bf16[8,528,256]{2,1,0:T(8,128)(2,1)}, u32[]{:S(2)}, u32[]{:S(2)}) async-start(bf16[8,528,256]{2,1,0:T(8,128)(2,1)} %get-tuple-element.18), calls=%async_computation.2 | async-start | bytes 4325376 | tf_op jit(solution)/shard_map/all_to_all | solution.py:306
  113.7 4.6 %collective-permute-start.3 = (bf16[192,4096]{1,0:T(8,128)(2,1)S(1)}, bf16[192,4096]{1,0:T(8,128)(2,1)S(1)}, u32[]{:S(2)}, u32[]{:S(2)}) collective-permute-start(bf16[192,4096]{1,0:T(8,128)(2,1)S(1)} %collective-permute-done.2.near_ref), channel_id=1, source_target_pairs={{0,8},{8,0},{1,9},{9,1},{2,10},{10,2},{3,11},{11,3},{4,12},{12,4},... | collective-permute-start | bytes 4718600 | tf_op jit(solution)/shard_map/ppermute | solution.py:253
  118.3 1.1 copy-start
  140.0 1.4 copy-start.1
  186.8 1.0 copy-start.8
Sparse Core Ops, SparseCore 0:
  9.2 52.5 all-gather.3
  63.6 75.6 all-gather.5

commit v2 on v1

--- a/solution.py
+++ b/solution.py
@@ -1,3 +1,5 @@
+import functools
+
 import jax
 import jax.numpy as jnp
 from jax import lax
@@ -12,14 +14,73 @@
 TP = ("y", "xl")
 
 
-def short_filter(signal, weights, leading):
-    extent = signal.shape[2]
-    padded = jnp.concatenate([leading, signal], axis=2)
-    return (
-        weights[:, :, 0:1] * padded[:, :, 2:]
-        + weights[:, :, 1:2] * padded[:, :, 1 : extent + 1]
-        + weights[:, :, 2:3] * padded[:, :, 0:extent]
-    )
+def gate_kernel(projected_ref, taps_ref, weight_ref, edge_ref, sent_ref, query_ref):
+    rows, width = taps_ref.shape
+    groups = sent_ref.shape[0]
+    weights = weight_ref[...].T
+    edges = edge_ref[...].astype(jnp.float32).T
+    lane = lax.broadcasted_iota(jnp.int32, (rows, width), 1)
+    shorts = []
+    for index in range(3):
+        value = projected_ref[index].astype(jnp.float32)
+        far, near = edges[:, 2 * index : 2 * index + 1], edges[:, 2 * index + 1 : 2 * index + 2]
+        once = jnp.where(lane == 0, near, pltpu.roll(value, 1, 1))
+        twice = jnp.where(lane == 0, far, jnp.where(lane == 1, near, pltpu.roll(value, 2, 1)))
+        taps = [weights[:, 3 * index + tap : 3 * index + tap + 1] for tap in range(3)]
+        shorts.append(taps[0] * value + taps[1] * once + taps[2] * twice)
+    query_ref[...] = shorts[0]
+    gated = (shorts[1] * shorts[2]).astype(jnp.bfloat16)
+    sent_ref[:, 0] = gated.reshape(groups, rows // groups, width)
+    sent_ref[:, 1] = taps_ref[...].reshape(groups, rows // groups, width)
+
+
+def make_gated(projected, taps, short_weight, edge, groups):
+    count, rows, width = projected.shape
+    weights = short_weight.transpose(0, 2, 1).reshape(9, rows)
+    return pl.pallas_call(
+        gate_kernel,
+        out_shape=(
+            jax.ShapeDtypeStruct((groups, 2, rows // groups, width), jnp.bfloat16),
+            jax.ShapeDtypeStruct((rows, width), jnp.float32),
+        ),
+        name="make_gated",
+    )(projected, taps, jnp.pad(weights, ((0, 7), (0, 0))), edge)
+
+
+def pack_first_kernel(split, gate_ref, up_ref, down_ref, first_ref, pair_ref):
+    gate, up = gate_ref[...].astype(jnp.float32), up_ref[...].astype(jnp.float32)
+    down = down_ref[...].astype(jnp.float32)
+    first = jnp.concatenate([down, gate[split:], up[split:]], axis=0)
+    first_ref[...] = first.astype(jnp.bfloat16)
+    pair_ref[...] = jnp.concatenate([gate[:split], up[:split]], axis=0).astype(jnp.bfloat16)
+
+
+def pack_first(gate, up, down):
+    rows, width = gate.shape
+    split = rows - (-rows % 16) // 2
+    return pl.pallas_call(
+        functools.partial(pack_first_kernel, split),
+        out_shape=(
+            jax.ShapeDtypeStruct((rows + 2 * (rows - split), width), gate.dtype),
+            jax.ShapeDtypeStruct((2 * split, width), gate.dtype),
+        ),
+        name="pack_first",
+    )(gate, up, down)
+
+
+def pack_second_kernel(pair_ref, other_ref, out_ref):
+    pair, other = pair_ref[...].astype(jnp.float32), other_ref[...].astype(jnp.float32)
+    blank = jnp.zeros((out_ref.shape[0] - 2 * pair.shape[0], pair.shape[1]), jnp.float32)
+    out_ref[...] = jnp.concatenate([pair, other, blank], axis=0).astype(jnp.bfloat16)
+
+
+def pack_second(pair, other):
+    rows = 2 * pair.shape[0]
+    return pl.pallas_call(
+        pack_second_kernel,
+        out_shape=jax.ShapeDtypeStruct((rows + -rows % 8, pair.shape[1]), pair.dtype),
+        name="pack_second",
+    )(pair, other)
 
 
 def build_table(taps_ref, channel, table_ref):
@@ -102,21 +163,6 @@
         name="long_mixing")(bias, gated, taps.reshape(channels, 1, seq_len))
 
 
-def pack_kernel(gate_ref, up_ref, other_ref, out_ref):
-    parts = [gate_ref[...], up_ref[...], other_ref[...]]
-    whole = jnp.concatenate([part.astype(jnp.float32) for part in parts], axis=0)
-    out_ref[...] = whole.astype(out_ref.dtype)
-
-
-def pack_rows(gate, up, other):
-    rows = gate.shape[0] + up.shape[0] + other.shape[0]
-    return pl.pallas_call(
-        pack_kernel,
-        out_shape=jax.ShapeDtypeStruct((rows, gate.shape[1]), gate.dtype),
-        name="pack_rows",
-    )(gate, up, other)
-
-
 def payload_kernel(query_ref, mixed_ref, gain_ref, hyena_ref, out_ref):
     rows = query_ref.shape[0]
     hyena = (query_ref[...] * mixed_ref[...].astype(jnp.float32)).astype(jnp.bfloat16)
@@ -147,17 +193,27 @@
     )(query, mixed, gain.reshape(rows, 1))
 
 
+def gated_product(gate, up):
+    return gate / (1.0 + jnp.exp(-gate)) * up
+
+
 def feed_kernel(
-    core_ref, sent_ref, weight_ref, own_ref, near_ref, far_ref, out_ref, x_ref, scale_ref, hidden_ref
+    sizes, core_ref, sent_ref, weight_ref, p0_ref, p1_ref, p2_ref, p3_ref, out_ref,
+    x_ref, scale_ref, hidden_ref, flat_ref, piece_ref, piece_sem,
 ):
+    units, split, block, per_step, first_steps = sizes
     step = pl.program_id(0)
-    first_steps = pl.num_programs(0) - sent_ref.shape[0] // out_ref.shape[0]
     members, rows = sent_ref.shape[0], out_ref.shape[2]
-    block = own_ref.shape[0] // (weight_ref.shape[0] * first_steps)
-    half = near_ref.shape[0]
+    core = core_ref[0]
+    copies = [
+        pltpu.make_async_copy(ref, piece_ref.at[index], piece_sem.at[index])
+        for index, ref in enumerate((p0_ref, p1_ref, p2_ref, p3_ref))
+    ]
 
     @pl.when(step == 0)
     def _():
+        for copy in copies:
+            copy.start()
         squares = jnp.zeros((1, x_ref.shape[1]), jnp.float32)
         for member in range(members):
             x_ref[member * rows : (member + 1) * rows, :] = sent_ref[member, :rows, :]
@@ -169,34 +225,52 @@
     @pl.when(step < first_steps)
     def _():
         scale = scale_ref[0:1, :]
-        for index in range(weight_ref.shape[0]):
-            sums = jnp.dot(weight_ref[index], x_ref[...], preferred_element_type=jnp.float32)
+        sums = jnp.dot(weight_ref[...], x_ref[...], preferred_element_type=jnp.float32) * scale
+        height = weight_ref.shape[0] // per_step
+        for index in range(per_step):
+            part = sums[index * height : (index + 1) * height]
+            for side in range(2):
+                base = 2 * side * split
+                value = gated_product(
+                    part[base : base + split], part[base + split : base + 2 * split]
+                )
+                blank = jnp.zeros((block - split, value.shape[1]), jnp.float32)
+                start = pl.multiple_of((step * (per_step // 2) + index // 2) * block, 8)
+                hidden_ref[side, index % 2, pl.ds(start, block), :] = jnp.concatenate(
+                    [value, blank], axis=0
+                )
+
+    @pl.when(step == first_steps)
+    def _():
+        for copy in copies:
+            copy.wait()
+        scale = scale_ref[0:1, :]
+        count = piece_ref.shape[1] // block
+        for index in range(4):
+            tails = [
+                piece_ref[index, z * block + block // 2 : (z + 1) * block, :] for z in range(count)
+            ]
+            sums = jnp.dot(
+                jnp.concatenate(tails, axis=0), x_ref[...], preferred_element_type=jnp.float32
+            )
             sums = sums * scale
-            units = sums.shape[0] // 4
-            for side in range(2):
-                gate = sums[2 * side * units : (2 * side + 1) * units]
-                up = sums[(2 * side + 1) * units : (2 * side + 2) * units]
-                value = gate / (1.0 + jnp.exp(-gate)) * up
-                blank = jnp.zeros((block - units, value.shape[1]), jnp.float32)
-                start = pl.multiple_of((step * weight_ref.shape[0] + index) * block, 8)
-                hidden_ref[side, pl.ds(start, block), :] = jnp.concatenate([value, blank], axis=0)
+            place = core if index % 2 == 0 else 1 - core
+            for z in range(count):
+                gate_at = z * (block // 2) + units - block // 2
+                up_at = gate_at + units - split
+                value = gated_product(sums[gate_at:up_at], sums[up_at : up_at + units - split])
+                hidden_ref[index // 2, place, z * block + split : z * block + units, :] = value
+            flat_ref[index] = hidden_ref[index // 2, place].T.astype(jnp.bfloat16)
 
     @pl.when(step >= first_steps)
     def _():
-        core = core_ref[0]
-        near_start = pl.multiple_of(core * half, 8)
-        far_start = pl.multiple_of((1 - core) * half, 8)
-        pieces = (
-            (hidden_ref[0], own_ref),
-            (hidden_ref[1, pl.ds(near_start, half), :], near_ref),
-            (hidden_ref[1, pl.ds(far_start, half), :], far_ref),
-        )
+        wide = out_ref.shape[0] * rows
+        start = pl.multiple_of((step - first_steps) * wide, LANES)
         total = None
-        for hidden, ref in pieces:
-            part = lax.dot_general(
-                hidden.astype(jnp.bfloat16),
-                ref[...],
-                (((0,), (0,)), ((), ())),
+        for index in range(4):
+            part = jnp.dot(
+                flat_ref[index],
+                piece_ref[index, :, pl.ds(start, wide)],
                 preferred_element_type=jnp.float32,
             )
             total = part if total is None else total + part
@@ -204,31 +278,31 @@
             out_ref[member] = total[:, member * rows : (member + 1) * rows].astype(jnp.bfloat16)
 
 
-def feed_forward(sent, weights, own, near, far, core):
+def feed_forward(sent, weights, pieces, core, units, split):
     members, padded, width = sent.shape
-    blocks, block_rows, channels = weights.shape
+    channels = weights.shape[1]
     rows = channels // members
-    per_step, out_step = 2, 2
+    length = pieces[0].shape[0]
+    block = 2 * units - split + units - split
+    blocks = 2 * length // block
+    per_step, out_step = 4, 2
     first_steps = blocks // per_step
-
-    def down_spec(rows_here):
-        return pl.BlockSpec(
-            (rows_here, out_step * rows), lambda i: (0, jnp.maximum(i - first_steps, 0))
-        )
-
-    return pl.pallas_call(
-        feed_kernel,
+    anywhere = pl.BlockSpec(memory_space=pl.ANY)
+    return pl.pallas_call(
+        functools.partial(feed_kernel, (units, split, block, per_step, first_steps)),
         grid=(first_steps + members // out_step,),
         out_shape=jax.ShapeDtypeStruct((members, width, rows), jnp.bfloat16),
         in_specs=[
             pl.BlockSpec(memory_space=pltpu.SMEM),
             pl.BlockSpec(memory_space=pltpu.VMEM),
             pl.BlockSpec(
-                (per_step, block_rows, channels), lambda i: (jnp.minimum(i, first_steps - 1), 0, 0)
+                (weights.shape[0] // first_steps, channels),
+                lambda i: (jnp.minimum(i, first_steps - 1), 0),
             ),
-            down_spec(own.shape[0]),
-            down_spec(near.shape[0]),
-            down_spec(far.shape[0]),
+            anywhere,
+            anywhere,
+            anywhere,
+            anywhere,
         ],
         out_specs=pl.BlockSpec(
             (out_step, width, rows), lambda i: (jnp.maximum(i - first_steps, 0), 0, 0)
@@ -236,17 +310,15 @@
         scratch_shapes=[
             pltpu.VMEM((channels, width), jnp.bfloat16),
             pltpu.VMEM((8, width), jnp.float32),
-            pltpu.VMEM((2, own.shape[0], width), jnp.float32),
+            pltpu.VMEM((2, 2, length, width), jnp.float32),
+            pltpu.VMEM((4, width, length), jnp.bfloat16),
+            pltpu.VMEM((4, length, channels), jnp.bfloat16),
+            pltpu.SemaphoreType.DMA((4,)),
         ],
         compiler_params=pltpu.CompilerParams(vmem_limit_bytes=48 * 1024 * 1024),
         cost_estimate=pl.CostEstimate(flops=10**10, bytes_accessed=3 * 10**7, transcendentals=0),
         name="feed_forward",
-    )(core, sent, weights, own, near, far)
-
-
-def padded_rows(weight):
-    rows = weight.shape[0]
-    return jnp.pad(weight, ((0, -rows % 8), (0, 0)))
+    )(core, sent, weights, *pieces)
 
 
 def swap(values, axis):
@@ -264,34 +336,23 @@
     offset = lax.axis_index(SEQ) * per_group
     bias_part = lax.dynamic_slice_in_dim(skip_bias, offset, per_group, 0)
 
+    first, pair = pack_first(gate_weight, up_weight, down_weight)
+    own_near = lax.all_gather(first, "z", axis=0, tiled=True)
+    edge = projected[:, :, block_len - 2 :].transpose(0, 2, 1).reshape(6, local_width)
     edge = lax.ppermute(
-        projected[:, :, block_len - 2 :].transpose(0, 2, 1).reshape(6, local_width),
-        SEQ,
-        [(i, i + 1) for i in range(groups - 1)],
-    )
-    edge = edge.reshape(3, 2, local_width).transpose(0, 2, 1)
-    shorts = short_filter(
-        projected.astype(jnp.float32), short_weight, edge.astype(jnp.float32)
-    )
-    query = shorts[0]
-    gated = (shorts[1] * shorts[2]).astype(jnp.bfloat16)
-    sent = jnp.stack([gated, filter_taps]).reshape(2, groups, per_group, block_len)
-    here = lax.all_to_all(
-        sent.transpose(1, 0, 2, 3), SEQ, split_axis=0, concat_axis=0, tiled=True
-    )
+        jnp.pad(edge, ((0, 2), (0, 0))), SEQ, [(i, i + 1) for i in range(groups - 1)]
+    )
+    sent, query = make_gated(projected, filter_taps, short_weight, edge, groups)
+    here = lax.all_to_all(sent, SEQ, split_axis=0, concat_axis=0, tiled=True)
 
     core = lax.axis_index("core")
-    down_own = lax.all_gather(padded_rows(down_weight), ("z", "core"), axis=0, tiled=True)
-    other_pair = swap(jnp.concatenate([gate_weight, up_weight], axis=0), "xh")
+    other_pair = swap(pair, "xh")
     here, other_pair = lax.optimization_barrier((here, other_pair))
-    gate_up = lax.all_gather(
-        pack_rows(gate_weight, up_weight, other_pair)[None], ("z", "core"), axis=0, tiled=True
-    )
-
-    half = down_own.shape[0] // 2
-    down_half = lax.dynamic_slice_in_dim(down_own, core * half, half, 0)
-    here, down_half = lax.optimization_barrier((here, down_half))
-    down_near = swap(down_half, "xh")
+    gate_up = lax.all_gather(pack_second(pair, other_pair), ("z", "core"), axis=0, tiled=True)
+
+    here, own_near = lax.optimization_barrier((here, own_near))
+    own_far = swap(own_near, "core")
+    near = swap(own_near, "xh")
     here = here.transpose(1, 2, 0, 3)
     mixed_term = long_mixing(here[0], here[1].reshape(per_group, seq_len), bias_part)
     returned = lax.all_to_all(
@@ -301,10 +362,11 @@
         norm_gain, lax.axis_index(TP) * local_width, local_width, 0
     )
     hyena, payload = make_payload(query, returned.reshape(local_width, block_len), gain, members)
-    payload, down_near = lax.optimization_barrier((payload, down_near))
-    down_far = swap(down_near, "core")
+    payload, near = lax.optimization_barrier((payload, near))
+    pieces = (own_near, own_far, near, swap(near, "core"))
     sent = lax.all_to_all(payload, TP, split_axis=0, concat_axis=0, tiled=True)
-    partial_sum = feed_forward(sent, gate_up, down_own, down_near, down_far, core.reshape(1))
+    units, split = gate_weight.shape[0], pair.shape[0] // 2
+    partial_sum = feed_forward(sent, gate_up, pieces, core.reshape(1), units, split)
     shares = lax.all_to_all(partial_sum, TP, split_axis=0, concat_axis=0, tiled=True)
     feed_out = jnp.sum(shares.astype(jnp.float32), axis=0).T
     return (hyena.astype(jnp.float32) + feed_out).astype(jnp.bfloat16)

time: 197 us -> 200 us (1.015)
  waiting for transfers between devices: 62.7 us -> 73.4 us
  local copies, waits for them, and re-layouts: 14.7 us -> 8.47 us
  Pallas kernels: 34.6 us -> 37.6 us
  other arithmetic: 4.02 us -> 1.06 us
    all_to_all x1, waiting for transfers between devices: 14.5 us -> 23.2 us  [per_device(): lax.all_to_all(mixed_term.transpose(1, 0, 2), SEQ, split_axis=0, concat_a...]
    all_to_all x1, waiting for transfers between devices: 20.5 us -> 27.5 us  [per_device(): sent = lax.all_to_all(payload, TP, split_axis=0, concat_axis=0, tiled=True)]
    ppermute x3 -> x4, waiting for transfers between devices: 16.1 us -> 10.7 us  [swap(): return lax.ppermute(values, axis, [(0, 1), (1, 0)])]
    pallas_call x2 -> x4, Pallas kernels: 17.2 us -> 20.2 us  [the longest x1 12.4 us: feed_forward(): pl.pallas_call(functools.partial(feed_kernel, (units, split, block, per_s...]
    dynamic_slice x1 -> x0, local copies, waits for them, and re-layouts: 2.75 us -> none  [per_device(): down_half = lax.dynamic_slice_in_dim(down_own, core * half, half, 0)]
    all_to_all x1, waiting for transfers between devices: 7.76 us -> 9.98 us  [per_device(): here = lax.all_to_all(sent, SEQ, split_axis=0, concat_axis=0, tiled=True)]
    unnamed x22 -> x12, local copies, waits for them, and re-layouts: 3.78 us -> 1.75 us
    ppermute x3 -> x4, starting transfers between devices: 7.21 us -> 6.39 us  [swap(): return lax.ppermute(values, axis, [(0, 1), (1, 0)])]
  transfers between devices with their start and end apart: 9 -> 10, of which waited for: 7 -> 5; matrix products, arithmetic and copies ran while one was open for 6% -> 3% of each run, Pallas kernels for 10% -> 12%
where the time goes in v2:
time: 200 us
  waiting for transfers between devices  73.4 us (37%)
  Pallas kernels  37.6 us (19%)
  starting transfers between devices  36.3 us (18%)
  blocking collectives  29.2 us (15%)
  between operations  13.5 us (7%)
  local copies, waits for them, and re-layouts  8.47 us (4%)
    all_to_all x1, blocking collectives, per_device(): lax.all_to_all(partial_sum, TP, split_axis=0, concat_axis=0, tiled=True)  29.2 us
    all_to_all x1, waiting for transfers between devices, per_device(): sent = lax.all_to_all(payload, TP, split_axis=0, concat_axis=0, tiled=True)  27.5 us
    all_to_all x1, waiting for transfers between devices, per_device(): lax.all_to_all(mixed_term.transpose(1, 0, 2), SEQ, split_axis=0, concat_a...  23.2 us
    pallas_call x1, Pallas kernels, long_mixing(): pl.pallas_call(conv_kernel, out_shape=jax.ShapeDtypeStruct(gated.shape, j...  14.4 us
    pallas_call x1, Pallas kernels, feed_forward(): pl.pallas_call(functools.partial(feed_kernel, (units, split, block, per_s...  12.4 us
    all_to_all x1, starting transfers between devices, per_device(): here = lax.all_to_all(sent, SEQ, split_axis=0, concat_axis=0, tiled=True)  12.4 us
    ppermute x4, waiting for transfers between devices, swap(): return lax.ppermute(values, axis, [(0, 1), (1, 0)])  10.7 us
    all_to_all x1, waiting for transfers between devices, per_device(): here = lax.all_to_all(sent, SEQ, split_axis=0, concat_axis=0, tiled=True)  9.98 us
  transfers between devices with their start and end apart: 10, of which 5 were waited for; matrix products, arithmetic and copies ran while one was open for 3% of the time, Pallas kernels for 12%

profile of v2, /device:TPU:1, one launch (start us, length us, event | category | flops | bytes accessed | tf_op | source)
XLA Modules:
  0.0 199.6 jit_solution(8852842674884760222)
XLA Ops:
  6.5 2.0 pack_first.1
  8.6 1.2 slice_bitcast_fusion
  10.0 4.9 %collective-permute-start = (bf16[8,512]{1,0:T(8,128)(2,1)S(1)}, bf16[8,512]{1,0:T(8,128)(2,1)S(1)}, u32[]{:S(2)}, u32[]{:S(2)}) collective-permute-start(bf16[8,512]{1,0:T(8,128)(2,1)S(1)} %pad.9), channel_id=1, source_target_pairs={{0,8},{8,16},{16,24},{24,32},{32,40},{40,48},{48,56},{56,64},{64,7... | collective-permute-start | bytes 24584 | tf_op jit(solution)/shard_map/ppermute | solution.py:342
  14.9 0.8 reshape.15
  15.7 0.6 pad.8.weight_ref
  16.3 0.6 copy-done.5
  16.9 3.8 %make_gated.1 = (bf16[32,2,16,256]{3,2,1,0:T(8,128)(2,1)}, f32[512,256]{1,0:T(8,128)}) custom-call(bf16[3,512,256]{2,1,0:T(8,128)(2,1)} %projected_ref.1, bf16[512,256]{1,0:T(8,128)(2,1)} %taps_ref.1, f32[16,512]{1,0:T(8,128)} %pad.8.weight_ref, bf16[8,512]{1,0:T(8,128)(2,1)} %copy-done.5), custom_call_target="tpu_custom_call" | custom-call | tf_op jit(solution)/shard_map/make_gated/pallas_call | solution.py:40
  20.7 12.4 %all-to-all-start = ((bf16[32,2,16,256]{3,2,1,0:T(8,128)(2,1)}), bf16[32,2,16,256]{3,2,1,0:T(8,128)(2,1)S(1)}, u32[]{:S(2)}, u32[]{:S(2)}) async-start(bf16[32,2,16,256]{3,2,1,0:T(8,128)(2,1)} %get-tuple-element.18), calls=%async_computation | async-start | bytes 1048576 | tf_op jit(solution)/shard_map/all_to_all | solution.py:346
  33.2 3.0 %collective-permute-start.1 = (bf16[34,4096]{1,0:T(8,128)(2,1)S(1)}, bf16[34,4096]{1,0:T(8,128)(2,1)S(1)}, u32[]{:S(2)}, u32[]{:S(2)}) collective-permute-start(bf16[34,4096]{1,0:T(8,128)(2,1)S(1)} %copy-done.2), channel_id=1, source_target_pairs={{0,128},{128,0},{1,129},{129,1},{2,130},{130,2},{3,131},{131,3},{4... | collective-permute-start | bytes 835592 | tf_op jit(solution)/shard_map/ppermute | solution.py:325
  36.2 10.7 %collective-permute-done.1.other_ref = bf16[34,4096]{1,0:T(8,128)(2,1)S(1)} collective-permute-done((bf16[34,4096]{1,0:T(8,128)(2,1)S(1)}, bf16[34,4096]{1,0:T(8,128)(2,1)S(1)}, u32[]{:S(2)}, u32[]{:S(2)}) %collective-permute-start.1) | collective-permute-done | bytes 278560 | tf_op jit(solution)/shard_map/ppermute | solution.py:325
  46.9 10.0 %all-to-all-done = bf16[32,2,16,256]{3,2,1,0:T(8,128)(2,1)S(1)} async-done(((bf16[32,2,16,256]{3,2,1,0:T(8,128)(2,1)}), bf16[32,2,16,256]{3,2,1,0:T(8,128)(2,1)S(1)}, u32[]{:S(2)}, u32[]{:S(2)}) %all-to-all-start) | async-done | bytes 524320 | tf_op jit(solution)/shard_map/all_to_all | solution.py:346
  56.9 2.0 pack_second.1
  58.9 1.9 all-gather.3.cloned.1.call-done.p0_ref
  60.9 2.7 %collective-permute-start.2 = (bf16[256,4096]{1,0:T(8,128)(2,1)}, bf16[256,4096]{1,0:T(8,128)(2,1)}, u32[]{:S(2)}, u32[]{:S(2)}) collective-permute-start(bf16[256,4096]{1,0:T(8,128)(2,1)} %all-gather.3.cloned.1.call-done.p0_ref), channel_id=1, source_target_pairs={{0,128},{128,0},{1,129},{129,1},{2,130},{130,2},{3,131},{131,3},{4... | collective-permute-start | bytes 6291464 | tf_op jit(solution)/shard_map/ppermute | solution.py:325
  63.6 0.8 dynamic_slice.6.bias_ref
  64.3 0.3 copy.24
  64.8 14.4 %long_mixing.1 = bf16[16,32,256]{2,1,0:T(8,128)(2,1)S(1)} custom-call(f32[16]{0:T(128)S(1)} %dynamic_slice.6.bias_ref, bf16[16,32,256]{2,1,0:T(8,128)(2,1)S(1)} %get-tuple-element.30.gated_ref, bf16[16,1,8192]{2,1,0:T(2,128)(2,1)S(1)} %reshape_reshape_squeeze.4.taps_ref), custom_call_target="tpu_custom_call" | custom-call | flops 8589934592 | bytes 786432 | tf_op jit(solution)/shard_map/long_mixing/pallas_call | solution.py:156
  79.3 0.9 copy.20
  80.1 7.7 %all-to-all-start.1 = ((bf16[32,16,256]{2,1,0:T(8,128)(2,1)}), bf16[32,16,256]{2,1,0:T(8,128)(2,1)S(1)}, u32[]{:S(2)}, u32[]{:S(2)}) async-start(bf16[32,16,256]{2,1,0:T(8,128)(2,1)} %copy.20), calls=%async_computation.1 | async-start | bytes 524288 | tf_op jit(solution)/shard_map/all_to_all | solution.py:358
  87.9 0.8 dynamic_slice.7
  88.6 0.9 copy.21.gain_ref
  89.8 23.2 %all-to-all-done.1 = bf16[32,16,256]{2,1,0:T(8,128)(2,1)S(1)} async-done(((bf16[32,16,256]{2,1,0:T(8,128)(2,1)}), bf16[32,16,256]{2,1,0:T(8,128)(2,1)S(1)}, u32[]{:S(2)}, u32[]{:S(2)}) %all-to-all-start.1) | async-done | bytes 262176 | tf_op jit(solution)/shard_map/all_to_all | solution.py:358
  113.0 0.7 copy-done.1
  113.7 2.9 %make_payload.1 = (bf16[512,256]{1,0:T(8,128)(2,1)}, bf16[8,528,256]{2,1,0:T(8,128)(2,1)}) custom-call(f32[512,256]{1,0:T(8,128)} %get-tuple-element.17.query_ref, bf16[512,256]{1,0:T(8,128)(2,1)} %bitcast.20, f32[512,1]{1,0:T(8,128)} %copy.21.gain_ref), custom_call_target="tpu_custom_call" | custom-call | tf_op jit(solution)/shard_map/make_payload/pallas_call | solution.py:186
  116.6 0.5 collective-permute-start.4
  117.1 4.8 %all-to-all-start.2 = ((bf16[8,528,256]{2,1,0:T(8,128)(2,1)}), bf16[8,528,256]{2,1,0:T(8,128)(2,1)}, u32[]{:S(2)}, u32[]{:S(2)}) async-start(bf16[8,528,256]{2,1,0:T(8,128)(2,1)} %get-tuple-element.26), calls=%async_computation.2 | async-start | bytes 4325376 | tf_op jit(solution)/shard_map/all_to_all | solution.py:367
  121.9 27.5 %all-to-all-done.2.sent_ref = bf16[8,528,256]{2,1,0:T(8,128)(2,1)} async-done(((bf16[8,528,256]{2,1,0:T(8,128)(2,1)}), bf16[8,528,256]{2,1,0:T(8,128)(2,1)}, u32[]{:S(2)}, u32[]{:S(2)}) %all-to-all-start.2) | async-done | bytes 2162720 | tf_op jit(solution)/shard_map/all_to_all | solution.py:367
  149.4 12.4 %feed_forward.1 = bf16[8,256,512]{2,1,0:T(8,128)(2,1)S(1)} custom-call(s32[1]{0:T(128)} %bitcast.7.core_ref, bf16[8,528,256]{2,1,0:T(8,128)(2,1)} %all-to-all-done.2.sent_ref, bf16[1152,4096]{1,0:T(8,128)(2,1)} %all-gather.5.cloned.1.call-done.weight_ref, bf16[256,4096]{1,0:T(8,128)(2,1)S(1)} %copy-done, bf16[256,4096]{1,0:T(8,128)(2,1)} %collective-permute-done.3.p1_ref, ...), custom_call_target="tpu_custom_call" | custom-call | flops 10000000000 | bytes 30000000 | tf_op jit(solution)/shard_map/feed_forward/pallas_call | solution.py:291
  161.9 29.2 %all_to_all.20 = bf16[8,256,512]{2,1,0:T(8,128)(2,1)S(1)} all-to-all(bf16[8,256,512]{2,1,0:T(8,128)(2,1)S(1)} %feed_forward.1), channel_id=1, replica_groups=mesh['xh'=2,'z'=8,'core'=2,'y'=4,'xl'=2] {'y','xl'}, dimensions={0} | all-to-all | bytes 4194304 | tf_op jit(solution)/shard_map/all_to_all | solution.py:370
  191.1 0.3 convert_reduce_fusion
  191.6 0.4 copy-done.4
  192.0 0.8 fusion
  (25 shorter events, 0.9 us)
Async XLA Ops:
  6.5 54.3 %all-gather.3.cloned.1.call-start = ((), (), s32[]{:S(2)}) async-start(), calls=%async_computation.4 | async-start | bytes 2359296 | tf_op jit(solution)/shard_map/all_gather | solution.py:340
  8.5 24.7 %copy-start.2 = (bf16[34,4096]{1,0:T(8,128)(2,1)S(1)}, bf16[34,4096]{1,0:T(8,128)(2,1)}, u32[]{:S(2)}) copy-start(bf16[34,4096]{1,0:T(8,128)(2,1)} %get-tuple-element.19.pair_ref) | copy-start | bytes 835588
  10.0 6.3 %collective-permute-start = (bf16[8,512]{1,0:T(8,128)(2,1)S(1)}, bf16[8,512]{1,0:T(8,128)(2,1)S(1)}, u32[]{:S(2)}, u32[]{:S(2)}) collective-permute-start(bf16[8,512]{1,0:T(8,128)(2,1)S(1)} %pad.9), channel_id=1, source_target_pairs={{0,8},{8,16},{16,24},{24,32},{32,40},{40,48},{48,56},{56,64},{64,7... | collective-permute-start | bytes 24584 | tf_op jit(solution)/shard_map/ppermute | solution.py:342
  16.3 0.6 copy-start.5
  20.7 36.2 %all-to-all-start = ((bf16[32,2,16,256]{3,2,1,0:T(8,128)(2,1)}), bf16[32,2,16,256]{3,2,1,0:T(8,128)(2,1)S(1)}, u32[]{:S(2)}, u32[]{:S(2)}) async-start(bf16[32,2,16,256]{3,2,1,0:T(8,128)(2,1)} %get-tuple-element.18), calls=%async_computation | async-start | bytes 1048576 | tf_op jit(solution)/shard_map/all_to_all | solution.py:346
  33.2 116.3 %all-gather.5.cloned.1.call-start = ((), (), s32[]{:S(2)}) async-start(), calls=%async_computation.5 | async-start | bytes 10027008 | tf_op jit(solution)/shard_map/all_gather | solution.py:351
  33.2 13.7 %collective-permute-start.1 = (bf16[34,4096]{1,0:T(8,128)(2,1)S(1)}, bf16[34,4096]{1,0:T(8,128)(2,1)S(1)}, u32[]{:S(2)}, u32[]{:S(2)}) collective-permute-start(bf16[34,4096]{1,0:T(8,128)(2,1)S(1)} %copy-done.2), channel_id=1, source_target_pairs={{0,128},{128,0},{1,129},{129,1},{2,130},{130,2},{3,131},{131,3},{4... | collective-permute-start | bytes 835592 | tf_op jit(solution)/shard_map/ppermute | solution.py:325
  46.9 10.0 %copy-start.3 = (bf16[34,4096]{1,0:T(8,128)(2,1)}, bf16[34,4096]{1,0:T(8,128)(2,1)S(1)}, u32[]{:S(2)}) copy-start(bf16[34,4096]{1,0:T(8,128)(2,1)S(1)} %collective-permute-done.1.other_ref) | copy-start | bytes 835588
  60.9 55.7 %collective-permute-start.2 = (bf16[256,4096]{1,0:T(8,128)(2,1)}, bf16[256,4096]{1,0:T(8,128)(2,1)}, u32[]{:S(2)}, u32[]{:S(2)}) collective-permute-start(bf16[256,4096]{1,0:T(8,128)(2,1)} %all-gather.3.cloned.1.call-done.p0_ref), channel_id=1, source_target_pairs={{0,128},{128,0},{1,129},{129,1},{2,130},{130,2},{3,131},{131,3},{4... | collective-permute-start | bytes 6291464 | tf_op jit(solution)/shard_map/ppermute | solution.py:325
  64.8 24.7 %copy-start = (bf16[256,4096]{1,0:T(8,128)(2,1)S(1)}, bf16[256,4096]{1,0:T(8,128)(2,1)}, u32[]{:S(2)}) copy-start(bf16[256,4096]{1,0:T(8,128)(2,1)} %all-gather.3.cloned.1.call-done.p0_ref) | copy-start | bytes 6291460
  80.1 32.9 %all-to-all-start.1 = ((bf16[32,16,256]{2,1,0:T(8,128)(2,1)}), bf16[32,16,256]{2,1,0:T(8,128)(2,1)S(1)}, u32[]{:S(2)}, u32[]{:S(2)}) async-start(bf16[32,16,256]{2,1,0:T(8,128)(2,1)} %copy.20), calls=%async_computation.1 | async-start | bytes 524288 | tf_op jit(solution)/shard_map/all_to_all | solution.py:358
  89.5 32.4 %collective-permute-start.3 = (bf16[256,4096]{1,0:T(8,128)(2,1)S(1)}, bf16[256,4096]{1,0:T(8,128)(2,1)}, u32[]{:S(2)}, u32[]{:S(2)}) collective-permute-start(bf16[256,4096]{1,0:T(8,128)(2,1)S(1)} %copy-done), channel_id=1, source_target_pairs={{0,8},{8,0},{1,9},{9,1},{2,10},{10,2},{3,11},{11,3},{4,12},{12,4},... | collective-permute-start | bytes 6291464 | tf_op jit(solution)/shard_map/ppermute | solution.py:325
  113.0 0.7 copy-start.1
  116.6 32.8 %collective-permute-start.4 = (bf16[256,4096]{1,0:T(8,128)(2,1)}, bf16[256,4096]{1,0:T(8,128)(2,1)}, u32[]{:S(2)}, u32[]{:S(2)}) collective-permute-start(bf16[256,4096]{1,0:T(8,128)(2,1)} %collective-permute-done.2.p2_ref), channel_id=1, source_target_pairs={{0,8},{8,0},{1,9},{9,1},{2,10},{10,2},{3,11},{11,3},{4,12},{12,4},... | collective-permute-start | bytes 6291464 | tf_op jit(solution)/shard_map/ppermute | solution.py:325
  117.1 32.3 %all-to-all-start.2 = ((bf16[8,528,256]{2,1,0:T(8,128)(2,1)}), bf16[8,528,256]{2,1,0:T(8,128)(2,1)}, u32[]{:S(2)}, u32[]{:S(2)}) async-start(bf16[8,528,256]{2,1,0:T(8,128)(2,1)} %get-tuple-element.26), calls=%async_computation.2 | async-start | bytes 4325376 | tf_op jit(solution)/shard_map/all_to_all | solution.py:367
  191.1 1.0 copy-start.4
Sparse Core Ops, SparseCore 0:
  9.1 51.6 all-gather.2
  62.7 67.7 all-gather.4

commit v3 on v2

--- a/solution.py
+++ b/solution.py
@@ -47,22 +47,21 @@
     )(projected, taps, jnp.pad(weights, ((0, 7), (0, 0))), edge)
 
 
-def pack_first_kernel(split, gate_ref, up_ref, down_ref, first_ref, pair_ref):
+def pack_first_kernel(gate_ref, up_ref, down_ref, first_ref, pair_ref):
     gate, up = gate_ref[...].astype(jnp.float32), up_ref[...].astype(jnp.float32)
     down = down_ref[...].astype(jnp.float32)
-    first = jnp.concatenate([down, gate[split:], up[split:]], axis=0)
-    first_ref[...] = first.astype(jnp.bfloat16)
-    pair_ref[...] = jnp.concatenate([gate[:split], up[:split]], axis=0).astype(jnp.bfloat16)
+    blank = jnp.zeros((first_ref.shape[0] - down.shape[0], down.shape[1]), jnp.float32)
+    first_ref[...] = jnp.concatenate([down, blank], axis=0).astype(jnp.bfloat16)
+    pair_ref[...] = jnp.concatenate([gate, up], axis=0).astype(jnp.bfloat16)
 
 
 def pack_first(gate, up, down):
     rows, width = gate.shape
-    split = rows - (-rows % 16) // 2
-    return pl.pallas_call(
-        functools.partial(pack_first_kernel, split),
+    return pl.pallas_call(
+        pack_first_kernel,
         out_shape=(
-            jax.ShapeDtypeStruct((rows + 2 * (rows - split), width), gate.dtype),
-            jax.ShapeDtypeStruct((2 * split, width), gate.dtype),
+            jax.ShapeDtypeStruct((rows + -rows % 8, width), gate.dtype),
+            jax.ShapeDtypeStruct((2 * rows, width), gate.dtype),
         ),
         name="pack_first",
     )(gate, up, down)
@@ -70,32 +69,31 @@
 
 def pack_second_kernel(pair_ref, other_ref, out_ref):
     pair, other = pair_ref[...].astype(jnp.float32), other_ref[...].astype(jnp.float32)
-    blank = jnp.zeros((out_ref.shape[0] - 2 * pair.shape[0], pair.shape[1]), jnp.float32)
-    out_ref[...] = jnp.concatenate([pair, other, blank], axis=0).astype(jnp.bfloat16)
+    out_ref[...] = jnp.concatenate([pair, other], axis=0).astype(jnp.bfloat16)
 
 
 def pack_second(pair, other):
-    rows = 2 * pair.shape[0]
     return pl.pallas_call(
         pack_second_kernel,
-        out_shape=jax.ShapeDtypeStruct((rows + -rows % 8, pair.shape[1]), pair.dtype),
+        out_shape=jax.ShapeDtypeStruct((2 * pair.shape[0], pair.shape[1]), pair.dtype),
         name="pack_second",
     )(pair, other)
 
 
 def build_table(taps_ref, channel, table_ref):
     seq_len = taps_ref.shape[2]
-    base = jnp.broadcast_to(taps_ref[channel].astype(jnp.float32), (8, seq_len))
+    taps = jnp.broadcast_to(taps_ref[channel].astype(jnp.float32), (8, seq_len))
+    base = jnp.concatenate([taps, jnp.zeros((8, LANES), jnp.float32)], axis=1)
     base = pltpu.roll(base, 0, 1, stride=1, stride_axis=0)
-    lane = lax.broadcasted_iota(jnp.int32, (8, seq_len), 1)
-    row = lax.broadcasted_iota(jnp.int32, (8, seq_len), 0)
-    base = jnp.where(lane >= row, base, 0.0)
     for pair in range(LANES // 16):
         parts = []
         for shift in (16 * pair, 16 * pair + 8):
             moved = pltpu.roll(base, shift, 1) if shift else base
-            parts.append(jnp.where(lane >= shift, moved, 0.0) if shift else moved)
-        table_ref[16 * pair : 16 * pair + 16, :] = jnp.concatenate(parts, axis=0).astype(jnp.bfloat16)
+            parts.append(moved[:, :seq_len])
+        table_ref[16 * pair : 16 * pair + 16, :] = jnp.concatenate(parts, axis=0).astype(
+            jnp.bfloat16
+        )
+
 
 def apply_table(gated_ref, bias_ref, channel, table_ref, out_ref):
     rows = gated_ref.shape[1]
@@ -193,22 +191,20 @@
     )(query, mixed, gain.reshape(rows, 1))
 
 
-def gated_product(gate, up):
-    return gate / (1.0 + jnp.exp(-gate)) * up
-
-
 def feed_kernel(
     sizes, core_ref, sent_ref, weight_ref, p0_ref, p1_ref, p2_ref, p3_ref, out_ref,
     x_ref, scale_ref, hidden_ref, flat_ref, piece_ref, piece_sem,
 ):
-    units, split, block, per_step, first_steps = sizes
+    units, block, per_step, first_steps = sizes
     step = pl.program_id(0)
     members, rows = sent_ref.shape[0], out_ref.shape[2]
     core = core_ref[0]
-    copies = [
-        pltpu.make_async_copy(ref, piece_ref.at[index], piece_sem.at[index])
-        for index, ref in enumerate((p0_ref, p1_ref, p2_ref, p3_ref))
-    ]
+    length = p0_ref.shape[0]
+    copies = []
+    for index, ref in enumerate((p0_ref, p1_ref, p2_ref, p3_ref)):
+        slot = 2 * (index // 2) + (core if index % 2 == 0 else 1 - core)
+        target = piece_ref.at[pl.ds(pl.multiple_of(slot * length, 16), length), :]
+        copies.append(pltpu.make_async_copy(ref, target, piece_sem.at[index]))
 
     @pl.when(step == 0)
     def _():
@@ -230,13 +226,13 @@
         for index in range(per_step):
             part = sums[index * height : (index + 1) * height]
             for side in range(2):
-                base = 2 * side * split
-                value = gated_product(
-                    part[base : base + split], part[base + split : base + 2 * split]
-                )
-                blank = jnp.zeros((block - split, value.shape[1]), jnp.float32)
-                start = pl.multiple_of((step * (per_step // 2) + index // 2) * block, 8)
-                hidden_ref[side, index % 2, pl.ds(start, block), :] = jnp.concatenate(
+                base = 2 * side * units
+                gate, up = part[base : base + units], part[base + units : base + 2 * units]
+                value = gate / (1.0 + jnp.exp(-gate)) * up
+                blank = jnp.zeros((block - units, value.shape[1]), jnp.float32)
+                start = (2 * side + index % 2) * length
+                start += (step * (per_step // 2) + index // 2) * block
+                hidden_ref[pl.ds(pl.multiple_of(start, 8), block), :] = jnp.concatenate(
                     [value, blank], axis=0
                 )
 
@@ -244,52 +240,31 @@
     def _():
         for copy in copies:
             copy.wait()
-        scale = scale_ref[0:1, :]
-        count = piece_ref.shape[1] // block
-        for index in range(4):
-            tails = [
-                piece_ref[index, z * block + block // 2 : (z + 1) * block, :] for z in range(count)
-            ]
-            sums = jnp.dot(
-                jnp.concatenate(tails, axis=0), x_ref[...], preferred_element_type=jnp.float32
-            )
-            sums = sums * scale
-            place = core if index % 2 == 0 else 1 - core
-            for z in range(count):
-                gate_at = z * (block // 2) + units - block // 2
-                up_at = gate_at + units - split
-                value = gated_product(sums[gate_at:up_at], sums[up_at : up_at + units - split])
-                hidden_ref[index // 2, place, z * block + split : z * block + units, :] = value
-            flat_ref[index] = hidden_ref[index // 2, place].T.astype(jnp.bfloat16)
+        flat_ref[...] = hidden_ref[...].T.astype(jnp.bfloat16)
 
     @pl.when(step >= first_steps)
     def _():
         wide = out_ref.shape[0] * rows
         start = pl.multiple_of((step - first_steps) * wide, LANES)
-        total = None
-        for index in range(4):
-            part = jnp.dot(
-                flat_ref[index],
-                piece_ref[index, :, pl.ds(start, wide)],
-                preferred_element_type=jnp.float32,
-            )
-            total = part if total is None else total + part
+        total = jnp.dot(
+            flat_ref[...], piece_ref[:, pl.ds(start, wide)], preferred_element_type=jnp.float32
+        )
         for member in range(out_ref.shape[0]):
             out_ref[member] = total[:, member * rows : (member + 1) * rows].astype(jnp.bfloat16)
 
 
-def feed_forward(sent, weights, pieces, core, units, split):
+def feed_forward(sent, weights, pieces, core, units):
     members, padded, width = sent.shape
     channels = weights.shape[1]
     rows = channels // members
     length = pieces[0].shape[0]
-    block = 2 * units - split + units - split
+    block = units + -units % 8
     blocks = 2 * length // block
     per_step, out_step = 4, 2
     first_steps = blocks // per_step
     anywhere = pl.BlockSpec(memory_space=pl.ANY)
     return pl.pallas_call(
-        functools.partial(feed_kernel, (units, split, block, per_step, first_steps)),
+        functools.partial(feed_kernel, (units, block, per_step, first_steps)),
         grid=(first_steps + members // out_step,),
         out_shape=jax.ShapeDtypeStruct((members, width, rows), jnp.bfloat16),
         in_specs=[
@@ -310,9 +285,9 @@
         scratch_shapes=[
             pltpu.VMEM((channels, width), jnp.bfloat16),
             pltpu.VMEM((8, width), jnp.float32),
-            pltpu.VMEM((2, 2, length, width), jnp.float32),
-            pltpu.VMEM((4, width, length), jnp.bfloat16),
-            pltpu.VMEM((4, length, channels), jnp.bfloat16),
+            pltpu.VMEM((4 * length, width), jnp.float32),
+            pltpu.VMEM((width, 4 * length), jnp.bfloat16),
+            pltpu.VMEM((4 * length, channels), jnp.bfloat16),
             pltpu.SemaphoreType.DMA((4,)),
         ],
         compiler_params=pltpu.CompilerParams(vmem_limit_bytes=48 * 1024 * 1024),
@@ -355,6 +330,7 @@
     near = swap(own_near, "xh")
     here = here.transpose(1, 2, 0, 3)
     mixed_term = long_mixing(here[0], here[1].reshape(per_group, seq_len), bias_part)
+    mixed_term, own_far = lax.optimization_barrier((mixed_term, own_far))
     returned = lax.all_to_all(
         mixed_term.transpose(1, 0, 2), SEQ, split_axis=0, concat_axis=0, tiled=True
     )
@@ -365,8 +341,7 @@
     payload, near = lax.optimization_barrier((payload, near))
     pieces = (own_near, own_far, near, swap(near, "core"))
     sent = lax.all_to_all(payload, TP, split_axis=0, concat_axis=0, tiled=True)
-    units, split = gate_weight.shape[0], pair.shape[0] // 2
-    partial_sum = feed_forward(sent, gate_up, pieces, core.reshape(1), units, split)
+    partial_sum = feed_forward(sent, gate_up, pieces, core.reshape(1), gate_weight.shape[0])
     shares = lax.all_to_all(partial_sum, TP, split_axis=0, concat_axis=0, tiled=True)
     feed_out = jnp.sum(shares.astype(jnp.float32), axis=0).T
     return (hyena.astype(jnp.float32) + feed_out).astype(jnp.bfloat16)

time: 200 us -> 189 us (0.945)
  waiting for transfers between devices: 73.4 us -> 62.5 us
    all_to_all x1, waiting for transfers between devices: 23.2 us -> 15.8 us  [per_device(): lax.all_to_all(mixed_term.transpose(1, 0, 2), SEQ, split_axis=0, concat_a...]
    ppermute x4, waiting for transfers between devices: 10.7 us -> 16.2 us  [swap(): return lax.ppermute(values, axis, [(0, 1), (1, 0)])]
    all_to_all x1, waiting for transfers between devices: 27.5 us -> 22.9 us  [per_device(): sent = lax.all_to_all(payload, TP, split_axis=0, concat_axis=0, tiled=True)]
    all_to_all x1, starting transfers between devices: 7.75 us -> 5.11 us  [per_device(): lax.all_to_all(mixed_term.transpose(1, 0, 2), SEQ, split_axis=0, concat_a...]
    all_to_all x1, waiting for transfers between devices: 9.98 us -> 7.54 us  [per_device(): here = lax.all_to_all(sent, SEQ, split_axis=0, concat_axis=0, tiled=True)]
where the time goes in v3:
time: 189 us
  waiting for transfers between devices  62.5 us (33%)
  starting transfers between devices  36.3 us (19%)
  Pallas kernels  35.9 us (19%)
  blocking collectives  31.1 us (16%)
  between operations  13.5 us (7%)
  local copies, waits for them, and re-layouts  8.45 us (4%)
    all_to_all x1, blocking collectives, per_device(): lax.all_to_all(partial_sum, TP, split_axis=0, concat_axis=0, tiled=True)  31.1 us
    all_to_all x1, waiting for transfers between devices, per_device(): sent = lax.all_to_all(payload, TP, split_axis=0, concat_axis=0, tiled=True)  22.9 us
    ppermute x4, waiting for transfers between devices, swap(): return lax.ppermute(values, axis, [(0, 1), (1, 0)])  16.2 us
    all_to_all x1, waiting for transfers between devices, per_device(): lax.all_to_all(mixed_term.transpose(1, 0, 2), SEQ, split_axis=0, concat_a...  15.8 us
    pallas_call x1, Pallas kernels, long_mixing(): pl.pallas_call(conv_kernel, out_shape=jax.ShapeDtypeStruct(gated.shape, j...  13.7 us
    all_to_all x1, starting transfers between devices, per_device(): here = lax.all_to_all(sent, SEQ, split_axis=0, concat_axis=0, tiled=True)  12.4 us
    pallas_call x1, Pallas kernels, feed_forward(): pl.pallas_call(functools.partial(feed_kernel, (units, block, per_step, fi...  11.5 us
    ppermute x4, starting transfers between devices, swap(): return lax.ppermute(values, axis, [(0, 1), (1, 0)])  8.34 us
  transfers between devices with their start and end apart: 10, of which 5 were waited for; matrix products, arithmetic and copies ran while one was open for 3% of the time, Pallas kernels for 12%

profile of v3, /device:TPU:1, one launch (start us, length us, event | category | flops | bytes accessed | tf_op | source)
XLA Modules:
  0.0 188.7 jit_solution(4318862769167616815)
XLA Ops:
  6.5 2.0 %pack_first.1 = (bf16[24,4096]{1,0:T(8,128)(2,1)}, bf16[44,4096]{1,0:T(8,128)(2,1)}) custom-call(bf16[22,4096]{1,0:T(8,128)(2,1)} %gate_ref.1, bf16[22,4096]{1,0:T(8,128)(2,1)} %up_ref.1, bf16[22,4096]{1,0:T(8,128)(2,1)} %down_ref.1), custom_call_target="tpu_custom_call" | custom-call | tf_op jit(solution)/shard_map/pack_first/pallas_call | solution.py:60
  8.5 1.2 slice_bitcast_fusion
  10.0 4.9 %collective-permute-start = (bf16[8,512]{1,0:T(8,128)(2,1)S(1)}, bf16[8,512]{1,0:T(8,128)(2,1)S(1)}, u32[]{:S(2)}, u32[]{:S(2)}) collective-permute-start(bf16[8,512]{1,0:T(8,128)(2,1)S(1)} %pad.9), channel_id=1, source_target_pairs={{0,8},{8,16},{16,24},{24,32},{32,40},{40,48},{48,56},{56,64},{64,7... | collective-permute-start | bytes 24584 | tf_op jit(solution)/shard_map/ppermute | solution.py:317
  14.9 0.8 reshape.15
  15.7 0.6 pad.8.weight_ref
  16.3 0.6 copy-done.5
  16.9 3.8 %make_gated.1 = (bf16[32,2,16,256]{3,2,1,0:T(8,128)(2,1)}, f32[512,256]{1,0:T(8,128)}) custom-call(bf16[3,512,256]{2,1,0:T(8,128)(2,1)} %projected_ref.1, bf16[512,256]{1,0:T(8,128)(2,1)} %taps_ref.1, f32[16,512]{1,0:T(8,128)} %pad.8.weight_ref, bf16[8,512]{1,0:T(8,128)(2,1)} %copy-done.5), custom_call_target="tpu_custom_call" | custom-call | tf_op jit(solution)/shard_map/make_gated/pallas_call | solution.py:40
  20.7 12.4 %all-to-all-start = ((bf16[32,2,16,256]{3,2,1,0:T(8,128)(2,1)}), bf16[32,2,16,256]{3,2,1,0:T(8,128)(2,1)S(1)}, u32[]{:S(2)}, u32[]{:S(2)}) async-start(bf16[32,2,16,256]{3,2,1,0:T(8,128)(2,1)} %get-tuple-element.20), calls=%async_computation | async-start | bytes 1048576 | tf_op jit(solution)/shard_map/all_to_all | solution.py:321
  33.2 3.0 %collective-permute-start.1 = (bf16[44,4096]{1,0:T(8,128)(2,1)S(1)}, bf16[44,4096]{1,0:T(8,128)(2,1)S(1)}, u32[]{:S(2)}, u32[]{:S(2)}) collective-permute-start(bf16[44,4096]{1,0:T(8,128)(2,1)S(1)} %copy-done.2), channel_id=1, source_target_pairs={{0,128},{128,0},{1,129},{129,1},{2,130},{130,2},{3,131},{131,3},{4... | collective-permute-start | bytes 1081352 | tf_op jit(solution)/shard_map/ppermute | solution.py:300
  36.2 12.8 %collective-permute-done.1.other_ref = bf16[44,4096]{1,0:T(8,128)(2,1)S(1)} collective-permute-done((bf16[44,4096]{1,0:T(8,128)(2,1)S(1)}, bf16[44,4096]{1,0:T(8,128)(2,1)S(1)}, u32[]{:S(2)}, u32[]{:S(2)}) %collective-permute-start.1) | collective-permute-done | bytes 360480 | tf_op jit(solution)/shard_map/ppermute | solution.py:300
  49.0 7.5 %all-to-all-done = bf16[32,2,16,256]{3,2,1,0:T(8,128)(2,1)S(1)} async-done(((bf16[32,2,16,256]{3,2,1,0:T(8,128)(2,1)}), bf16[32,2,16,256]{3,2,1,0:T(8,128)(2,1)S(1)}, u32[]{:S(2)}, u32[]{:S(2)}) %all-to-all-start) | async-done | bytes 524320 | tf_op jit(solution)/shard_map/all_to_all | solution.py:321
  56.6 2.1 %pack_second.1 = bf16[88,4096]{1,0:T(8,128)(2,1)} custom-call(bf16[44,4096]{1,0:T(8,128)(2,1)} %get-tuple-element.21.pair_ref, bf16[44,4096]{1,0:T(8,128)(2,1)} %copy-done.3), custom_call_target="tpu_custom_call" | custom-call | tf_op jit(solution)/shard_map/pack_second/pallas_call | solution.py:76
  58.7 2.0 %collective-permute-start.2 = (bf16[192,4096]{1,0:T(8,128)(2,1)}, bf16[192,4096]{1,0:T(8,128)(2,1)S(1)}, u32[]{:S(2)}, u32[]{:S(2)}) collective-permute-start(bf16[192,4096]{1,0:T(8,128)(2,1)} %all-gather.3.cloned.1.call-done.p0_ref), channel_id=1, source_target_pairs={{0,8},{8,0},{1,9},{9,1},{2,10},{10,2},{3,11},{11,3},{4,12},{12,4},... | collective-permute-start | bytes 4718600 | tf_op jit(solution)/shard_map/ppermute | solution.py:300
  60.7 2.6 %collective-permute-start.3 = (bf16[192,4096]{1,0:T(8,128)(2,1)}, bf16[192,4096]{1,0:T(8,128)(2,1)}, u32[]{:S(2)}, u32[]{:S(2)}) collective-permute-start(bf16[192,4096]{1,0:T(8,128)(2,1)} %all-gather.3.cloned.1.call-done.p0_ref), channel_id=1, source_target_pairs={{0,128},{128,0},{1,129},{129,1},{2,130},{130,2},{3,131},{131,3},{4... | collective-permute-start | bytes 4718600 | tf_op jit(solution)/shard_map/ppermute | solution.py:300
  63.3 0.8 dynamic_slice.6.bias_ref
  64.5 13.7 %long_mixing.1 = bf16[16,32,256]{2,1,0:T(8,128)(2,1)S(1)} custom-call(f32[16]{0:T(128)S(1)} %dynamic_slice.6.bias_ref, bf16[16,32,256]{2,1,0:T(8,128)(2,1)S(1)} %get-tuple-element.34.gated_ref, bf16[16,1,8192]{2,1,0:T(2,128)(2,1)S(1)} %reshape_reshape_squeeze.4.taps_ref), custom_call_target="tpu_custom_call" | custom-call | flops 8589934592 | bytes 786432 | tf_op jit(solution)/shard_map/long_mixing/pallas_call | solution.py:154
  78.2 0.9 copy.20
  79.1 5.1 %all-to-all-start.1 = ((bf16[32,16,256]{2,1,0:T(8,128)(2,1)}), bf16[32,16,256]{2,1,0:T(8,128)(2,1)S(1)}, u32[]{:S(2)}, u32[]{:S(2)}) async-start(bf16[32,16,256]{2,1,0:T(8,128)(2,1)} %copy.20), calls=%async_computation.1 | async-start | bytes 524288 | tf_op jit(solution)/shard_map/all_to_all | solution.py:334
  84.2 0.8 dynamic_slice.7
  85.0 0.9 copy.21.gain_ref
  85.8 15.8 %all-to-all-done.1 = bf16[32,16,256]{2,1,0:T(8,128)(2,1)S(1)} async-done(((bf16[32,16,256]{2,1,0:T(8,128)(2,1)}), bf16[32,16,256]{2,1,0:T(8,128)(2,1)S(1)}, u32[]{:S(2)}, u32[]{:S(2)}) %all-to-all-start.1) | async-done | bytes 262176 | tf_op jit(solution)/shard_map/all_to_all | solution.py:334
  101.6 0.7 copy-done.1
  102.3 2.8 %make_payload.1 = (bf16[512,256]{1,0:T(8,128)(2,1)}, bf16[8,528,256]{2,1,0:T(8,128)(2,1)}) custom-call(f32[512,256]{1,0:T(8,128)} %get-tuple-element.19.query_ref, bf16[512,256]{1,0:T(8,128)(2,1)} %bitcast.20, f32[512,1]{1,0:T(8,128)} %copy.21.gain_ref), custom_call_target="tpu_custom_call" | custom-call | tf_op jit(solution)/shard_map/make_payload/pallas_call | solution.py:184
  105.1 5.4 %all-to-all-start.2 = ((bf16[8,528,256]{2,1,0:T(8,128)(2,1)}), bf16[8,528,256]{2,1,0:T(8,128)(2,1)}, u32[]{:S(2)}, u32[]{:S(2)}) async-start(bf16[8,528,256]{2,1,0:T(8,128)(2,1)} %get-tuple-element.29), calls=%async_computation.2 | async-start | bytes 4325376 | tf_op jit(solution)/shard_map/all_to_all | solution.py:343
  110.5 0.8 collective-permute-start.4
  111.3 3.4 %collective-permute-done.4.p3_ref = bf16[192,4096]{1,0:T(8,128)(2,1)} collective-permute-done((bf16[192,4096]{1,0:T(8,128)(2,1)}, bf16[192,4096]{1,0:T(8,128)(2,1)}, u32[]{:S(2)}, u32[]{:S(2)}) %collective-permute-start.4) | collective-permute-done | bytes 1572896 | tf_op jit(solution)/shard_map/ppermute | solution.py:300
  114.7 22.9 %all-to-all-done.2.sent_ref = bf16[8,528,256]{2,1,0:T(8,128)(2,1)} async-done(((bf16[8,528,256]{2,1,0:T(8,128)(2,1)}), bf16[8,528,256]{2,1,0:T(8,128)(2,1)}, u32[]{:S(2)}, u32[]{:S(2)}) %all-to-all-start.2) | async-done | bytes 2162720 | tf_op jit(solution)/shard_map/all_to_all | solution.py:343
  137.6 11.5 %feed_forward.1 = bf16[8,256,512]{2,1,0:T(8,128)(2,1)} custom-call(s32[1]{0:T(128)} %bitcast.7.core_ref, bf16[8,528,256]{2,1,0:T(8,128)(2,1)} %all-to-all-done.2.sent_ref, bf16[1408,4096]{1,0:T(8,128)(2,1)} %all-gather.5.cloned.1.call-done.weight_ref, bf16[192,4096]{1,0:T(8,128)(2,1)S(1)} %copy-done, bf16[192,4096]{1,0:T(8,128)(2,1)S(1)} %collective-permute-done.2.p1_ref, ...), custom_call_target="tpu_custom_call" | custom-call | flops 10000000000 | bytes 30000000 | tf_op jit(solution)/shard_map/feed_forward/pallas_call | solution.py:266
  149.1 31.1 %all_to_all.20 = bf16[8,256,512]{2,1,0:T(8,128)(2,1)S(1)} all-to-all(bf16[8,256,512]{2,1,0:T(8,128)(2,1)} %feed_forward.1), channel_id=1, replica_groups=mesh['xh'=2,'z'=8,'core'=2,'y'=4,'xl'=2] {'y','xl'}, dimensions={0} | all-to-all | bytes 4194304 | tf_op jit(solution)/shard_map/all_to_all | solution.py:345
  180.1 0.3 convert_reduce_fusion
  180.7 0.4 copy-done.4
  181.1 0.8 fusion
  (25 shorter events, 1.0 us)
Async XLA Ops:
  6.5 52.2 %all-gather.3.cloned.1.call-start = ((), (), s32[]{:S(2)}) async-start(), calls=%async_computation.4 | async-start | bytes 1769472 | tf_op jit(solution)/shard_map/all_gather | solution.py:315
  8.5 24.7 %copy-start.2 = (bf16[44,4096]{1,0:T(8,128)(2,1)S(1)}, bf16[44,4096]{1,0:T(8,128)(2,1)}, u32[]{:S(2)}) copy-start(bf16[44,4096]{1,0:T(8,128)(2,1)} %get-tuple-element.21.pair_ref) | copy-start | bytes 1081348
  10.0 6.3 %collective-permute-start = (bf16[8,512]{1,0:T(8,128)(2,1)S(1)}, bf16[8,512]{1,0:T(8,128)(2,1)S(1)}, u32[]{:S(2)}, u32[]{:S(2)}) collective-permute-start(bf16[8,512]{1,0:T(8,128)(2,1)S(1)} %pad.9), channel_id=1, source_target_pairs={{0,8},{8,16},{16,24},{24,32},{32,40},{40,48},{48,56},{56,64},{64,7... | collective-permute-start | bytes 24584 | tf_op jit(solution)/shard_map/ppermute | solution.py:317
  16.3 0.6 copy-start.5
  20.7 35.9 %all-to-all-start = ((bf16[32,2,16,256]{3,2,1,0:T(8,128)(2,1)}), bf16[32,2,16,256]{3,2,1,0:T(8,128)(2,1)S(1)}, u32[]{:S(2)}, u32[]{:S(2)}) async-start(bf16[32,2,16,256]{3,2,1,0:T(8,128)(2,1)} %get-tuple-element.20), calls=%async_computation | async-start | bytes 1048576 | tf_op jit(solution)/shard_map/all_to_all | solution.py:321
  33.1 104.4 %all-gather.5.cloned.1.call-start = ((), (), s32[]{:S(2)}) async-start(), calls=%async_computation.5 | async-start | bytes 12255232 | tf_op jit(solution)/shard_map/all_gather | solution.py:326
  33.2 15.8 %collective-permute-start.1 = (bf16[44,4096]{1,0:T(8,128)(2,1)S(1)}, bf16[44,4096]{1,0:T(8,128)(2,1)S(1)}, u32[]{:S(2)}, u32[]{:S(2)}) collective-permute-start(bf16[44,4096]{1,0:T(8,128)(2,1)S(1)} %copy-done.2), channel_id=1, source_target_pairs={{0,128},{128,0},{1,129},{129,1},{2,130},{130,2},{3,131},{131,3},{4... | collective-permute-start | bytes 1081352 | tf_op jit(solution)/shard_map/ppermute | solution.py:300
  49.0 7.5 %copy-start.3 = (bf16[44,4096]{1,0:T(8,128)(2,1)}, bf16[44,4096]{1,0:T(8,128)(2,1)S(1)}, u32[]{:S(2)}) copy-start(bf16[44,4096]{1,0:T(8,128)(2,1)S(1)} %collective-permute-done.1.other_ref) | copy-start | bytes 1081348
  58.7 19.5 %collective-permute-start.2 = (bf16[192,4096]{1,0:T(8,128)(2,1)}, bf16[192,4096]{1,0:T(8,128)(2,1)S(1)}, u32[]{:S(2)}, u32[]{:S(2)}) collective-permute-start(bf16[192,4096]{1,0:T(8,128)(2,1)} %all-gather.3.cloned.1.call-done.p0_ref), channel_id=1, source_target_pairs={{0,8},{8,0},{1,9},{9,1},{2,10},{10,2},{3,11},{11,3},{4,12},{12,4},... | collective-permute-start | bytes 4718600 | tf_op jit(solution)/shard_map/ppermute | solution.py:300
  60.7 44.4 %collective-permute-start.3 = (bf16[192,4096]{1,0:T(8,128)(2,1)}, bf16[192,4096]{1,0:T(8,128)(2,1)}, u32[]{:S(2)}, u32[]{:S(2)}) collective-permute-start(bf16[192,4096]{1,0:T(8,128)(2,1)} %all-gather.3.cloned.1.call-done.p0_ref), channel_id=1, source_target_pairs={{0,128},{128,0},{1,129},{129,1},{2,130},{130,2},{3,131},{131,3},{4... | collective-permute-start | bytes 4718600 | tf_op jit(solution)/shard_map/ppermute | solution.py:300
  79.1 22.5 %all-to-all-start.1 = ((bf16[32,16,256]{2,1,0:T(8,128)(2,1)}), bf16[32,16,256]{2,1,0:T(8,128)(2,1)S(1)}, u32[]{:S(2)}, u32[]{:S(2)}) async-start(bf16[32,16,256]{2,1,0:T(8,128)(2,1)} %copy.20), calls=%async_computation.1 | async-start | bytes 524288 | tf_op jit(solution)/shard_map/all_to_all | solution.py:334
  101.6 0.7 copy-start.1
  105.1 32.4 %copy-start = (bf16[192,4096]{1,0:T(8,128)(2,1)S(1)}, bf16[192,4096]{1,0:T(8,128)(2,1)}, u32[]{:S(2)}) copy-start(bf16[192,4096]{1,0:T(8,128)(2,1)} %all-gather.3.cloned.1.call-done.p0_ref) | copy-start | bytes 4718596
  105.1 32.4 %all-to-all-start.2 = ((bf16[8,528,256]{2,1,0:T(8,128)(2,1)}), bf16[8,528,256]{2,1,0:T(8,128)(2,1)}, u32[]{:S(2)}, u32[]{:S(2)}) async-start(bf16[8,528,256]{2,1,0:T(8,128)(2,1)} %get-tuple-element.29), calls=%async_computation.2 | async-start | bytes 4325376 | tf_op jit(solution)/shard_map/all_to_all | solution.py:343
  110.5 4.2 %collective-permute-start.4 = (bf16[192,4096]{1,0:T(8,128)(2,1)}, bf16[192,4096]{1,0:T(8,128)(2,1)}, u32[]{:S(2)}, u32[]{:S(2)}) collective-permute-start(bf16[192,4096]{1,0:T(8,128)(2,1)} %collective-permute-done.3.p2_ref), channel_id=1, source_target_pairs={{0,8},{8,0},{1,9},{9,1},{2,10},{10,2},{3,11},{11,3},{4,12},{12,4},... | collective-permute-start | bytes 4718600 | tf_op jit(solution)/shard_map/ppermute | solution.py:300
  180.1 1.0 copy-start.4
Sparse Core Ops, SparseCore 0:
  9.1 48.5 all-gather.2
  59.6 77.8 all-gather.4

commit v4 on v3

--- a/solution.py
+++ b/solution.py
@@ -47,21 +47,22 @@
     )(projected, taps, jnp.pad(weights, ((0, 7), (0, 0))), edge)
 
 
-def pack_first_kernel(gate_ref, up_ref, down_ref, first_ref, pair_ref):
+def pack_first_kernel(split, gate_ref, up_ref, down_ref, first_ref, pair_ref):
     gate, up = gate_ref[...].astype(jnp.float32), up_ref[...].astype(jnp.float32)
     down = down_ref[...].astype(jnp.float32)
-    blank = jnp.zeros((first_ref.shape[0] - down.shape[0], down.shape[1]), jnp.float32)
-    first_ref[...] = jnp.concatenate([down, blank], axis=0).astype(jnp.bfloat16)
-    pair_ref[...] = jnp.concatenate([gate, up], axis=0).astype(jnp.bfloat16)
+    first = jnp.concatenate([down, gate[split:], up[split:]], axis=0)
+    first_ref[...] = first.astype(jnp.bfloat16)
+    pair_ref[...] = jnp.concatenate([gate[:split], up[:split]], axis=0).astype(jnp.bfloat16)
 
 
 def pack_first(gate, up, down):
     rows, width = gate.shape
-    return pl.pallas_call(
-        pack_first_kernel,
+    split = rows - (-rows % 16) // 2
+    return pl.pallas_call(
+        functools.partial(pack_first_kernel, split),
         out_shape=(
-            jax.ShapeDtypeStruct((rows + -rows % 8, width), gate.dtype),
-            jax.ShapeDtypeStruct((2 * rows, width), gate.dtype),
+            jax.ShapeDtypeStruct((rows + 2 * (rows - split), width), gate.dtype),
+            jax.ShapeDtypeStruct((2 * split, width), gate.dtype),
         ),
         name="pack_first",
     )(gate, up, down)
@@ -69,13 +70,15 @@
 
 def pack_second_kernel(pair_ref, other_ref, out_ref):
     pair, other = pair_ref[...].astype(jnp.float32), other_ref[...].astype(jnp.float32)
-    out_ref[...] = jnp.concatenate([pair, other], axis=0).astype(jnp.bfloat16)
+    blank = jnp.zeros((out_ref.shape[0] - 2 * pair.shape[0], pair.shape[1]), jnp.float32)
+    out_ref[...] = jnp.concatenate([pair, other, blank], axis=0).astype(jnp.bfloat16)
 
 
 def pack_second(pair, other):
+    rows = 2 * pair.shape[0]
     return pl.pallas_call(
         pack_second_kernel,
-        out_shape=jax.ShapeDtypeStruct((2 * pair.shape[0], pair.shape[1]), pair.dtype),
+        out_shape=jax.ShapeDtypeStruct((rows + -rows % 8, pair.shape[1]), pair.dtype),
         name="pack_second",
     )(pair, other)
 
@@ -85,14 +88,10 @@
     taps = jnp.broadcast_to(taps_ref[channel].astype(jnp.float32), (8, seq_len))
     base = jnp.concatenate([taps, jnp.zeros((8, LANES), jnp.float32)], axis=1)
     base = pltpu.roll(base, 0, 1, stride=1, stride_axis=0)
-    for pair in range(LANES // 16):
-        parts = []
-        for shift in (16 * pair, 16 * pair + 8):
-            moved = pltpu.roll(base, shift, 1) if shift else base
-            parts.append(moved[:, :seq_len])
-        table_ref[16 * pair : 16 * pair + 16, :] = jnp.concatenate(parts, axis=0).astype(
-            jnp.bfloat16
-        )
+    base = jnp.concatenate([base, pltpu.roll(base, 8, 1)], axis=0).astype(jnp.bfloat16)
+    for shift in range(0, LANES, 16):
+        moved = pltpu.roll(base, shift, 1) if shift else base
+        table_ref[shift : shift + 16, :] = moved[:, :seq_len]
 
 
 def apply_table(gated_ref, bias_ref, channel, table_ref, out_ref):
@@ -191,11 +190,15 @@
     )(query, mixed, gain.reshape(rows, 1))
 
 
+def gated_product(gate, up):
+    return gate / (1.0 + jnp.exp(-gate)) * up
+
+
 def feed_kernel(
     sizes, core_ref, sent_ref, weight_ref, p0_ref, p1_ref, p2_ref, p3_ref, out_ref,
     x_ref, scale_ref, hidden_ref, flat_ref, piece_ref, piece_sem,
 ):
-    units, block, per_step, first_steps = sizes
+    units, split, block, per_step, first_steps = sizes
     step = pl.program_id(0)
     members, rows = sent_ref.shape[0], out_ref.shape[2]
     core = core_ref[0]
@@ -226,10 +229,11 @@
         for index in range(per_step):
             part = sums[index * height : (index + 1) * height]
             for side in range(2):
-                base = 2 * side * units
-                gate, up = part[base : base + units], part[base + units : base + 2 * units]
-                value = gate / (1.0 + jnp.exp(-gate)) * up
-                blank = jnp.zeros((block - units, value.shape[1]), jnp.float32)
+                base = 2 * side * split
+                value = gated_product(
+                    part[base : base + split], part[base + split : base + 2 * split]
+                )
+                blank = jnp.zeros((block - split, value.shape[1]), jnp.float32)
                 start = (2 * side + index % 2) * length
                 start += (step * (per_step // 2) + index // 2) * block
                 hidden_ref[pl.ds(pl.multiple_of(start, 8), block), :] = jnp.concatenate(
@@ -240,6 +244,19 @@
     def _():
         for copy in copies:
             copy.wait()
+        tails = [
+            piece_ref[start + block // 2 : start + block, :]
+            for start in range(0, piece_ref.shape[0], block)
+        ]
+        sums = jnp.dot(
+            jnp.concatenate(tails, axis=0), x_ref[...], preferred_element_type=jnp.float32
+        )
+        sums = sums * scale_ref[0:1, :]
+        for index in range(len(tails)):
+            gate_at = index * (block // 2) + units - block // 2
+            up_at = gate_at + units - split
+            value = gated_product(sums[gate_at:up_at], sums[up_at : up_at + units - split])
+            hidden_ref[index * block + split : index * block + units, :] = value
         flat_ref[...] = hidden_ref[...].T.astype(jnp.bfloat16)
 
     @pl.when(step >= first_steps)
@@ -253,18 +270,18 @@
             out_ref[member] = total[:, member * rows : (member + 1) * rows].astype(jnp.bfloat16)
 
 
-def feed_forward(sent, weights, pieces, core, units):
+def feed_forward(sent, weights, pieces, core, units, split):
     members, padded, width = sent.shape
     channels = weights.shape[1]
     rows = channels // members
     length = pieces[0].shape[0]
-    block = units + -units % 8
+    block = 3 * units - 2 * split
     blocks = 2 * length // block
-    per_step, out_step = 4, 2
+    per_step, out_step = 8, 4
     first_steps = blocks // per_step
     anywhere = pl.BlockSpec(memory_space=pl.ANY)
     return pl.pallas_call(
-        functools.partial(feed_kernel, (units, block, per_step, first_steps)),
+        functools.partial(feed_kernel, (units, split, block, per_step, first_steps)),
         grid=(first_steps + members // out_step,),
         out_shape=jax.ShapeDtypeStruct((members, width, rows), jnp.bfloat16),
         in_specs=[
@@ -312,18 +329,19 @@
     bias_part = lax.dynamic_slice_in_dim(skip_bias, offset, per_group, 0)
 
     first, pair = pack_first(gate_weight, up_weight, down_weight)
+    other_pair = swap(pair, "xh")
     own_near = lax.all_gather(first, "z", axis=0, tiled=True)
     edge = projected[:, :, block_len - 2 :].transpose(0, 2, 1).reshape(6, local_width)
     edge = lax.ppermute(
         jnp.pad(edge, ((0, 2), (0, 0))), SEQ, [(i, i + 1) for i in range(groups - 1)]
     )
     sent, query = make_gated(projected, filter_taps, short_weight, edge, groups)
+    second = pack_second(pair, other_pair)
+    sent, second = lax.optimization_barrier((sent, second))
     here = lax.all_to_all(sent, SEQ, split_axis=0, concat_axis=0, tiled=True)
 
     core = lax.axis_index("core")
-    other_pair = swap(pair, "xh")
-    here, other_pair = lax.optimization_barrier((here, other_pair))
-    gate_up = lax.all_gather(pack_second(pair, other_pair), ("z", "core"), axis=0, tiled=True)
+    gate_up = lax.all_gather(second, ("z", "core"), axis=0, tiled=True)
 
     here, own_near = lax.optimization_barrier((here, own_near))
     own_far = swap(own_near, "core")
@@ -341,7 +359,8 @@
     payload, near = lax.optimization_barrier((payload, near))
     pieces = (own_near, own_far, near, swap(near, "core"))
     sent = lax.all_to_all(payload, TP, split_axis=0, concat_axis=0, tiled=True)
-    partial_sum = feed_forward(sent, gate_up, pieces, core.reshape(1), gate_weight.shape[0])
+    units, split = gate_weight.shape[0], pair.shape[0] // 2
+    partial_sum = feed_forward(sent, gate_up, pieces, core.reshape(1), units, split)
     shares = lax.all_to_all(partial_sum, TP, split_axis=0, concat_axis=0, tiled=True)
     feed_out = jnp.sum(shares.astype(jnp.float32), axis=0).T
     return (hyena.astype(jnp.float32) + feed_out).astype(jnp.bfloat16)

time: 189 us -> 201 us (1.063)
  blocking collectives: 31.1 us -> 94.5 us
  waiting for transfers between devices: 62.5 us -> 27.2 us
  starting transfers between devices: 36.3 us -> 19.6 us
    all_to_all x0 -> x2, blocking collectives: none -> 66 us  [the longest x1 33.9 us: per_device(): here = lax.all_to_all(sent, SEQ, split_axis=0, concat_axis=0, tiled=True)]
    all_to_all x2 -> x0, waiting for transfers between devices: 30.4 us -> none  [the longest x1 22.9 us: per_device(): sent = lax.all_to_all(payload, TP, split_axis=0, concat_axis=0, tiled=True)]
    all_to_all x2 -> x0, starting transfers between devices: 17.8 us -> none  [the longest x1 12.4 us: per_device(): here = lax.all_to_all(sent, SEQ, split_axis=0, concat_axis=0, tiled=True)]
    ppermute x4, waiting for transfers between devices: 16.2 us -> 0.01 us  [swap(): return lax.ppermute(values, axis, [(0, 1), (1, 0)])]
    all_to_all x1, waiting for transfers between devices: 15.8 us -> 26.8 us  [per_device(): lax.all_to_all(mixed_term.transpose(1, 0, 2), SEQ, split_axis=0, concat_a...]
    all_to_all x1, blocking collectives: 31.1 us -> 28.4 us  [per_device(): lax.all_to_all(partial_sum, TP, split_axis=0, concat_axis=0, tiled=True)]
  transfers between devices with their start and end apart: 10 -> 8, of which waited for: 5 -> 2; matrix products, arithmetic and copies ran while one was open for 3% -> 3% of each run, Pallas kernels for 12% -> 11%
where the time goes in v4:
time: 201 us; the launch traced here: 200 us
  blocking collectives  94.5 us (47%)
  Pallas kernels  35 us (17%)
  waiting for transfers between devices  27.2 us (14%)
  starting transfers between devices  19.6 us (10%)
  between operations  13.5 us (7%)
  local copies, waits for them, and re-layouts  9.24 us (5%)
    all_to_all x1, blocking collectives, per_device(): here = lax.all_to_all(sent, SEQ, split_axis=0, concat_axis=0, tiled=True)  33.9 us
    all_to_all x1, blocking collectives, per_device(): sent = lax.all_to_all(payload, TP, split_axis=0, concat_axis=0, tiled=True)  32.2 us
    all_to_all x1, blocking collectives, per_device(): lax.all_to_all(partial_sum, TP, split_axis=0, concat_axis=0, tiled=True)  28.4 us
    all_to_all x1, waiting for transfers between devices, per_device(): lax.all_to_all(mixed_term.transpose(1, 0, 2), SEQ, split_axis=0, concat_a...  26.8 us
    pallas_call x1, Pallas kernels, long_mixing(): pl.pallas_call(conv_kernel, out_shape=jax.ShapeDtypeStruct(gated.shape, j...  13.7 us
    pallas_call x1, Pallas kernels, feed_forward(): pl.pallas_call(functools.partial(feed_kernel, (units, split, block, per_s...  10.5 us
    ppermute x4, starting transfers between devices, swap(): return lax.ppermute(values, axis, [(0, 1), (1, 0)])  10.1 us
    all_to_all x1, starting transfers between devices, per_device(): lax.all_to_all(mixed_term.transpose(1, 0, 2), SEQ, split_axis=0, concat_a...  5.02 us
  transfers between devices with their start and end apart: 8, of which 2 were waited for; matrix products, arithmetic and copies ran while one was open for 3% of the time, Pallas kernels for 11%

profile of v4, /device:TPU:1, one launch (start us, length us, event | category | flops | bytes accessed | tf_op | source)
XLA Modules:
  0.0 200.1 jit_solution(15478912486707322085)
XLA Ops:
  6.5 2.0 pack_first.1
  8.6 3.7 %collective-permute-start.1 = (bf16[34,4096]{1,0:T(8,128)(2,1)}, bf16[34,4096]{1,0:T(8,128)(2,1)S(1)}, u32[]{:S(2)}, u32[]{:S(2)}) collective-permute-start(bf16[34,4096]{1,0:T(8,128)(2,1)} %get-tuple-element.21.pair_ref), channel_id=1, source_target_pairs={{0,128},{128,0},{1,129},{129,1},{2,130},{130,2},{3,131},{131,3},{4... | collective-permute-start | bytes 835592 | tf_op jit(solution)/shard_map/ppermute | solution.py:317
  12.2 1.2 slice_bitcast_fusion
  13.6 4.4 %collective-permute-start = (bf16[8,512]{1,0:T(8,128)(2,1)S(1)}, bf16[8,512]{1,0:T(8,128)(2,1)S(1)}, u32[]{:S(2)}, u32[]{:S(2)}) collective-permute-start(bf16[8,512]{1,0:T(8,128)(2,1)S(1)} %pad.9), channel_id=1, source_target_pairs={{0,8},{8,16},{16,24},{24,32},{32,40},{40,48},{48,56},{56,64},{64,7... | collective-permute-start | bytes 24584 | tf_op jit(solution)/shard_map/ppermute | solution.py:335
  18.0 0.8 reshape.15
  18.8 0.6 pad.8.weight_ref
  19.4 0.6 copy-done.5
  20.0 3.8 %make_gated.1 = (bf16[32,2,16,256]{3,2,1,0:T(8,128)(2,1)}, f32[512,256]{1,0:T(8,128)}) custom-call(bf16[3,512,256]{2,1,0:T(8,128)(2,1)} %projected_ref.1, bf16[512,256]{1,0:T(8,128)(2,1)} %taps_ref.1, f32[16,512]{1,0:T(8,128)} %pad.8.weight_ref, bf16[8,512]{1,0:T(8,128)(2,1)} %copy-done.5), custom_call_target="tpu_custom_call" | custom-call | tf_op jit(solution)/shard_map/make_gated/pallas_call | solution.py:40
  23.8 0.7 copy-done.3
  24.5 2.0 pack_second.1
  26.6 33.9 %all_to_all.20 = bf16[32,2,16,256]{3,2,1,0:T(8,128)(2,1)S(1)} all-to-all(bf16[32,2,16,256]{3,2,1,0:T(8,128)(2,1)S(1)} %copy-done.2), channel_id=1, replica_groups=mesh['xh'=2,'z'=8,'core'=2,'y'=4,'xl'=2] {'xh','z','core'}, dimensions={0} | all-to-all | bytes 1048576 | tf_op jit(solution)/shard_map/all_to_all | solution.py:341
  60.4 0.4 all-gather.3.cloned.1.call-done.p0_ref
  60.8 3.2 %collective-permute-start.2 = (bf16[256,4096]{1,0:T(8,128)(2,1)}, bf16[256,4096]{1,0:T(8,128)(2,1)S(1)}, u32[]{:S(2)}, u32[]{:S(2)}) collective-permute-start(bf16[256,4096]{1,0:T(8,128)(2,1)} %all-gather.3.cloned.1.call-done.p0_ref), channel_id=1, source_target_pairs={{0,8},{8,0},{1,9},{9,1},{2,10},{10,2},{3,11},{11,3},{4,12},{12,4},... | collective-permute-start | bytes 6291464 | tf_op jit(solution)/shard_map/ppermute | solution.py:317
  64.0 2.7 %collective-permute-start.3 = (bf16[256,4096]{1,0:T(8,128)(2,1)}, bf16[256,4096]{1,0:T(8,128)(2,1)}, u32[]{:S(2)}, u32[]{:S(2)}) collective-permute-start(bf16[256,4096]{1,0:T(8,128)(2,1)} %all-gather.3.cloned.1.call-done.p0_ref), channel_id=1, source_target_pairs={{0,128},{128,0},{1,129},{129,1},{2,130},{130,2},{3,131},{131,3},{4... | collective-permute-start | bytes 6291464 | tf_op jit(solution)/shard_map/ppermute | solution.py:317
  66.7 0.8 dynamic_slice.6.bias_ref
  67.5 0.3 copy.24
  67.9 13.7 %long_mixing.1 = bf16[16,32,256]{2,1,0:T(8,128)(2,1)S(1)} custom-call(f32[16]{0:T(128)S(1)} %dynamic_slice.6.bias_ref, bf16[16,32,256]{2,1,0:T(8,128)(2,1)S(1)} %get-tuple-element.34.gated_ref, bf16[16,1,8192]{2,1,0:T(2,128)(2,1)S(1)} %reshape_reshape_squeeze.4.taps_ref), custom_call_target="tpu_custom_call" | custom-call | flops 8589934592 | bytes 786432 | tf_op jit(solution)/shard_map/long_mixing/pallas_call | solution.py:153
  81.7 1.0 copy.20
  82.7 5.0 %all-to-all-start.1 = ((bf16[32,16,256]{2,1,0:T(8,128)(2,1)}), bf16[32,16,256]{2,1,0:T(8,128)(2,1)S(1)}, u32[]{:S(2)}, u32[]{:S(2)}) async-start(bf16[32,16,256]{2,1,0:T(8,128)(2,1)} %copy.20), calls=%async_computation.1 | async-start | bytes 524288 | tf_op jit(solution)/shard_map/all_to_all | solution.py:352
  87.8 0.8 dynamic_slice.7
  88.5 0.8 copy.21.gain_ref
  89.4 26.8 %all-to-all-done.1 = bf16[32,16,256]{2,1,0:T(8,128)(2,1)S(1)} async-done(((bf16[32,16,256]{2,1,0:T(8,128)(2,1)}), bf16[32,16,256]{2,1,0:T(8,128)(2,1)S(1)}, u32[]{:S(2)}, u32[]{:S(2)}) %all-to-all-start.1) | async-done | bytes 262176 | tf_op jit(solution)/shard_map/all_to_all | solution.py:352
  116.1 0.7 copy-done.1
  116.8 2.9 %make_payload.1 = (bf16[512,256]{1,0:T(8,128)(2,1)}, bf16[8,528,256]{2,1,0:T(8,128)(2,1)}) custom-call(f32[512,256]{1,0:T(8,128)} %get-tuple-element.19.query_ref, bf16[512,256]{1,0:T(8,128)(2,1)} %bitcast.20, f32[512,1]{1,0:T(8,128)} %copy.21.gain_ref), custom_call_target="tpu_custom_call" | custom-call | tf_op jit(solution)/shard_map/make_payload/pallas_call | solution.py:183
  119.8 0.6 collective-permute-start.4
  120.4 32.2 %all_to_all.21.sent_ref = bf16[8,528,256]{2,1,0:T(8,128)(2,1)} all-to-all(bf16[8,528,256]{2,1,0:T(8,128)(2,1)} %get-tuple-element.29), channel_id=1, replica_groups=mesh['xh'=2,'z'=8,'core'=2,'y'=4,'xl'=2] {'y','xl'}, dimensions={0} | all-to-all | bytes 4325376 | tf_op jit(solution)/shard_map/all_to_all | solution.py:361
  152.6 10.5 %feed_forward.1 = bf16[8,256,512]{2,1,0:T(8,128)(2,1)S(1)} custom-call(s32[1]{0:T(128)} %bitcast.7.core_ref, bf16[8,528,256]{2,1,0:T(8,128)(2,1)} %all_to_all.21.sent_ref, bf16[1152,4096]{1,0:T(8,128)(2,1)} %all-gather.5.cloned.1.call-done.weight_ref, bf16[256,4096]{1,0:T(8,128)(2,1)S(1)} %copy-done, bf16[256,4096]{1,0:T(8,128)(2,1)} %copy-done.6, ...), custom_call_target="tpu_custom_call" | custom-call | flops 10000000000 | bytes 30000000 | tf_op jit(solution)/shard_map/feed_forward/pallas_call | solution.py:283
  163.1 28.4 %all_to_all.22 = bf16[8,256,512]{2,1,0:T(8,128)(2,1)S(1)} all-to-all(bf16[8,256,512]{2,1,0:T(8,128)(2,1)S(1)} %feed_forward.1), channel_id=1, replica_groups=mesh['xh'=2,'z'=8,'core'=2,'y'=4,'xl'=2] {'y','xl'}, dimensions={0} | all-to-all | bytes 4194304 | tf_op jit(solution)/shard_map/all_to_all | solution.py:364
  191.5 0.3 convert_reduce_fusion
  191.8 0.2 copy.22
  192.0 0.4 copy-done.4
  192.5 0.8 fusion
  (25 shorter events, 0.5 us)
Async XLA Ops:
  6.5 54.3 %all-gather.3.cloned.1.call-start = ((), (), s32[]{:S(2)}) async-start(), calls=%async_computation.4 | async-start | bytes 2359296 | tf_op jit(solution)/shard_map/all_gather | solution.py:333
  8.5 144.0 %all-gather.5.cloned.1.call-start = ((), (), s32[]{:S(2)}) async-start(), calls=%async_computation.5 | async-start | bytes 10027008 | tf_op jit(solution)/shard_map/all_gather | solution.py:344
  8.6 15.2 %collective-permute-start.1 = (bf16[34,4096]{1,0:T(8,128)(2,1)}, bf16[34,4096]{1,0:T(8,128)(2,1)S(1)}, u32[]{:S(2)}, u32[]{:S(2)}) collective-permute-start(bf16[34,4096]{1,0:T(8,128)(2,1)} %get-tuple-element.21.pair_ref), channel_id=1, source_target_pairs={{0,128},{128,0},{1,129},{129,1},{2,130},{130,2},{3,131},{131,3},{4... | collective-permute-start | bytes 835592 | tf_op jit(solution)/shard_map/ppermute | solution.py:317
  13.6 5.8 %collective-permute-start = (bf16[8,512]{1,0:T(8,128)(2,1)S(1)}, bf16[8,512]{1,0:T(8,128)(2,1)S(1)}, u32[]{:S(2)}, u32[]{:S(2)}) collective-permute-start(bf16[8,512]{1,0:T(8,128)(2,1)S(1)} %pad.9), channel_id=1, source_target_pairs={{0,8},{8,16},{16,24},{24,32},{32,40},{40,48},{48,56},{56,64},{64,7... | collective-permute-start | bytes 24584 | tf_op jit(solution)/shard_map/ppermute | solution.py:335
  19.4 0.6 copy-start.5
  23.8 2.8 %copy-start.2 = (bf16[32,2,16,256]{3,2,1,0:T(8,128)(2,1)S(1)}, bf16[32,2,16,256]{3,2,1,0:T(8,128)(2,1)}, u32[]{:S(2)}) copy-start(bf16[32,2,16,256]{3,2,1,0:T(8,128)(2,1)} %get-tuple-element.22) | copy-start | bytes 1572868
  23.8 0.7 copy-start.3
  60.8 20.9 %collective-permute-start.2 = (bf16[256,4096]{1,0:T(8,128)(2,1)}, bf16[256,4096]{1,0:T(8,128)(2,1)S(1)}, u32[]{:S(2)}, u32[]{:S(2)}) collective-permute-start(bf16[256,4096]{1,0:T(8,128)(2,1)} %all-gather.3.cloned.1.call-done.p0_ref), channel_id=1, source_target_pairs={{0,8},{8,0},{1,9},{9,1},{2,10},{10,2},{3,11},{11,3},{4,12},{12,4},... | collective-permute-start | bytes 6291464 | tf_op jit(solution)/shard_map/ppermute | solution.py:317
  64.0 55.7 %collective-permute-start.3 = (bf16[256,4096]{1,0:T(8,128)(2,1)}, bf16[256,4096]{1,0:T(8,128)(2,1)}, u32[]{:S(2)}, u32[]{:S(2)}) collective-permute-start(bf16[256,4096]{1,0:T(8,128)(2,1)} %all-gather.3.cloned.1.call-done.p0_ref), channel_id=1, source_target_pairs={{0,128},{128,0},{1,129},{129,1},{2,130},{130,2},{3,131},{131,3},{4... | collective-permute-start | bytes 6291464 | tf_op jit(solution)/shard_map/ppermute | solution.py:317
  81.7 38.1 %copy-start.6 = (bf16[256,4096]{1,0:T(8,128)(2,1)}, bf16[256,4096]{1,0:T(8,128)(2,1)S(1)}, u32[]{:S(2)}) copy-start(bf16[256,4096]{1,0:T(8,128)(2,1)S(1)} %collective-permute-done.2.p1_ref) | copy-start | bytes 6291460
  82.7 33.4 %all-to-all-start.1 = ((bf16[32,16,256]{2,1,0:T(8,128)(2,1)}), bf16[32,16,256]{2,1,0:T(8,128)(2,1)S(1)}, u32[]{:S(2)}, u32[]{:S(2)}) async-start(bf16[32,16,256]{2,1,0:T(8,128)(2,1)} %copy.20), calls=%async_computation.1 | async-start | bytes 524288 | tf_op jit(solution)/shard_map/all_to_all | solution.py:352
  116.1 0.7 copy-start.1
  119.8 32.8 %copy-start = (bf16[256,4096]{1,0:T(8,128)(2,1)S(1)}, bf16[256,4096]{1,0:T(8,128)(2,1)}, u32[]{:S(2)}) copy-start(bf16[256,4096]{1,0:T(8,128)(2,1)} %all-gather.3.cloned.1.call-done.p0_ref) | copy-start | bytes 6291460
  119.8 32.8 %collective-permute-start.4 = (bf16[256,4096]{1,0:T(8,128)(2,1)}, bf16[256,4096]{1,0:T(8,128)(2,1)}, u32[]{:S(2)}, u32[]{:S(2)}) collective-permute-start(bf16[256,4096]{1,0:T(8,128)(2,1)} %collective-permute-done.3.p2_ref), channel_id=1, source_target_pairs={{0,8},{8,0},{1,9},{9,1},{2,10},{10,2},{3,11},{11,3},{4,12},{12,4},... | collective-permute-start | bytes 6291464 | tf_op jit(solution)/shard_map/ppermute | solution.py:317
  191.5 1.0 copy-start.4
Sparse Core Ops, SparseCore 0:
  9.1 51.6 all-gather.2
  62.7 68.0 all-gather.4

commit v5 on v3

--- a/solution.py
+++ b/solution.py
@@ -14,9 +14,8 @@
 TP = ("y", "xl")
 
 
-def gate_kernel(projected_ref, taps_ref, weight_ref, edge_ref, sent_ref, query_ref):
-    rows, width = taps_ref.shape
-    groups = sent_ref.shape[0]
+def gate_kernel(projected_ref, weight_ref, edge_ref, gated_ref, query_ref):
+    rows, width = query_ref.shape
     weights = weight_ref[...].T
     edges = edge_ref[...].astype(jnp.float32).T
     lane = lax.broadcasted_iota(jnp.int32, (rows, width), 1)
@@ -29,22 +28,20 @@
         taps = [weights[:, 3 * index + tap : 3 * index + tap + 1] for tap in range(3)]
         shorts.append(taps[0] * value + taps[1] * once + taps[2] * twice)
     query_ref[...] = shorts[0]
-    gated = (shorts[1] * shorts[2]).astype(jnp.bfloat16)
-    sent_ref[:, 0] = gated.reshape(groups, rows // groups, width)
-    sent_ref[:, 1] = taps_ref[...].reshape(groups, rows // groups, width)
-
-
-def make_gated(projected, taps, short_weight, edge, groups):
+    gated_ref[...] = (shorts[1] * shorts[2]).astype(jnp.bfloat16)
+
+
+def make_gated(projected, short_weight, edge):
     count, rows, width = projected.shape
     weights = short_weight.transpose(0, 2, 1).reshape(9, rows)
     return pl.pallas_call(
         gate_kernel,
         out_shape=(
-            jax.ShapeDtypeStruct((groups, 2, rows // groups, width), jnp.bfloat16),
+            jax.ShapeDtypeStruct((rows, width), jnp.bfloat16),
             jax.ShapeDtypeStruct((rows, width), jnp.float32),
         ),
         name="make_gated",
-    )(projected, taps, jnp.pad(weights, ((0, 7), (0, 0))), edge)
+    )(projected, jnp.pad(weights, ((0, 7), (0, 0))), edge)
 
 
 def pack_first_kernel(gate_ref, up_ref, down_ref, first_ref, pair_ref):
@@ -85,14 +82,10 @@
     taps = jnp.broadcast_to(taps_ref[channel].astype(jnp.float32), (8, seq_len))
     base = jnp.concatenate([taps, jnp.zeros((8, LANES), jnp.float32)], axis=1)
     base = pltpu.roll(base, 0, 1, stride=1, stride_axis=0)
-    for pair in range(LANES // 16):
-        parts = []
-        for shift in (16 * pair, 16 * pair + 8):
-            moved = pltpu.roll(base, shift, 1) if shift else base
-            parts.append(moved[:, :seq_len])
-        table_ref[16 * pair : 16 * pair + 16, :] = jnp.concatenate(parts, axis=0).astype(
-            jnp.bfloat16
-        )
+    base = jnp.concatenate([base, pltpu.roll(base, 8, 1)], axis=0).astype(jnp.bfloat16)
+    for shift in range(0, LANES, 16):
+        moved = pltpu.roll(base, shift, 1) if shift else base
+        table_ref[shift : shift + 16, :] = moved[:, :seq_len]
 
 
 def apply_table(gated_ref, bias_ref, channel, table_ref, out_ref):
@@ -260,7 +253,7 @@
     length = pieces[0].shape[0]
     block = units + -units % 8
     blocks = 2 * length // block
-    per_step, out_step = 4, 2
+    per_step, out_step = 8, 4
     first_steps = blocks // per_step
     anywhere = pl.BlockSpec(memory_space=pl.ANY)
     return pl.pallas_call(
@@ -317,19 +310,29 @@
     edge = lax.ppermute(
         jnp.pad(edge, ((0, 2), (0, 0))), SEQ, [(i, i + 1) for i in range(groups - 1)]
     )
-    sent, query = make_gated(projected, filter_taps, short_weight, edge, groups)
-    here = lax.all_to_all(sent, SEQ, split_axis=0, concat_axis=0, tiled=True)
+    taps = lax.all_to_all(
+        filter_taps.reshape(groups, per_group, block_len),
+        SEQ,
+        split_axis=0,
+        concat_axis=0,
+        tiled=True,
+    )
+    gated, query = make_gated(projected, short_weight, edge)
+    other_pair = swap(pair, "xh")
+    second = pack_second(pair, other_pair)
+    gated, taps, second = lax.optimization_barrier((gated, taps, second))
+    here = lax.all_to_all(
+        gated.reshape(groups, per_group, block_len), SEQ, split_axis=0, concat_axis=0, tiled=True
+    )
 
     core = lax.axis_index("core")
-    other_pair = swap(pair, "xh")
-    here, other_pair = lax.optimization_barrier((here, other_pair))
-    gate_up = lax.all_gather(pack_second(pair, other_pair), ("z", "core"), axis=0, tiled=True)
+    gate_up = lax.all_gather(second, ("z", "core"), axis=0, tiled=True)
 
     here, own_near = lax.optimization_barrier((here, own_near))
     own_far = swap(own_near, "core")
     near = swap(own_near, "xh")
-    here = here.transpose(1, 2, 0, 3)
-    mixed_term = long_mixing(here[0], here[1].reshape(per_group, seq_len), bias_part)
+    taps = taps.transpose(1, 0, 2).reshape(per_group, seq_len)
+    mixed_term = long_mixing(here.transpose(1, 0, 2), taps, bias_part)
     mixed_term, own_far = lax.optimization_barrier((mixed_term, own_far))
     returned = lax.all_to_all(
         mixed_term.transpose(1, 0, 2), SEQ, split_axis=0, concat_axis=0, tiled=True

time: 189 us -> 188 us (level)
  blocking collectives: 31.1 us -> 51.9 us
  waiting for transfers between devices: 62.5 us -> 46 us
  starting transfers between devices: 36.3 us -> 31.5 us
    all_to_all x0 -> x1, blocking collectives: none -> 22.8 us  [per_device(): lax.all_to_all(gated.reshape(groups, per_group, block_len), SEQ, split_ax...]
    ppermute x4, waiting for transfers between devices: 16.2 us -> 5.51 us  [swap(): return lax.ppermute(values, axis, [(0, 1), (1, 0)])]
    all_to_all x1, waiting for transfers between devices: 7.54 us -> 0.01 us  [per_device(): lax.all_to_all(filter_taps.reshape(groups, per_group, block_len), SEQ, sp...]
    ppermute x4, starting transfers between devices: 8.34 us -> 4.48 us  [swap(): return lax.ppermute(values, axis, [(0, 1), (1, 0)])]
    all_to_all x1, blocking collectives: 31.1 us -> 29.1 us  [per_device(): lax.all_to_all(partial_sum, TP, split_axis=0, concat_axis=0, tiled=True)]
where the time goes in v5:
time: 188 us; the launch traced here: 187 us
  blocking collectives  51.9 us (28%)
  waiting for transfers between devices  46 us (24%)
  Pallas kernels  34.8 us (19%)
  starting transfers between devices  31.5 us (17%)
  between operations  13.5 us (7%)
  local copies, waits for them, and re-layouts  8.23 us (4%)
    all_to_all x1, blocking collectives, per_device(): lax.all_to_all(partial_sum, TP, split_axis=0, concat_axis=0, tiled=True)  29.1 us
    all_to_all x1, waiting for transfers between devices, per_device(): sent = lax.all_to_all(payload, TP, split_axis=0, concat_axis=0, tiled=True)  23.2 us
    all_to_all x1, blocking collectives, per_device(): lax.all_to_all(gated.reshape(groups, per_group, block_len), SEQ, split_ax...  22.8 us
    all_to_all x1, waiting for transfers between devices, per_device(): lax.all_to_all(mixed_term.transpose(1, 0, 2), SEQ, split_axis=0, concat_a...  17.1 us
    pallas_call x1, Pallas kernels, long_mixing(): pl.pallas_call(conv_kernel, out_shape=jax.ShapeDtypeStruct(gated.shape, j...  13.7 us
    all_to_all x1, starting transfers between devices, per_device(): lax.all_to_all(filter_taps.reshape(groups, per_group, block_len), SEQ, sp...  12.6 us
    pallas_call x1, Pallas kernels, feed_forward(): pl.pallas_call(functools.partial(feed_kernel, (units, block, per_step, fi...  10.5 us
    all_to_all x1, starting transfers between devices, per_device(): lax.all_to_all(mixed_term.transpose(1, 0, 2), SEQ, split_axis=0, concat_a...  6.19 us
  transfers between devices with their start and end apart: 10, of which 5 were waited for; matrix products, arithmetic and copies ran while one was open for 3% of the time, Pallas kernels for 12%

profile of v5, /device:TPU:1, one launch (start us, length us, event | category | flops | bytes accessed | tf_op | source)
XLA Modules:
  0.0 187.0 jit_solution(1021308884948748299)
XLA Ops:
  6.5 2.0 %pack_first.1 = (bf16[24,4096]{1,0:T(8,128)(2,1)}, bf16[44,4096]{1,0:T(8,128)(2,1)}) custom-call(bf16[22,4096]{1,0:T(8,128)(2,1)} %gate_ref.1, bf16[22,4096]{1,0:T(8,128)(2,1)} %up_ref.1, bf16[22,4096]{1,0:T(8,128)(2,1)} %down_ref.1), custom_call_target="tpu_custom_call" | custom-call | tf_op jit(solution)/shard_map/pack_first/pallas_call | solution.py:57
  8.6 12.6 %all-to-all-start = ((bf16[32,16,256]{2,1,0:T(8,128)(2,1)}), bf16[32,16,256]{2,1,0:T(8,128)(2,1)S(1)}, u32[]{:S(2)}, u32[]{:S(2)}) async-start(bf16[32,16,256]{2,1,0:T(8,128)(2,1)} %bitcast.21), calls=%async_computation | async-start | bytes 524288 | tf_op jit(solution)/shard_map/all_to_all | solution.py:313
  21.2 3.0 %collective-permute-start.1 = (bf16[44,4096]{1,0:T(8,128)(2,1)}, bf16[44,4096]{1,0:T(8,128)(2,1)S(1)}, u32[]{:S(2)}, u32[]{:S(2)}) collective-permute-start(bf16[44,4096]{1,0:T(8,128)(2,1)} %get-tuple-element.22.pair_ref), channel_id=1, source_target_pairs={{0,128},{128,0},{1,129},{129,1},{2,130},{130,2},{3,131},{131,3},{4... | collective-permute-start | bytes 1081352 | tf_op jit(solution)/shard_map/ppermute | solution.py:293
  24.2 1.2 slice_bitcast_fusion
  25.6 3.6 %collective-permute-start = (bf16[8,512]{1,0:T(8,128)(2,1)S(1)}, bf16[8,512]{1,0:T(8,128)(2,1)S(1)}, u32[]{:S(2)}, u32[]{:S(2)}) collective-permute-start(bf16[8,512]{1,0:T(8,128)(2,1)S(1)} %pad.9), channel_id=1, source_target_pairs={{0,8},{8,16},{16,24},{24,32},{32,40},{40,48},{48,56},{56,64},{64,7... | collective-permute-start | bytes 24584 | tf_op jit(solution)/shard_map/ppermute | solution.py:310
  29.2 0.6 pad.8.weight_ref
  30.0 0.6 copy-done.6
  30.6 3.6 %make_gated.1 = (bf16[512,256]{1,0:T(8,128)(2,1)}, f32[512,256]{1,0:T(8,128)}) custom-call(bf16[3,512,256]{2,1,0:T(8,128)(2,1)} %projected_ref.1, f32[16,512]{1,0:T(8,128)} %pad.8.weight_ref, bf16[8,512]{1,0:T(8,128)(2,1)} %copy-done.6), custom_call_target="tpu_custom_call" | custom-call | tf_op jit(solution)/shard_map/make_gated/pallas_call | solution.py:37
  34.2 2.0 %collective-permute-done.1.other_ref = bf16[44,4096]{1,0:T(8,128)(2,1)S(1)} collective-permute-done((bf16[44,4096]{1,0:T(8,128)(2,1)}, bf16[44,4096]{1,0:T(8,128)(2,1)S(1)}, u32[]{:S(2)}, u32[]{:S(2)}) %collective-permute-start.1) | collective-permute-done | bytes 360480 | tf_op jit(solution)/shard_map/ppermute | solution.py:293
  36.2 0.7 copy-done.2
  37.0 2.1 %pack_second.1 = bf16[88,4096]{1,0:T(8,128)(2,1)} custom-call(bf16[44,4096]{1,0:T(8,128)(2,1)} %get-tuple-element.22.pair_ref, bf16[44,4096]{1,0:T(8,128)(2,1)} %copy-done.2), custom_call_target="tpu_custom_call" | custom-call | tf_op jit(solution)/shard_map/pack_second/pallas_call | solution.py:73
  39.1 22.8 %all_to_all.25 = bf16[32,16,256]{2,1,0:T(8,128)(2,1)S(1)} all-to-all(bf16[32,16,256]{2,1,0:T(8,128)(2,1)S(1)} %bitcast.22), channel_id=1, replica_groups=mesh['xh'=2,'z'=8,'core'=2,'y'=4,'xl'=2] {'xh','z','core'}, dimensions={0} | all-to-all | bytes 524288 | tf_op jit(solution)/shard_map/all_to_all | solution.py:324
  61.9 0.6 collective-permute-start.2
  62.6 0.3 collective-permute-start.3
  62.8 0.8 dynamic_slice.6.bias_ref
  63.9 13.7 %long_mixing.1 = bf16[16,32,256]{2,1,0:T(8,128)(2,1)S(1)} custom-call(f32[16]{0:T(128)S(1)} %dynamic_slice.6.bias_ref, bf16[16,32,256]{2,1,0:T(8,128)(2,1)S(1)} %bitcast.18, bf16[16,1,8192]{2,1,0:T(2,128)(2,1)S(1)} %reshape_reshape.4.taps_ref), custom_call_target="tpu_custom_call" | custom-call | flops 8589934592 | bytes 786432 | tf_op jit(solution)/shard_map/long_mixing/pallas_call | solution.py:147
  77.7 0.9 copy.22
  78.5 6.2 %all-to-all-start.2 = ((bf16[32,16,256]{2,1,0:T(8,128)(2,1)}), bf16[32,16,256]{2,1,0:T(8,128)(2,1)S(1)}, u32[]{:S(2)}, u32[]{:S(2)}) async-start(bf16[32,16,256]{2,1,0:T(8,128)(2,1)} %copy.22), calls=%async_computation.2 | async-start | bytes 524288 | tf_op jit(solution)/shard_map/all_to_all | solution.py:337
  84.7 0.8 dynamic_slice.7
  85.5 0.9 copy.23.gain_ref
  86.4 17.1 %all-to-all-done.2 = bf16[32,16,256]{2,1,0:T(8,128)(2,1)S(1)} async-done(((bf16[32,16,256]{2,1,0:T(8,128)(2,1)}), bf16[32,16,256]{2,1,0:T(8,128)(2,1)S(1)}, u32[]{:S(2)}, u32[]{:S(2)}) %all-to-all-start.2) | async-done | bytes 262176 | tf_op jit(solution)/shard_map/all_to_all | solution.py:337
  103.4 0.7 copy-done.1
  104.1 2.9 %make_payload.1 = (bf16[512,256]{1,0:T(8,128)(2,1)}, bf16[8,528,256]{2,1,0:T(8,128)(2,1)}) custom-call(f32[512,256]{1,0:T(8,128)} %get-tuple-element.20.query_ref, bf16[512,256]{1,0:T(8,128)(2,1)} %bitcast.20, f32[512,1]{1,0:T(8,128)} %copy.23.gain_ref), custom_call_target="tpu_custom_call" | custom-call | tf_op jit(solution)/shard_map/make_payload/pallas_call | solution.py:177
  107.0 4.6 %all-to-all-start.3 = ((bf16[8,528,256]{2,1,0:T(8,128)(2,1)}), bf16[8,528,256]{2,1,0:T(8,128)(2,1)}, u32[]{:S(2)}, u32[]{:S(2)}) async-start(bf16[8,528,256]{2,1,0:T(8,128)(2,1)} %get-tuple-element.31), calls=%async_computation.3 | async-start | bytes 4325376 | tf_op jit(solution)/shard_map/all_to_all | solution.py:346
  111.6 0.6 collective-permute-start.4
  112.1 3.5 %collective-permute-done.4.p3_ref = bf16[192,4096]{1,0:T(8,128)(2,1)} collective-permute-done((bf16[192,4096]{1,0:T(8,128)(2,1)}, bf16[192,4096]{1,0:T(8,128)(2,1)}, u32[]{:S(2)}, u32[]{:S(2)}) %collective-permute-start.4) | collective-permute-done | bytes 1572896 | tf_op jit(solution)/shard_map/ppermute | solution.py:293
  115.7 23.2 %all-to-all-done.3.sent_ref = bf16[8,528,256]{2,1,0:T(8,128)(2,1)} async-done(((bf16[8,528,256]{2,1,0:T(8,128)(2,1)}), bf16[8,528,256]{2,1,0:T(8,128)(2,1)}, u32[]{:S(2)}, u32[]{:S(2)}) %all-to-all-start.3) | async-done | bytes 2162720 | tf_op jit(solution)/shard_map/all_to_all | solution.py:346
  138.9 10.5 %feed_forward.1 = bf16[8,256,512]{2,1,0:T(8,128)(2,1)} custom-call(s32[1]{0:T(128)} %bitcast.9.core_ref, bf16[8,528,256]{2,1,0:T(8,128)(2,1)} %all-to-all-done.3.sent_ref, bf16[1408,4096]{1,0:T(8,128)(2,1)} %all-gather.5.cloned.1.call-done.weight_ref, bf16[192,4096]{1,0:T(8,128)(2,1)S(1)} %copy-done, bf16[192,4096]{1,0:T(8,128)(2,1)S(1)} %collective-permute-done.2.p1_ref, ...), custom_call_target="tpu_custom_call" | custom-call | flops 10000000000 | bytes 30000000 | tf_op jit(solution)/shard_map/feed_forward/pallas_call | solution.py:259
  149.4 29.1 %all_to_all.26 = bf16[8,256,512]{2,1,0:T(8,128)(2,1)S(1)} all-to-all(bf16[8,256,512]{2,1,0:T(8,128)(2,1)} %feed_forward.1), channel_id=1, replica_groups=mesh['xh'=2,'z'=8,'core'=2,'y'=4,'xl'=2] {'y','xl'}, dimensions={0} | all-to-all | bytes 4194304 | tf_op jit(solution)/shard_map/all_to_all | solution.py:348
  178.4 0.3 convert_reduce_fusion
  178.9 0.4 copy-done.4
  179.4 0.8 fusion
  (28 shorter events, 1.0 us)
Async XLA Ops:
  6.5 22.7 %copy-start.5 = (f32[3,512,3]{1,2,0:T(4,128)S(1)}, f32[3,512,3]{1,2,0:T(4,128)}, u32[]{:S(2)}) copy-start(f32[3,512,3]{1,2,0:T(4,128)} %param.10) | copy-start | bytes 55300
  6.5 55.4 %all-gather.3.cloned.1.call-start = ((), (), s32[]{:S(2)}) async-start(), calls=%async_computation.5 | async-start | bytes 1769472 | tf_op jit(solution)/shard_map/all_gather | solution.py:308
  8.6 30.5 %all-to-all-start = ((bf16[32,16,256]{2,1,0:T(8,128)(2,1)}), bf16[32,16,256]{2,1,0:T(8,128)(2,1)S(1)}, u32[]{:S(2)}, u32[]{:S(2)}) async-start(bf16[32,16,256]{2,1,0:T(8,128)(2,1)} %bitcast.21), calls=%async_computation | async-start | bytes 524288 | tf_op jit(solution)/shard_map/all_to_all | solution.py:313
  21.2 117.7 %all-gather.5.cloned.1.call-start = ((), (), s32[]{:S(2)}) async-start(), calls=%async_computation.6 | async-start | bytes 12255232 | tf_op jit(solution)/shard_map/all_gather | solution.py:329
  21.2 15.0 %collective-permute-start.1 = (bf16[44,4096]{1,0:T(8,128)(2,1)}, bf16[44,4096]{1,0:T(8,128)(2,1)S(1)}, u32[]{:S(2)}, u32[]{:S(2)}) collective-permute-start(bf16[44,4096]{1,0:T(8,128)(2,1)} %get-tuple-element.22.pair_ref), channel_id=1, source_target_pairs={{0,128},{128,0},{1,129},{129,1},{2,130},{130,2},{3,131},{131,3},{4... | collective-permute-start | bytes 1081352 | tf_op jit(solution)/shard_map/ppermute | solution.py:293
  25.6 4.4 %collective-permute-start = (bf16[8,512]{1,0:T(8,128)(2,1)S(1)}, bf16[8,512]{1,0:T(8,128)(2,1)S(1)}, u32[]{:S(2)}, u32[]{:S(2)}) collective-permute-start(bf16[8,512]{1,0:T(8,128)(2,1)S(1)} %pad.9), channel_id=1, source_target_pairs={{0,8},{8,16},{16,24},{24,32},{32,40},{40,48},{48,56},{56,64},{64,7... | collective-permute-start | bytes 24584 | tf_op jit(solution)/shard_map/ppermute | solution.py:310
  30.0 0.6 copy-start.6
  34.2 4.9 %copy-start.3 = (bf16[512,256]{1,0:T(8,128)(2,1)S(1)}, bf16[512,256]{1,0:T(8,128)(2,1)}, u32[]{:S(2)}) copy-start(bf16[512,256]{1,0:T(8,128)(2,1)} %get-tuple-element.23) | copy-start | bytes 786436
  36.2 0.7 copy-start.2
  61.9 15.7 %collective-permute-start.2 = (bf16[192,4096]{1,0:T(8,128)(2,1)}, bf16[192,4096]{1,0:T(8,128)(2,1)S(1)}, u32[]{:S(2)}, u32[]{:S(2)}) collective-permute-start(bf16[192,4096]{1,0:T(8,128)(2,1)} %all-gather.3.cloned.1.call-done.p0_ref), channel_id=1, source_target_pairs={{0,8},{8,0},{1,9},{9,1},{2,10},{10,2},{3,11},{11,3},{4,12},{12,4},... | collective-permute-start | bytes 4718600 | tf_op jit(solution)/shard_map/ppermute | solution.py:293
  62.6 44.4 %collective-permute-start.3 = (bf16[192,4096]{1,0:T(8,128)(2,1)}, bf16[192,4096]{1,0:T(8,128)(2,1)}, u32[]{:S(2)}, u32[]{:S(2)}) collective-permute-start(bf16[192,4096]{1,0:T(8,128)(2,1)} %all-gather.3.cloned.1.call-done.p0_ref), channel_id=1, source_target_pairs={{0,128},{128,0},{1,129},{129,1},{2,130},{130,2},{3,131},{131,3},{4... | collective-permute-start | bytes 4718600 | tf_op jit(solution)/shard_map/ppermute | solution.py:293
  78.5 24.9 %all-to-all-start.2 = ((bf16[32,16,256]{2,1,0:T(8,128)(2,1)}), bf16[32,16,256]{2,1,0:T(8,128)(2,1)S(1)}, u32[]{:S(2)}, u32[]{:S(2)}) async-start(bf16[32,16,256]{2,1,0:T(8,128)(2,1)} %copy.22), calls=%async_computation.2 | async-start | bytes 524288 | tf_op jit(solution)/shard_map/all_to_all | solution.py:337
  103.4 0.7 copy-start.1
  107.0 31.9 %copy-start = (bf16[192,4096]{1,0:T(8,128)(2,1)S(1)}, bf16[192,4096]{1,0:T(8,128)(2,1)}, u32[]{:S(2)}) copy-start(bf16[192,4096]{1,0:T(8,128)(2,1)} %all-gather.3.cloned.1.call-done.p0_ref) | copy-start | bytes 4718596
  107.0 31.9 %all-to-all-start.3 = ((bf16[8,528,256]{2,1,0:T(8,128)(2,1)}), bf16[8,528,256]{2,1,0:T(8,128)(2,1)}, u32[]{:S(2)}, u32[]{:S(2)}) async-start(bf16[8,528,256]{2,1,0:T(8,128)(2,1)} %get-tuple-element.31), calls=%async_computation.3 | async-start | bytes 4325376 | tf_op jit(solution)/shard_map/all_to_all | solution.py:346
  111.6 4.1 %collective-permute-start.4 = (bf16[192,4096]{1,0:T(8,128)(2,1)}, bf16[192,4096]{1,0:T(8,128)(2,1)}, u32[]{:S(2)}, u32[]{:S(2)}) collective-permute-start(bf16[192,4096]{1,0:T(8,128)(2,1)} %collective-permute-done.3.p2_ref), channel_id=1, source_target_pairs={{0,8},{8,0},{1,9},{9,1},{2,10},{10,2},{3,11},{11,3},{4,12},{12,4},... | collective-permute-start | bytes 4718600 | tf_op jit(solution)/shard_map/ppermute | solution.py:293
  178.4 1.0 copy-start.4
Sparse Core Ops, SparseCore 0:
  9.1 43.8 all-gather.2
  54.8 81.4 all-gather.4

commit v6 on v5

--- a/solution.py
+++ b/solution.py
@@ -319,13 +319,14 @@
     )
     gated, query = make_gated(projected, short_weight, edge)
     other_pair = swap(pair, "xh")
-    second = pack_second(pair, other_pair)
-    gated, taps, second = lax.optimization_barrier((gated, taps, second))
+    gated, taps = lax.optimization_barrier((gated, taps))
     here = lax.all_to_all(
         gated.reshape(groups, per_group, block_len), SEQ, split_axis=0, concat_axis=0, tiled=True
     )
 
     core = lax.axis_index("core")
+    here, other_pair = lax.optimization_barrier((here, other_pair))
+    second = pack_second(pair, other_pair)
     gate_up = lax.all_gather(second, ("z", "core"), axis=0, tiled=True)
 
     here, own_near = lax.optimization_barrier((here, own_near))

time: 188 us -> 190 us (1.011)
  blocking collectives: 51.9 us -> 31.3 us
  starting transfers between devices: 31.5 us -> 43.9 us
  waiting for transfers between devices: 46 us -> 57.1 us
    all_to_all x1 -> x0, blocking collectives: 22.8 us -> none  [per_device(): lax.all_to_all(gated.reshape(groups, per_group, block_len), SEQ, split_ax...]
    ppermute x4, waiting for transfers between devices: 5.51 us -> 15.3 us  [swap(): return lax.ppermute(values, axis, [(0, 1), (1, 0)])]
    all_to_all x0 -> x1, starting transfers between devices: none -> 8.31 us  [per_device(): lax.all_to_all(gated.reshape(groups, per_group, block_len), SEQ, split_ax...]
    all_to_all x1, waiting for transfers between devices: 0.01 us -> 4.24 us  [per_device(): lax.all_to_all(filter_taps.reshape(groups, per_group, block_len), SEQ, sp...]
    ppermute x4, starting transfers between devices: 4.48 us -> 7.3 us  [swap(): return lax.ppermute(values, axis, [(0, 1), (1, 0)])]
    all_to_all x1, waiting for transfers between devices: 17.1 us -> 14.5 us  [per_device(): lax.all_to_all(mixed_term.transpose(1, 0, 2), SEQ, split_axis=0, concat_a...]
    all_to_all x1, waiting for transfers between devices: 23.2 us -> 20.9 us  [per_device(): sent = lax.all_to_all(payload, TP, split_axis=0, concat_axis=0, tiled=True)]
    all_to_all x1, blocking collectives: 29.1 us -> 31.3 us  [per_device(): lax.all_to_all(partial_sum, TP, split_axis=0, concat_axis=0, tiled=True)]
  transfers between devices with their start and end apart: 10 -> 11, of which waited for: 5 -> 8; matrix products, arithmetic and copies ran while one was open for 3% -> 3% of each run, Pallas kernels for 12% -> 12%
where the time goes in v6:
time: 190 us; the launch traced here: 189 us
  waiting for transfers between devices  57.1 us (30%)
  starting transfers between devices  43.9 us (23%)
  Pallas kernels  34.7 us (18%)
  blocking collectives  31.3 us (16%)
  between operations  13.6 us (7%)
  local copies, waits for them, and re-layouts  7.48 us (4%)
    all_to_all x1, blocking collectives, per_device(): lax.all_to_all(partial_sum, TP, split_axis=0, concat_axis=0, tiled=True)  31.3 us
    all_to_all x1, waiting for transfers between devices, per_device(): sent = lax.all_to_all(payload, TP, split_axis=0, concat_axis=0, tiled=True)  20.9 us
    ppermute x4, waiting for transfers between devices, swap(): return lax.ppermute(values, axis, [(0, 1), (1, 0)])  15.3 us
    all_to_all x1, waiting for transfers between devices, per_device(): lax.all_to_all(mixed_term.transpose(1, 0, 2), SEQ, split_axis=0, concat_a...  14.5 us
    pallas_call x1, Pallas kernels, long_mixing(): pl.pallas_call(conv_kernel, out_shape=jax.ShapeDtypeStruct(gated.shape, j...  13.7 us
    all_to_all x1, starting transfers between devices, per_device(): lax.all_to_all(filter_taps.reshape(groups, per_group, block_len), SEQ, sp...  12.7 us
    pallas_call x1, Pallas kernels, feed_forward(): pl.pallas_call(functools.partial(feed_kernel, (units, block, per_step, fi...  10.5 us
    all_to_all x1, starting transfers between devices, per_device(): lax.all_to_all(gated.reshape(groups, per_group, block_len), SEQ, split_ax...  8.31 us
  transfers between devices with their start and end apart: 11, of which 8 were waited for; matrix products, arithmetic and copies ran while one was open for 3% of the time, Pallas kernels for 12%

profile of v6, /device:TPU:1, one launch (start us, length us, event | category | flops | bytes accessed | tf_op | source)
XLA Modules:
  0.0 189.1 jit_solution(13396352731948419339)
XLA Ops:
  6.5 2.0 %pack_first.1 = (bf16[24,4096]{1,0:T(8,128)(2,1)}, bf16[44,4096]{1,0:T(8,128)(2,1)}) custom-call(bf16[22,4096]{1,0:T(8,128)(2,1)} %gate_ref.1, bf16[22,4096]{1,0:T(8,128)(2,1)} %up_ref.1, bf16[22,4096]{1,0:T(8,128)(2,1)} %down_ref.1), custom_call_target="tpu_custom_call" | custom-call | tf_op jit(solution)/shard_map/pack_first/pallas_call | solution.py:57
  8.5 12.7 %all-to-all-start = ((bf16[32,16,256]{2,1,0:T(8,128)(2,1)}), bf16[32,16,256]{2,1,0:T(8,128)(2,1)S(1)}, u32[]{:S(2)}, u32[]{:S(2)}) async-start(bf16[32,16,256]{2,1,0:T(8,128)(2,1)} %bitcast.21), calls=%async_computation | async-start | bytes 524288 | tf_op jit(solution)/shard_map/all_to_all | solution.py:313
  21.3 1.2 slice_bitcast_fusion
  22.7 3.5 %collective-permute-start = (bf16[8,512]{1,0:T(8,128)(2,1)S(1)}, bf16[8,512]{1,0:T(8,128)(2,1)S(1)}, u32[]{:S(2)}, u32[]{:S(2)}) collective-permute-start(bf16[8,512]{1,0:T(8,128)(2,1)S(1)} %pad.9), channel_id=1, source_target_pairs={{0,8},{8,16},{16,24},{24,32},{32,40},{40,48},{48,56},{56,64},{64,7... | collective-permute-start | bytes 24584 | tf_op jit(solution)/shard_map/ppermute | solution.py:310
  26.2 0.6 pad.8.weight_ref
  27.0 0.6 copy-done.6
  27.6 3.6 %make_gated.1 = (bf16[512,256]{1,0:T(8,128)(2,1)}, f32[512,256]{1,0:T(8,128)}) custom-call(bf16[3,512,256]{2,1,0:T(8,128)(2,1)} %projected_ref.1, f32[16,512]{1,0:T(8,128)} %pad.8.weight_ref, bf16[8,512]{1,0:T(8,128)(2,1)} %copy-done.6), custom_call_target="tpu_custom_call" | custom-call | tf_op jit(solution)/shard_map/make_gated/pallas_call | solution.py:37
  31.2 4.2 %all-to-all-done = bf16[32,16,256]{2,1,0:T(8,128)(2,1)S(1)} async-done(((bf16[32,16,256]{2,1,0:T(8,128)(2,1)}), bf16[32,16,256]{2,1,0:T(8,128)(2,1)S(1)}, u32[]{:S(2)}, u32[]{:S(2)}) %all-to-all-start) | async-done | bytes 262176 | tf_op jit(solution)/shard_map/all_to_all | solution.py:313
  35.5 8.3 %all-to-all-start.1 = ((bf16[32,16,256]{2,1,0:T(8,128)(2,1)}), bf16[32,16,256]{2,1,0:T(8,128)(2,1)S(1)}, u32[]{:S(2)}, u32[]{:S(2)}) async-start(bf16[32,16,256]{2,1,0:T(8,128)(2,1)} %bitcast.22), calls=%async_computation.1 | async-start | bytes 524288 | tf_op jit(solution)/shard_map/all_to_all | solution.py:323
  43.8 3.0 %collective-permute-start.1 = (bf16[44,4096]{1,0:T(8,128)(2,1)S(1)}, bf16[44,4096]{1,0:T(8,128)(2,1)S(1)}, u32[]{:S(2)}, u32[]{:S(2)}) collective-permute-start(bf16[44,4096]{1,0:T(8,128)(2,1)S(1)} %copy-done.2), channel_id=1, source_target_pairs={{0,128},{128,0},{1,129},{129,1},{2,130},{130,2},{3,131},{131,3},{4... | collective-permute-start | bytes 1081352 | tf_op jit(solution)/shard_map/ppermute | solution.py:293
  46.8 11.8 %collective-permute-done.1.other_ref = bf16[44,4096]{1,0:T(8,128)(2,1)S(1)} collective-permute-done((bf16[44,4096]{1,0:T(8,128)(2,1)S(1)}, bf16[44,4096]{1,0:T(8,128)(2,1)S(1)}, u32[]{:S(2)}, u32[]{:S(2)}) %collective-permute-start.1) | collective-permute-done | bytes 360480 | tf_op jit(solution)/shard_map/ppermute | solution.py:293
  58.6 1.6 all-to-all-done.1
  60.2 2.1 %pack_second.1 = bf16[88,4096]{1,0:T(8,128)(2,1)} custom-call(bf16[44,4096]{1,0:T(8,128)(2,1)} %get-tuple-element.24.pair_ref, bf16[44,4096]{1,0:T(8,128)(2,1)} %copy-done.3), custom_call_target="tpu_custom_call" | custom-call | tf_op jit(solution)/shard_map/pack_second/pallas_call | solution.py:73
  62.3 0.5 collective-permute-start.2
  62.8 2.2 %collective-permute-start.3 = (bf16[192,4096]{1,0:T(8,128)(2,1)}, bf16[192,4096]{1,0:T(8,128)(2,1)}, u32[]{:S(2)}, u32[]{:S(2)}) collective-permute-start(bf16[192,4096]{1,0:T(8,128)(2,1)} %all-gather.3.cloned.1.call-done.p0_ref), channel_id=1, source_target_pairs={{0,128},{128,0},{1,129},{129,1},{2,130},{130,2},{3,131},{131,3},{4... | collective-permute-start | bytes 4718600 | tf_op jit(solution)/shard_map/ppermute | solution.py:293
  65.0 0.8 dynamic_slice.6.bias_ref
  66.1 13.7 %long_mixing.1 = bf16[16,32,256]{2,1,0:T(8,128)(2,1)S(1)} custom-call(f32[16]{0:T(128)S(1)} %dynamic_slice.6.bias_ref, bf16[16,32,256]{2,1,0:T(8,128)(2,1)S(1)} %bitcast.18, bf16[16,1,8192]{2,1,0:T(2,128)(2,1)S(1)} %reshape_reshape.4.taps_ref), custom_call_target="tpu_custom_call" | custom-call | flops 8589934592 | bytes 786432 | tf_op jit(solution)/shard_map/long_mixing/pallas_call | solution.py:147
  79.9 0.9 copy.22
  80.7 7.5 %all-to-all-start.2 = ((bf16[32,16,256]{2,1,0:T(8,128)(2,1)}), bf16[32,16,256]{2,1,0:T(8,128)(2,1)S(1)}, u32[]{:S(2)}, u32[]{:S(2)}) async-start(bf16[32,16,256]{2,1,0:T(8,128)(2,1)} %copy.22), calls=%async_computation.2 | async-start | bytes 524288 | tf_op jit(solution)/shard_map/all_to_all | solution.py:338
  88.2 0.8 dynamic_slice.7
  89.0 0.9 copy.23.gain_ref
  89.9 14.5 %all-to-all-done.2 = bf16[32,16,256]{2,1,0:T(8,128)(2,1)S(1)} async-done(((bf16[32,16,256]{2,1,0:T(8,128)(2,1)}), bf16[32,16,256]{2,1,0:T(8,128)(2,1)S(1)}, u32[]{:S(2)}, u32[]{:S(2)}) %all-to-all-start.2) | async-done | bytes 262176 | tf_op jit(solution)/shard_map/all_to_all | solution.py:338
  104.4 0.7 copy-done.1
  105.1 2.8 %make_payload.1 = (bf16[512,256]{1,0:T(8,128)(2,1)}, bf16[8,528,256]{2,1,0:T(8,128)(2,1)}) custom-call(f32[512,256]{1,0:T(8,128)} %get-tuple-element.21.query_ref, bf16[512,256]{1,0:T(8,128)(2,1)} %bitcast.20, f32[512,1]{1,0:T(8,128)} %copy.23.gain_ref), custom_call_target="tpu_custom_call" | custom-call | tf_op jit(solution)/shard_map/make_payload/pallas_call | solution.py:177
  107.9 4.5 %all-to-all-start.3 = ((bf16[8,528,256]{2,1,0:T(8,128)(2,1)}), bf16[8,528,256]{2,1,0:T(8,128)(2,1)}, u32[]{:S(2)}, u32[]{:S(2)}) async-start(bf16[8,528,256]{2,1,0:T(8,128)(2,1)} %get-tuple-element.33), calls=%async_computation.3 | async-start | bytes 4325376 | tf_op jit(solution)/shard_map/all_to_all | solution.py:347
  112.4 1.6 collective-permute-start.4
  114.0 3.5 %collective-permute-done.4.p3_ref = bf16[192,4096]{1,0:T(8,128)(2,1)} collective-permute-done((bf16[192,4096]{1,0:T(8,128)(2,1)}, bf16[192,4096]{1,0:T(8,128)(2,1)}, u32[]{:S(2)}, u32[]{:S(2)}) %collective-permute-start.4) | collective-permute-done | bytes 1572896 | tf_op jit(solution)/shard_map/ppermute | solution.py:293
  117.5 20.9 %all-to-all-done.3.sent_ref = bf16[8,528,256]{2,1,0:T(8,128)(2,1)} async-done(((bf16[8,528,256]{2,1,0:T(8,128)(2,1)}), bf16[8,528,256]{2,1,0:T(8,128)(2,1)}, u32[]{:S(2)}, u32[]{:S(2)}) %all-to-all-start.3) | async-done | bytes 2162720 | tf_op jit(solution)/shard_map/all_to_all | solution.py:347
  138.8 10.5 %feed_forward.1 = bf16[8,256,512]{2,1,0:T(8,128)(2,1)} custom-call(s32[1]{0:T(128)} %bitcast.9.core_ref, bf16[8,528,256]{2,1,0:T(8,128)(2,1)} %all-to-all-done.3.sent_ref, bf16[1408,4096]{1,0:T(8,128)(2,1)} %all-gather.5.cloned.1.call-done.weight_ref, bf16[192,4096]{1,0:T(8,128)(2,1)S(1)} %copy-done, bf16[192,4096]{1,0:T(8,128)(2,1)S(1)} %collective-permute-done.2.p1_ref, ...), custom_call_target="tpu_custom_call" | custom-call | flops 10000000000 | bytes 30000000 | tf_op jit(solution)/shard_map/feed_forward/pallas_call | solution.py:259
  149.3 31.3 %all_to_all.25 = bf16[8,256,512]{2,1,0:T(8,128)(2,1)S(1)} all-to-all(bf16[8,256,512]{2,1,0:T(8,128)(2,1)} %feed_forward.1), channel_id=1, replica_groups=mesh['xh'=2,'z'=8,'core'=2,'y'=4,'xl'=2] {'y','xl'}, dimensions={0} | all-to-all | bytes 4194304 | tf_op jit(solution)/shard_map/all_to_all | solution.py:349
  181.1 0.4 copy-done.4
  181.5 0.8 fusion
  (29 shorter events, 1.6 us)
Async XLA Ops:
  6.5 19.7 %copy-start.5 = (f32[3,512,3]{1,2,0:T(4,128)S(1)}, f32[3,512,3]{1,2,0:T(4,128)}, u32[]{:S(2)}) copy-start(f32[3,512,3]{1,2,0:T(4,128)} %param.10) | copy-start | bytes 55300
  6.5 55.8 %all-gather.3.cloned.1.call-start = ((), (), s32[]{:S(2)}) async-start(), calls=%async_computation.5 | async-start | bytes 1769472 | tf_op jit(solution)/shard_map/all_gather | solution.py:308
  8.5 35.3 %copy-start.2 = (bf16[44,4096]{1,0:T(8,128)(2,1)S(1)}, bf16[44,4096]{1,0:T(8,128)(2,1)}, u32[]{:S(2)}) copy-start(bf16[44,4096]{1,0:T(8,128)(2,1)} %get-tuple-element.24.pair_ref) | copy-start | bytes 1081348
  8.5 26.9 %all-to-all-start = ((bf16[32,16,256]{2,1,0:T(8,128)(2,1)}), bf16[32,16,256]{2,1,0:T(8,128)(2,1)S(1)}, u32[]{:S(2)}, u32[]{:S(2)}) async-start(bf16[32,16,256]{2,1,0:T(8,128)(2,1)} %bitcast.21), calls=%async_computation | async-start | bytes 524288 | tf_op jit(solution)/shard_map/all_to_all | solution.py:313
  22.7 4.3 %collective-permute-start = (bf16[8,512]{1,0:T(8,128)(2,1)S(1)}, bf16[8,512]{1,0:T(8,128)(2,1)S(1)}, u32[]{:S(2)}, u32[]{:S(2)}) collective-permute-start(bf16[8,512]{1,0:T(8,128)(2,1)S(1)} %pad.9), channel_id=1, source_target_pairs={{0,8},{8,16},{16,24},{24,32},{32,40},{40,48},{48,56},{56,64},{64,7... | collective-permute-start | bytes 24584 | tf_op jit(solution)/shard_map/ppermute | solution.py:310
  27.0 0.6 copy-start.6
  35.5 24.7 %all-to-all-start.1 = ((bf16[32,16,256]{2,1,0:T(8,128)(2,1)}), bf16[32,16,256]{2,1,0:T(8,128)(2,1)S(1)}, u32[]{:S(2)}, u32[]{:S(2)}) async-start(bf16[32,16,256]{2,1,0:T(8,128)(2,1)} %bitcast.22), calls=%async_computation.1 | async-start | bytes 524288 | tf_op jit(solution)/shard_map/all_to_all | solution.py:323
  43.8 95.0 %all-gather.5.cloned.1.call-start = ((), (), s32[]{:S(2)}) async-start(), calls=%async_computation.6 | async-start | bytes 12255232 | tf_op jit(solution)/shard_map/all_gather | solution.py:330
  43.8 14.8 %collective-permute-start.1 = (bf16[44,4096]{1,0:T(8,128)(2,1)S(1)}, bf16[44,4096]{1,0:T(8,128)(2,1)S(1)}, u32[]{:S(2)}, u32[]{:S(2)}) collective-permute-start(bf16[44,4096]{1,0:T(8,128)(2,1)S(1)} %copy-done.2), channel_id=1, source_target_pairs={{0,128},{128,0},{1,129},{129,1},{2,130},{130,2},{3,131},{131,3},{4... | collective-permute-start | bytes 1081352 | tf_op jit(solution)/shard_map/ppermute | solution.py:293
  58.6 1.6 copy-start.3
  62.3 17.5 %collective-permute-start.2 = (bf16[192,4096]{1,0:T(8,128)(2,1)}, bf16[192,4096]{1,0:T(8,128)(2,1)S(1)}, u32[]{:S(2)}, u32[]{:S(2)}) collective-permute-start(bf16[192,4096]{1,0:T(8,128)(2,1)} %all-gather.3.cloned.1.call-done.p0_ref), channel_id=1, source_target_pairs={{0,8},{8,0},{1,9},{9,1},{2,10},{10,2},{3,11},{11,3},{4,12},{12,4},... | collective-permute-start | bytes 4718600 | tf_op jit(solution)/shard_map/ppermute | solution.py:293
  62.8 45.1 %collective-permute-start.3 = (bf16[192,4096]{1,0:T(8,128)(2,1)}, bf16[192,4096]{1,0:T(8,128)(2,1)}, u32[]{:S(2)}, u32[]{:S(2)}) collective-permute-start(bf16[192,4096]{1,0:T(8,128)(2,1)} %all-gather.3.cloned.1.call-done.p0_ref), channel_id=1, source_target_pairs={{0,128},{128,0},{1,129},{129,1},{2,130},{130,2},{3,131},{131,3},{4... | collective-permute-start | bytes 4718600 | tf_op jit(solution)/shard_map/ppermute | solution.py:293
  80.7 23.6 %all-to-all-start.2 = ((bf16[32,16,256]{2,1,0:T(8,128)(2,1)}), bf16[32,16,256]{2,1,0:T(8,128)(2,1)S(1)}, u32[]{:S(2)}, u32[]{:S(2)}) async-start(bf16[32,16,256]{2,1,0:T(8,128)(2,1)} %copy.22), calls=%async_computation.2 | async-start | bytes 524288 | tf_op jit(solution)/shard_map/all_to_all | solution.py:338
  104.3 0.7 copy-start.1
  107.9 30.9 %copy-start = (bf16[192,4096]{1,0:T(8,128)(2,1)S(1)}, bf16[192,4096]{1,0:T(8,128)(2,1)}, u32[]{:S(2)}) copy-start(bf16[192,4096]{1,0:T(8,128)(2,1)} %all-gather.3.cloned.1.call-done.p0_ref) | copy-start | bytes 4718596
  107.9 30.6 %all-to-all-start.3 = ((bf16[8,528,256]{2,1,0:T(8,128)(2,1)}), bf16[8,528,256]{2,1,0:T(8,128)(2,1)}, u32[]{:S(2)}, u32[]{:S(2)}) async-start(bf16[8,528,256]{2,1,0:T(8,128)(2,1)} %get-tuple-element.33), calls=%async_computation.3 | async-start | bytes 4325376 | tf_op jit(solution)/shard_map/all_to_all | solution.py:347
  112.4 5.1 %collective-permute-start.4 = (bf16[192,4096]{1,0:T(8,128)(2,1)}, bf16[192,4096]{1,0:T(8,128)(2,1)}, u32[]{:S(2)}, u32[]{:S(2)}) collective-permute-start(bf16[192,4096]{1,0:T(8,128)(2,1)} %collective-permute-done.3.p2_ref), channel_id=1, source_target_pairs={{0,8},{8,0},{1,9},{9,1},{2,10},{10,2},{3,11},{11,3},{4,12},{12,4},... | collective-permute-start | bytes 4718600 | tf_op jit(solution)/shard_map/ppermute | solution.py:293
  180.6 1.0 copy-start.4
Sparse Core Ops, SparseCore 0:
  9.1 46.6 all-gather.2
  62.4 76.3 all-gather.4

commit v7 on v5

--- a/solution.py
+++ b/solution.py
@@ -12,6 +12,7 @@
 LANES = 128
 SEQ = ("xh", "z", "core")
 TP = ("y", "xl")
+SMALL = pltpu.CompilerParams(vmem_limit_bytes=12 * 1024 * 1024)
 
 
 def gate_kernel(projected_ref, weight_ref, edge_ref, gated_ref, query_ref):
@@ -40,6 +41,7 @@
             jax.ShapeDtypeStruct((rows, width), jnp.bfloat16),
             jax.ShapeDtypeStruct((rows, width), jnp.float32),
         ),
+        compiler_params=SMALL,
         name="make_gated",
     )(projected, jnp.pad(weights, ((0, 7), (0, 0))), edge)
 
@@ -73,6 +75,7 @@
     return pl.pallas_call(
         pack_second_kernel,
         out_shape=jax.ShapeDtypeStruct((2 * pair.shape[0], pair.shape[1]), pair.dtype),
+        compiler_params=SMALL,
         name="pack_second",
     )(pair, other)
 
@@ -180,6 +183,7 @@
             jax.ShapeDtypeStruct((rows, width), jnp.bfloat16),
             jax.ShapeDtypeStruct((members, rows + 16, width), jnp.bfloat16),
         ),
+        compiler_params=SMALL,
         name="make_payload",
     )(query, mixed, gain.reshape(rows, 1))
 
@@ -283,10 +287,26 @@
             pltpu.VMEM((4 * length, channels), jnp.bfloat16),
             pltpu.SemaphoreType.DMA((4,)),
         ],
-        compiler_params=pltpu.CompilerParams(vmem_limit_bytes=48 * 1024 * 1024),
+        compiler_params=pltpu.CompilerParams(vmem_limit_bytes=52 * 1024 * 1024),
         cost_estimate=pl.CostEstimate(flops=10**10, bytes_accessed=3 * 10**7, transcendentals=0),
         name="feed_forward",
     )(core, sent, weights, *pieces)
+
+
+def finish_kernel(shares_ref, hyena_ref, out_ref):
+    total = shares_ref[0].astype(jnp.float32)
+    for member in range(1, shares_ref.shape[0]):
+        total = total + shares_ref[member].astype(jnp.float32)
+    out_ref[...] = (hyena_ref[...].astype(jnp.float32) + total.T).astype(jnp.bfloat16)
+
+
+def finish(shares, hyena):
+    return pl.pallas_call(
+        finish_kernel,
+        out_shape=jax.ShapeDtypeStruct(hyena.shape, jnp.bfloat16),
+        compiler_params=SMALL,
+        name="finish",
+    )(shares, hyena)
 
 
 def swap(values, axis):
@@ -320,7 +340,7 @@
     gated, query = make_gated(projected, short_weight, edge)
     other_pair = swap(pair, "xh")
     second = pack_second(pair, other_pair)
-    gated, taps, second = lax.optimization_barrier((gated, taps, second))
+    gated, taps, second, bias_part = lax.optimization_barrier((gated, taps, second, bias_part))
     here = lax.all_to_all(
         gated.reshape(groups, per_group, block_len), SEQ, split_axis=0, concat_axis=0, tiled=True
     )
@@ -346,8 +366,7 @@
     sent = lax.all_to_all(payload, TP, split_axis=0, concat_axis=0, tiled=True)
     partial_sum = feed_forward(sent, gate_up, pieces, core.reshape(1), gate_weight.shape[0])
     shares = lax.all_to_all(partial_sum, TP, split_axis=0, concat_axis=0, tiled=True)
-    feed_out = jnp.sum(shares.astype(jnp.float32), axis=0).T
-    return (hyena.astype(jnp.float32) + feed_out).astype(jnp.bfloat16)
+    return finish(shares, hyena)
 
 
 def solution(mesh):

time: 188 us -> 185 us (0.984)
  local copies, waits for them, and re-layouts: 8.23 us -> 4.24 us
  waiting for transfers between devices: 46 us -> 49.5 us
  Pallas kernels: 34.8 us -> 31.5 us
  blocking collectives: 51.9 us -> 54 us
    ppermute x4, waiting for transfers between devices: 5.51 us -> 8.06 us  [swap(): return lax.ppermute(values, axis, [(0, 1), (1, 0)])]
    unnamed x14 -> x8, local copies, waits for them, and re-layouts: 2.49 us -> 0.01 us
  transfers between devices with their start and end apart: 10 -> 10, of which waited for: 5 -> 4; matrix products, arithmetic and copies ran while one was open for 3% -> 2% of each run, Pallas kernels for 12% -> 10%
where the time goes in v7:
time: 185 us
  blocking collectives  54 us (29%)
  waiting for transfers between devices  49.5 us (27%)
  starting transfers between devices  32 us (17%)
  Pallas kernels  31.5 us (17%)
  between operations  13.6 us (7%)
  local copies, waits for them, and re-layouts  4.24 us (2%)
    all_to_all x1, blocking collectives, per_device(): lax.all_to_all(partial_sum, TP, split_axis=0, concat_axis=0, tiled=True)  30.7 us
    all_to_all x1, blocking collectives, per_device(): lax.all_to_all(gated.reshape(groups, per_group, block_len), SEQ, split_ax...  23.3 us
    all_to_all x1, waiting for transfers between devices, per_device(): sent = lax.all_to_all(payload, TP, split_axis=0, concat_axis=0, tiled=True)  22.9 us
    all_to_all x1, waiting for transfers between devices, per_device(): lax.all_to_all(mixed_term.transpose(1, 0, 2), SEQ, split_axis=0, concat_a...  18.6 us
    pallas_call x1, Pallas kernels, long_mixing(): pl.pallas_call(conv_kernel, out_shape=jax.ShapeDtypeStruct(gated.shape, j...  13.7 us
    all_to_all x1, starting transfers between devices, per_device(): lax.all_to_all(filter_taps.reshape(groups, per_group, block_len), SEQ, sp...  12.7 us
    pallas_call x1, Pallas kernels, feed_forward(): pl.pallas_call(functools.partial(feed_kernel, (units, block, per_step, fi...  10.4 us
    ppermute x4, waiting for transfers between devices, swap(): return lax.ppermute(values, axis, [(0, 1), (1, 0)])  8.06 us
  transfers between devices with their start and end apart: 10, of which 4 were waited for; matrix products, arithmetic and copies ran while one was open for 2% of the time, Pallas kernels for 10%

profile of v7, /device:TPU:1, one launch (start us, length us, event | category | flops | bytes accessed | tf_op | source)
XLA Modules:
  0.0 184.8 jit_solution(2858405550629783695)
XLA Ops:
  6.5 2.0 %pack_first.1 = (bf16[24,4096]{1,0:T(8,128)(2,1)}, bf16[44,4096]{1,0:T(8,128)(2,1)}) custom-call(bf16[22,4096]{1,0:T(8,128)(2,1)} %gate_ref.1, bf16[22,4096]{1,0:T(8,128)(2,1)} %up_ref.1, bf16[22,4096]{1,0:T(8,128)(2,1)} %down_ref.1), custom_call_target="tpu_custom_call" | custom-call | tf_op jit(solution)/shard_map/pack_first/pallas_call | solution.py:59
  8.6 12.7 %all-to-all-start = ((bf16[32,16,256]{2,1,0:T(8,128)(2,1)}), bf16[32,16,256]{2,1,0:T(8,128)(2,1)S(1)}, u32[]{:S(2)}, u32[]{:S(2)}) async-start(bf16[32,16,256]{2,1,0:T(8,128)(2,1)} %bitcast.18), calls=%async_computation | async-start | bytes 524288 | tf_op jit(solution)/shard_map/all_to_all | solution.py:333
  21.3 0.0 all-gather.5.cloned.1.call-start
  21.4 3.0 %collective-permute-start.1 = (bf16[44,4096]{1,0:T(8,128)(2,1)}, bf16[44,4096]{1,0:T(8,128)(2,1)S(1)}, u32[]{:S(2)}, u32[]{:S(2)}) collective-permute-start(bf16[44,4096]{1,0:T(8,128)(2,1)} %get-tuple-element.23.pair_ref), channel_id=1, source_target_pairs={{0,128},{128,0},{1,129},{129,1},{2,130},{130,2},{3,131},{131,3},{4... | collective-permute-start | bytes 1081352 | tf_op jit(solution)/shard_map/ppermute | solution.py:313
  24.4 1.2 slice_bitcast_fusion
  25.5 0.2 copy.18
  25.8 3.6 %collective-permute-start = (bf16[8,512]{1,0:T(8,128)(2,1)S(1)}, bf16[8,512]{1,0:T(8,128)(2,1)S(1)}, u32[]{:S(2)}, u32[]{:S(2)}) collective-permute-start(bf16[8,512]{1,0:T(8,128)(2,1)S(1)} %pad.9), channel_id=1, source_target_pairs={{0,8},{8,16},{16,24},{24,32},{32,40},{40,48},{48,56},{56,64},{64,7... | collective-permute-start | bytes 24584 | tf_op jit(solution)/shard_map/ppermute | solution.py:330
  29.4 0.8 dynamic_slice.6.bias_ref
  30.2 1.8 make_gated.1
  32.0 4.4 %collective-permute-done.1.other_ref = bf16[44,4096]{1,0:T(8,128)(2,1)S(1)} collective-permute-done((bf16[44,4096]{1,0:T(8,128)(2,1)}, bf16[44,4096]{1,0:T(8,128)(2,1)S(1)}, u32[]{:S(2)}, u32[]{:S(2)}) %collective-permute-start.1) | collective-permute-done | bytes 360480 | tf_op jit(solution)/shard_map/ppermute | solution.py:313
  36.4 1.0 pack_second.1
  37.4 0.0 all-gather.5.cloned.1.call-update
  37.4 23.3 %all_to_all.25 = bf16[32,16,256]{2,1,0:T(8,128)(2,1)S(1)} all-to-all(bf16[32,16,256]{2,1,0:T(8,128)(2,1)S(1)} %bitcast.14), channel_id=1, replica_groups=mesh['xh'=2,'z'=8,'core'=2,'y'=4,'xl'=2] {'xh','z','core'}, dimensions={0} | all-to-all | bytes 524288 | tf_op jit(solution)/shard_map/all_to_all | solution.py:344
  60.7 1.0 collective-permute-start.2
  61.7 0.3 collective-permute-start.3
  62.0 0.1 copy.20
  62.1 0.1 reshape_reshape.4.taps_ref
  62.2 0.1 copy.25
  62.3 13.7 %long_mixing.1 = bf16[16,32,256]{2,1,0:T(8,128)(2,1)S(1)} custom-call(f32[16]{0:T(128)S(1)} %dynamic_slice.6.bias_ref, bf16[16,32,256]{2,1,0:T(8,128)(2,1)S(1)} %bitcast.16, bf16[16,1,8192]{2,1,0:T(2,128)(2,1)S(1)} %reshape_reshape.4.taps_ref), custom_call_target="tpu_custom_call" | custom-call | flops 8589934592 | bytes 786432 | tf_op jit(solution)/shard_map/long_mixing/pallas_call | solution.py:150
  76.1 0.9 copy.22
  76.9 6.2 %all-to-all-start.2 = ((bf16[32,16,256]{2,1,0:T(8,128)(2,1)}), bf16[32,16,256]{2,1,0:T(8,128)(2,1)S(1)}, u32[]{:S(2)}, u32[]{:S(2)}) async-start(bf16[32,16,256]{2,1,0:T(8,128)(2,1)} %copy.22), calls=%async_computation.2 | async-start | bytes 524288 | tf_op jit(solution)/shard_map/all_to_all | solution.py:357
  83.1 0.8 dynamic_slice.7
  83.9 0.1 copy.23.gain_ref
  84.0 18.6 %all-to-all-done.2 = bf16[32,16,256]{2,1,0:T(8,128)(2,1)S(1)} async-done(((bf16[32,16,256]{2,1,0:T(8,128)(2,1)}), bf16[32,16,256]{2,1,0:T(8,128)(2,1)S(1)}, u32[]{:S(2)}, u32[]{:S(2)}) %all-to-all-start.2) | async-done | bytes 262176 | tf_op jit(solution)/shard_map/all_to_all | solution.py:357
  102.6 1.6 make_payload.1
  104.1 4.5 %all-to-all-start.3 = ((bf16[8,528,256]{2,1,0:T(8,128)(2,1)}), bf16[8,528,256]{2,1,0:T(8,128)(2,1)}, u32[]{:S(2)}, u32[]{:S(2)}) async-start(bf16[8,528,256]{2,1,0:T(8,128)(2,1)} %get-tuple-element.32), calls=%async_computation.3 | async-start | bytes 4325376 | tf_op jit(solution)/shard_map/all_to_all | solution.py:366
  108.6 0.6 collective-permute-start.4
  109.3 3.6 %collective-permute-done.4.p3_ref = bf16[192,4096]{1,0:T(8,128)(2,1)} collective-permute-done((bf16[192,4096]{1,0:T(8,128)(2,1)}, bf16[192,4096]{1,0:T(8,128)(2,1)}, u32[]{:S(2)}, u32[]{:S(2)}) %collective-permute-start.4) | collective-permute-done | bytes 1572896 | tf_op jit(solution)/shard_map/ppermute | solution.py:313
  112.9 22.9 %all-to-all-done.3.sent_ref = bf16[8,528,256]{2,1,0:T(8,128)(2,1)} async-done(((bf16[8,528,256]{2,1,0:T(8,128)(2,1)}), bf16[8,528,256]{2,1,0:T(8,128)(2,1)}, u32[]{:S(2)}, u32[]{:S(2)}) %all-to-all-start.3) | async-done | bytes 2162720 | tf_op jit(solution)/shard_map/all_to_all | solution.py:366
  135.8 10.4 %feed_forward.1 = bf16[8,256,512]{2,1,0:T(8,128)(2,1)} custom-call(s32[1]{0:T(128)} %bitcast.core_ref, bf16[8,528,256]{2,1,0:T(8,128)(2,1)} %all-to-all-done.3.sent_ref, bf16[1408,4096]{1,0:T(8,128)(2,1)} %all-gather.5.cloned.1.call-done.weight_ref, bf16[192,4096]{1,0:T(8,128)(2,1)S(1)} %copy-done.2, bf16[192,4096]{1,0:T(8,128)(2,1)} %collective-permute-done.2.p1_ref, ...), custom_call_target="tpu_custom_call" | custom-call | flops 10000000000 | bytes 30000000 | tf_op jit(solution)/shard_map/feed_forward/pallas_call | solution.py:263
  146.2 30.7 %all_to_all.26.shares_ref = bf16[8,256,512]{2,1,0:T(8,128)(2,1)S(1)} all-to-all(bf16[8,256,512]{2,1,0:T(8,128)(2,1)} %feed_forward.1), channel_id=1, replica_groups=mesh['xh'=2,'z'=8,'core'=2,'y'=4,'xl'=2] {'y','xl'}, dimensions={0} | all-to-all | bytes 4194304 | tf_op jit(solution)/shard_map/all_to_all | solution.py:368
  176.9 1.0 finish.1
  (20 shorter events, 0.1 us)
Async XLA Ops:
  6.5 23.7 %copy-start = (bf16[3,512,256]{2,1,0:T(8,128)(2,1)S(1)}, bf16[3,512,256]{2,1,0:T(8,128)(2,1)}, u32[]{:S(2)}) copy-start(bf16[3,512,256]{2,1,0:T(8,128)(2,1)} %projected_ref.1) | copy-start | bytes 2359300
  6.5 22.9 %copy-start.3 = (f32[3,512,3]{1,2,0:T(4,128)S(1)}, f32[3,512,3]{1,2,0:T(4,128)}, u32[]{:S(2)}) copy-start(f32[3,512,3]{1,2,0:T(4,128)} %param.10) | copy-start | bytes 55300
  6.5 54.1 %all-gather.3.cloned.1.call-start = ((), (), s32[]{:S(2)}) async-start(), calls=%async_computation.5 | async-start | bytes 1769472 | tf_op jit(solution)/shard_map/all_gather | solution.py:328
  8.6 27.8 %copy-start.1 = (bf16[44,4096]{1,0:T(8,128)(2,1)S(1)}, bf16[44,4096]{1,0:T(8,128)(2,1)}, u32[]{:S(2)}) copy-start(bf16[44,4096]{1,0:T(8,128)(2,1)} %get-tuple-element.23.pair_ref) | copy-start | bytes 1081348
  8.6 28.8 %all-to-all-start = ((bf16[32,16,256]{2,1,0:T(8,128)(2,1)}), bf16[32,16,256]{2,1,0:T(8,128)(2,1)S(1)}, u32[]{:S(2)}, u32[]{:S(2)}) async-start(bf16[32,16,256]{2,1,0:T(8,128)(2,1)} %bitcast.18), calls=%async_computation | async-start | bytes 524288 | tf_op jit(solution)/shard_map/all_to_all | solution.py:333
  21.3 114.5 %all-gather.5.cloned.1.call-start = ((), (), s32[]{:S(2)}) async-start(), calls=%async_computation.6 | async-start | bytes 12255232 | tf_op jit(solution)/shard_map/all_gather | solution.py:349
  21.4 15.0 %collective-permute-start.1 = (bf16[44,4096]{1,0:T(8,128)(2,1)}, bf16[44,4096]{1,0:T(8,128)(2,1)S(1)}, u32[]{:S(2)}, u32[]{:S(2)}) collective-permute-start(bf16[44,4096]{1,0:T(8,128)(2,1)} %get-tuple-element.23.pair_ref), channel_id=1, source_target_pairs={{0,128},{128,0},{1,129},{129,1},{2,130},{130,2},{3,131},{131,3},{4... | collective-permute-start | bytes 1081352 | tf_op jit(solution)/shard_map/ppermute | solution.py:313
  25.8 4.4 %collective-permute-start = (bf16[8,512]{1,0:T(8,128)(2,1)S(1)}, bf16[8,512]{1,0:T(8,128)(2,1)S(1)}, u32[]{:S(2)}, u32[]{:S(2)}) collective-permute-start(bf16[8,512]{1,0:T(8,128)(2,1)S(1)} %pad.9), channel_id=1, source_target_pairs={{0,8},{8,16},{16,24},{24,32},{32,40},{40,48},{48,56},{56,64},{64,7... | collective-permute-start | bytes 24584 | tf_op jit(solution)/shard_map/ppermute | solution.py:330
  60.7 15.4 %collective-permute-start.2 = (bf16[192,4096]{1,0:T(8,128)(2,1)}, bf16[192,4096]{1,0:T(8,128)(2,1)}, u32[]{:S(2)}, u32[]{:S(2)}) collective-permute-start(bf16[192,4096]{1,0:T(8,128)(2,1)} %all-gather.3.cloned.1.call-done.p0_ref), channel_id=1, source_target_pairs={{0,8},{8,0},{1,9},{9,1},{2,10},{10,2},{3,11},{11,3},{4,12},{12,4},... | collective-permute-start | bytes 4718600 | tf_op jit(solution)/shard_map/ppermute | solution.py:313
  61.7 42.4 %collective-permute-start.3 = (bf16[192,4096]{1,0:T(8,128)(2,1)}, bf16[192,4096]{1,0:T(8,128)(2,1)}, u32[]{:S(2)}, u32[]{:S(2)}) collective-permute-start(bf16[192,4096]{1,0:T(8,128)(2,1)} %all-gather.3.cloned.1.call-done.p0_ref), channel_id=1, source_target_pairs={{0,128},{128,0},{1,129},{129,1},{2,130},{130,2},{3,131},{131,3},{4... | collective-permute-start | bytes 4718600 | tf_op jit(solution)/shard_map/ppermute | solution.py:313
  76.9 25.7 %all-to-all-start.2 = ((bf16[32,16,256]{2,1,0:T(8,128)(2,1)}), bf16[32,16,256]{2,1,0:T(8,128)(2,1)S(1)}, u32[]{:S(2)}, u32[]{:S(2)}) async-start(bf16[32,16,256]{2,1,0:T(8,128)(2,1)} %copy.22), calls=%async_computation.2 | async-start | bytes 524288 | tf_op jit(solution)/shard_map/all_to_all | solution.py:357
  104.1 31.6 %copy-start.2 = (bf16[192,4096]{1,0:T(8,128)(2,1)S(1)}, bf16[192,4096]{1,0:T(8,128)(2,1)}, u32[]{:S(2)}) copy-start(bf16[192,4096]{1,0:T(8,128)(2,1)} %all-gather.3.cloned.1.call-done.p0_ref) | copy-start | bytes 4718596
  104.1 31.6 %all-to-all-start.3 = ((bf16[8,528,256]{2,1,0:T(8,128)(2,1)}), bf16[8,528,256]{2,1,0:T(8,128)(2,1)}, u32[]{:S(2)}, u32[]{:S(2)}) async-start(bf16[8,528,256]{2,1,0:T(8,128)(2,1)} %get-tuple-element.32), calls=%async_computation.3 | async-start | bytes 4325376 | tf_op jit(solution)/shard_map/all_to_all | solution.py:366
  108.6 4.3 %collective-permute-start.4 = (bf16[192,4096]{1,0:T(8,128)(2,1)}, bf16[192,4096]{1,0:T(8,128)(2,1)}, u32[]{:S(2)}, u32[]{:S(2)}) collective-permute-start(bf16[192,4096]{1,0:T(8,128)(2,1)} %collective-permute-done.3.p2_ref), channel_id=1, source_target_pairs={{0,8},{8,0},{1,9},{9,1},{2,10},{10,2},{3,11},{11,3},{4,12},{12,4},... | collective-permute-start | bytes 4718600 | tf_op jit(solution)/shard_map/ppermute | solution.py:313
Sparse Core Ops, SparseCore 0:
  9.1 45.5 all-gather.2
  56.5 78.8 all-gather.4

commit v8 on v3

--- a/solution.py
+++ b/solution.py
@@ -12,6 +12,7 @@
 LANES = 128
 SEQ = ("xh", "z", "core")
 TP = ("y", "xl")
+SMALL = pltpu.CompilerParams(vmem_limit_bytes=12 * 1024 * 1024)
 
 
 def gate_kernel(projected_ref, taps_ref, weight_ref, edge_ref, sent_ref, query_ref):
@@ -43,6 +44,7 @@
             jax.ShapeDtypeStruct((groups, 2, rows // groups, width), jnp.bfloat16),
             jax.ShapeDtypeStruct((rows, width), jnp.float32),
         ),
+        compiler_params=SMALL,
         name="make_gated",
     )(projected, taps, jnp.pad(weights, ((0, 7), (0, 0))), edge)
 
@@ -76,6 +78,7 @@
     return pl.pallas_call(
         pack_second_kernel,
         out_shape=jax.ShapeDtypeStruct((2 * pair.shape[0], pair.shape[1]), pair.dtype),
+        compiler_params=SMALL,
         name="pack_second",
     )(pair, other)
 
@@ -187,6 +190,7 @@
             jax.ShapeDtypeStruct((rows, width), jnp.bfloat16),
             jax.ShapeDtypeStruct((members, rows + 16, width), jnp.bfloat16),
         ),
+        compiler_params=SMALL,
         name="make_payload",
     )(query, mixed, gain.reshape(rows, 1))
 
@@ -260,7 +264,7 @@
     length = pieces[0].shape[0]
     block = units + -units % 8
     blocks = 2 * length // block
-    per_step, out_step = 4, 2
+    per_step, out_step = 8, 4
     first_steps = blocks // per_step
     anywhere = pl.BlockSpec(memory_space=pl.ANY)
     return pl.pallas_call(
@@ -290,10 +294,26 @@
             pltpu.VMEM((4 * length, channels), jnp.bfloat16),
             pltpu.SemaphoreType.DMA((4,)),
         ],
-        compiler_params=pltpu.CompilerParams(vmem_limit_bytes=48 * 1024 * 1024),
+        compiler_params=pltpu.CompilerParams(vmem_limit_bytes=52 * 1024 * 1024),
         cost_estimate=pl.CostEstimate(flops=10**10, bytes_accessed=3 * 10**7, transcendentals=0),
         name="feed_forward",
     )(core, sent, weights, *pieces)
+
+
+def finish_kernel(shares_ref, hyena_ref, out_ref):
+    total = shares_ref[0].astype(jnp.float32)
+    for member in range(1, shares_ref.shape[0]):
+        total = total + shares_ref[member].astype(jnp.float32)
+    out_ref[...] = (hyena_ref[...].astype(jnp.float32) + total.T).astype(jnp.bfloat16)
+
+
+def finish(shares, hyena):
+    return pl.pallas_call(
+        finish_kernel,
+        out_shape=jax.ShapeDtypeStruct(hyena.shape, jnp.bfloat16),
+        compiler_params=SMALL,
+        name="finish",
+    )(shares, hyena)
 
 
 def swap(values, axis):
@@ -318,6 +338,7 @@
         jnp.pad(edge, ((0, 2), (0, 0))), SEQ, [(i, i + 1) for i in range(groups - 1)]
     )
     sent, query = make_gated(projected, filter_taps, short_weight, edge, groups)
+    sent, bias_part = lax.optimization_barrier((sent, bias_part))
     here = lax.all_to_all(sent, SEQ, split_axis=0, concat_axis=0, tiled=True)
 
     core = lax.axis_index("core")
@@ -343,8 +364,7 @@
     sent = lax.all_to_all(payload, TP, split_axis=0, concat_axis=0, tiled=True)
     partial_sum = feed_forward(sent, gate_up, pieces, core.reshape(1), gate_weight.shape[0])
     shares = lax.all_to_all(partial_sum, TP, split_axis=0, concat_axis=0, tiled=True)
-    feed_out = jnp.sum(shares.astype(jnp.float32), axis=0).T
-    return (hyena.astype(jnp.float32) + feed_out).astype(jnp.bfloat16)
+    return finish(shares, hyena)
 
 
 def solution(mesh):

time: 189 us -> 188 us (level)
  waiting for transfers between devices: 62.5 us -> 67.8 us
  Pallas kernels: 35.9 us -> 32.2 us
  local copies, waits for them, and re-layouts: 8.45 us -> 5.38 us
    all_gather x1, waiting for transfers between devices: 0.01 us -> 2.15 us  [per_device(): lax.all_gather(pack_second(pair, other_pair), ('z', 'core'), axis=0, tile...]
  transfers between devices with their start and end apart: 10 -> 10, of which waited for: 5 -> 7; matrix products, arithmetic and copies ran while one was open for 3% -> 3% of each run, Pallas kernels for 12% -> 10%
where the time goes in v8:
time: 188 us; the launch traced here: 187 us
  waiting for transfers between devices  67.8 us (36%)
  starting transfers between devices  36.9 us (20%)
  Pallas kernels  32.2 us (17%)
  blocking collectives  31.1 us (17%)
  between operations  13.6 us (7%)
  local copies, waits for them, and re-layouts  5.38 us (3%)
    all_to_all x1, blocking collectives, per_device(): lax.all_to_all(partial_sum, TP, split_axis=0, concat_axis=0, tiled=True)  31.1 us
    all_to_all x1, waiting for transfers between devices, per_device(): sent = lax.all_to_all(payload, TP, split_axis=0, concat_axis=0, tiled=True)  23 us
    all_to_all x1, waiting for transfers between devices, per_device(): lax.all_to_all(mixed_term.transpose(1, 0, 2), SEQ, split_axis=0, concat_a...  17.3 us
    ppermute x4, waiting for transfers between devices, swap(): return lax.ppermute(values, axis, [(0, 1), (1, 0)])  16.2 us
    pallas_call x1, Pallas kernels, long_mixing(): pl.pallas_call(conv_kernel, out_shape=jax.ShapeDtypeStruct(gated.shape, j...  13.6 us
    all_to_all x1, starting transfers between devices, per_device(): here = lax.all_to_all(sent, SEQ, split_axis=0, concat_axis=0, tiled=True)  12.3 us
    pallas_call x1, Pallas kernels, feed_forward(): pl.pallas_call(functools.partial(feed_kernel, (units, block, per_step, fi...  10.3 us
    ppermute x4, starting transfers between devices, swap(): return lax.ppermute(values, axis, [(0, 1), (1, 0)])  10.1 us
  transfers between devices with their start and end apart: 10, of which 7 were waited for; matrix products, arithmetic and copies ran while one was open for 3% of the time, Pallas kernels for 10%

profile of v8, /device:TPU:1, one launch (start us, length us, event | category | flops | bytes accessed | tf_op | source)
XLA Modules:
  0.0 187.0 jit_solution(5356416371459249259)
XLA Ops:
  6.5 2.1 %pack_first.1 = (bf16[24,4096]{1,0:T(8,128)(2,1)}, bf16[44,4096]{1,0:T(8,128)(2,1)}) custom-call(bf16[22,4096]{1,0:T(8,128)(2,1)} %gate_ref.1, bf16[22,4096]{1,0:T(8,128)(2,1)} %up_ref.1, bf16[22,4096]{1,0:T(8,128)(2,1)} %down_ref.1), custom_call_target="tpu_custom_call" | custom-call | tf_op jit(solution)/shard_map/pack_first/pallas_call | solution.py:62
  8.6 1.2 slice_bitcast_fusion
  9.8 0.2 copy.17
  10.1 4.9 %collective-permute-start = (bf16[8,512]{1,0:T(8,128)(2,1)S(1)}, bf16[8,512]{1,0:T(8,128)(2,1)S(1)}, u32[]{:S(2)}, u32[]{:S(2)}) collective-permute-start(bf16[8,512]{1,0:T(8,128)(2,1)S(1)} %pad.9), channel_id=1, source_target_pairs={{0,8},{8,16},{16,24},{24,32},{32,40},{40,48},{48,56},{56,64},{64,7... | collective-permute-start | bytes 24584 | tf_op jit(solution)/shard_map/ppermute | solution.py:337
  15.0 0.8 reshape.16
  15.8 0.8 dynamic_slice.6.bias_ref
  16.6 2.6 %make_gated.1 = (bf16[32,2,16,256]{3,2,1,0:T(8,128)(2,1)}, f32[512,256]{1,0:T(8,128)S(1)}) custom-call(bf16[3,512,256]{2,1,0:T(8,128)(2,1)S(1)} %copy-done, bf16[512,256]{1,0:T(8,128)(2,1)S(1)} %copy-done.2, f32[16,512]{1,0:T(8,128)S(1)} %pad.8.weight_ref, bf16[8,512]{1,0:T(8,128)(2,1)S(1)} %collective-permute-done.edge_ref), custom_call_target="tpu_custom_call" | custom-call | tf_op jit(solution)/shard_map/make_gated/pallas_call | solution.py:41
  19.2 12.3 %all-to-all-start = ((bf16[32,2,16,256]{3,2,1,0:T(8,128)(2,1)}), bf16[32,2,16,256]{3,2,1,0:T(8,128)(2,1)S(1)}, u32[]{:S(2)}, u32[]{:S(2)}) async-start(bf16[32,2,16,256]{3,2,1,0:T(8,128)(2,1)} %get-tuple-element.24), calls=%async_computation | async-start | bytes 1048576 | tf_op jit(solution)/shard_map/all_to_all | solution.py:342
  31.5 3.0 %collective-permute-start.1 = (bf16[44,4096]{1,0:T(8,128)(2,1)S(1)}, bf16[44,4096]{1,0:T(8,128)(2,1)S(1)}, u32[]{:S(2)}, u32[]{:S(2)}) collective-permute-start(bf16[44,4096]{1,0:T(8,128)(2,1)S(1)} %copy-done.1), channel_id=1, source_target_pairs={{0,128},{128,0},{1,129},{129,1},{2,130},{130,2},{3,131},{131,3},{4... | collective-permute-start | bytes 1081352 | tf_op jit(solution)/shard_map/ppermute | solution.py:320
  34.5 12.7 %collective-permute-done.1.other_ref = bf16[44,4096]{1,0:T(8,128)(2,1)S(1)} collective-permute-done((bf16[44,4096]{1,0:T(8,128)(2,1)S(1)}, bf16[44,4096]{1,0:T(8,128)(2,1)S(1)}, u32[]{:S(2)}, u32[]{:S(2)}) %collective-permute-start.1) | collective-permute-done | bytes 360480 | tf_op jit(solution)/shard_map/ppermute | solution.py:320
  47.2 7.4 %all-to-all-done = bf16[32,2,16,256]{3,2,1,0:T(8,128)(2,1)S(1)} async-done(((bf16[32,2,16,256]{3,2,1,0:T(8,128)(2,1)}), bf16[32,2,16,256]{3,2,1,0:T(8,128)(2,1)S(1)}, u32[]{:S(2)}, u32[]{:S(2)}) %all-to-all-start) | async-done | bytes 524320 | tf_op jit(solution)/shard_map/all_to_all | solution.py:342
  54.5 1.0 pack_second.1
  55.5 1.7 all-gather.3.cloned.1.call-done.p0_ref
  57.2 3.8 %collective-permute-start.2 = (bf16[192,4096]{1,0:T(8,128)(2,1)}, bf16[192,4096]{1,0:T(8,128)(2,1)S(1)}, u32[]{:S(2)}, u32[]{:S(2)}) collective-permute-start(bf16[192,4096]{1,0:T(8,128)(2,1)} %all-gather.3.cloned.1.call-done.p0_ref), channel_id=1, source_target_pairs={{0,8},{8,0},{1,9},{9,1},{2,10},{10,2},{3,11},{11,3},{4,12},{12,4},... | collective-permute-start | bytes 4718600 | tf_op jit(solution)/shard_map/ppermute | solution.py:320
  61.0 2.7 %collective-permute-start.3 = (bf16[192,4096]{1,0:T(8,128)(2,1)}, bf16[192,4096]{1,0:T(8,128)(2,1)}, u32[]{:S(2)}, u32[]{:S(2)}) collective-permute-start(bf16[192,4096]{1,0:T(8,128)(2,1)} %all-gather.3.cloned.1.call-done.p0_ref), channel_id=1, source_target_pairs={{0,128},{128,0},{1,129},{129,1},{2,130},{130,2},{3,131},{131,3},{4... | collective-permute-start | bytes 4718600 | tf_op jit(solution)/shard_map/ppermute | solution.py:320
  63.7 0.3 copy.23
  64.0 0.1 reshape_reshape_squeeze.4.taps_ref
  64.2 13.6 %long_mixing.1 = bf16[16,32,256]{2,1,0:T(8,128)(2,1)S(1)} custom-call(f32[16]{0:T(128)S(1)} %dynamic_slice.6.bias_ref, bf16[16,32,256]{2,1,0:T(8,128)(2,1)S(1)} %get-tuple-element.38.gated_ref, bf16[16,1,8192]{2,1,0:T(2,128)(2,1)S(1)} %reshape_reshape_squeeze.4.taps_ref), custom_call_target="tpu_custom_call" | custom-call | flops 8589934592 | bytes 786432 | tf_op jit(solution)/shard_map/long_mixing/pallas_call | solution.py:157
  77.9 1.0 copy.20
  78.9 4.7 %all-to-all-start.1 = ((bf16[32,16,256]{2,1,0:T(8,128)(2,1)}), bf16[32,16,256]{2,1,0:T(8,128)(2,1)S(1)}, u32[]{:S(2)}, u32[]{:S(2)}) async-start(bf16[32,16,256]{2,1,0:T(8,128)(2,1)} %copy.20), calls=%async_computation.1 | async-start | bytes 524288 | tf_op jit(solution)/shard_map/all_to_all | solution.py:355
  83.6 0.8 dynamic_slice.7
  84.4 0.1 copy.21.gain_ref
  84.5 17.3 %all-to-all-done.1 = bf16[32,16,256]{2,1,0:T(8,128)(2,1)S(1)} async-done(((bf16[32,16,256]{2,1,0:T(8,128)(2,1)}), bf16[32,16,256]{2,1,0:T(8,128)(2,1)S(1)}, u32[]{:S(2)}, u32[]{:S(2)}) %all-to-all-start.1) | async-done | bytes 262176 | tf_op jit(solution)/shard_map/all_to_all | solution.py:355
  101.9 1.6 make_payload.1
  103.4 4.8 %all-to-all-start.2 = ((bf16[8,528,256]{2,1,0:T(8,128)(2,1)}), bf16[8,528,256]{2,1,0:T(8,128)(2,1)}, u32[]{:S(2)}, u32[]{:S(2)}) async-start(bf16[8,528,256]{2,1,0:T(8,128)(2,1)} %get-tuple-element.32), calls=%async_computation.2 | async-start | bytes 4325376 | tf_op jit(solution)/shard_map/all_to_all | solution.py:364
  108.3 0.7 collective-permute-start.4
  108.9 3.5 %collective-permute-done.4.p3_ref = bf16[192,4096]{1,0:T(8,128)(2,1)} collective-permute-done((bf16[192,4096]{1,0:T(8,128)(2,1)}, bf16[192,4096]{1,0:T(8,128)(2,1)}, u32[]{:S(2)}, u32[]{:S(2)}) %collective-permute-start.4) | collective-permute-done | bytes 1572896 | tf_op jit(solution)/shard_map/ppermute | solution.py:320
  112.5 23.0 %all-to-all-done.2.sent_ref = bf16[8,528,256]{2,1,0:T(8,128)(2,1)} async-done(((bf16[8,528,256]{2,1,0:T(8,128)(2,1)}), bf16[8,528,256]{2,1,0:T(8,128)(2,1)}, u32[]{:S(2)}, u32[]{:S(2)}) %all-to-all-start.2) | async-done | bytes 2162720 | tf_op jit(solution)/shard_map/all_to_all | solution.py:364
  135.5 2.2 %all-gather.5.cloned.1.call-done.weight_ref = bf16[1408,4096]{1,0:T(8,128)(2,1)} async-done(((bf16[88,4096]{1,0:T(8,128)(2,1)}), bf16[1408,4096]{1,0:T(8,128)(2,1)}) %all-gather.5.cloned.1.call-update) | async-done | bytes 11534352 | tf_op jit(solution)/shard_map/all_gather | solution.py:347
  137.6 10.3 %feed_forward.1 = bf16[8,256,512]{2,1,0:T(8,128)(2,1)} custom-call(s32[1]{0:T(128)} %bitcast.core_ref, bf16[8,528,256]{2,1,0:T(8,128)(2,1)} %all-to-all-done.2.sent_ref, bf16[1408,4096]{1,0:T(8,128)(2,1)} %all-gather.5.cloned.1.call-done.weight_ref, bf16[192,4096]{1,0:T(8,128)(2,1)S(1)} %copy-done.3, bf16[192,4096]{1,0:T(8,128)(2,1)} %copy-done.4, ...), custom_call_target="tpu_custom_call" | custom-call | flops 10000000000 | bytes 30000000 | tf_op jit(solution)/shard_map/feed_forward/pallas_call | solution.py:270
  148.0 31.1 %all_to_all.20.shares_ref = bf16[8,256,512]{2,1,0:T(8,128)(2,1)S(1)} all-to-all(bf16[8,256,512]{2,1,0:T(8,128)(2,1)} %feed_forward.1), channel_id=1, replica_groups=mesh['xh'=2,'z'=8,'core'=2,'y'=4,'xl'=2] {'y','xl'}, dimensions={0} | all-to-all | bytes 4194304 | tf_op jit(solution)/shard_map/all_to_all | solution.py:366
  179.1 1.0 finish.1
  (21 shorter events, 0.2 us)
Async XLA Ops:
  6.5 10.0 %copy-start = (bf16[3,512,256]{2,1,0:T(8,128)(2,1)S(1)}, bf16[3,512,256]{2,1,0:T(8,128)(2,1)}, u32[]{:S(2)}) copy-start(bf16[3,512,256]{2,1,0:T(8,128)(2,1)} %projected_ref.1) | copy-start | bytes 2359300
  6.5 10.0 %copy-start.2 = (bf16[512,256]{1,0:T(8,128)(2,1)S(1)}, bf16[512,256]{1,0:T(8,128)(2,1)}, u32[]{:S(2)}) copy-start(bf16[512,256]{1,0:T(8,128)(2,1)} %taps_ref.1) | copy-start | bytes 786436
  6.5 50.7 %all-gather.3.cloned.1.call-start = ((), (), s32[]{:S(2)}) async-start(), calls=%async_computation.4 | async-start | bytes 1769472 | tf_op jit(solution)/shard_map/all_gather | solution.py:335
  8.6 22.9 %copy-start.1 = (bf16[44,4096]{1,0:T(8,128)(2,1)S(1)}, bf16[44,4096]{1,0:T(8,128)(2,1)}, u32[]{:S(2)}) copy-start(bf16[44,4096]{1,0:T(8,128)(2,1)} %get-tuple-element.25.pair_ref) | copy-start | bytes 1081348
  10.1 6.5 %collective-permute-start = (bf16[8,512]{1,0:T(8,128)(2,1)S(1)}, bf16[8,512]{1,0:T(8,128)(2,1)S(1)}, u32[]{:S(2)}, u32[]{:S(2)}) collective-permute-start(bf16[8,512]{1,0:T(8,128)(2,1)S(1)} %pad.9), channel_id=1, source_target_pairs={{0,8},{8,16},{16,24},{24,32},{32,40},{40,48},{48,56},{56,64},{64,7... | collective-permute-start | bytes 24584 | tf_op jit(solution)/shard_map/ppermute | solution.py:337
  19.2 35.4 %all-to-all-start = ((bf16[32,2,16,256]{3,2,1,0:T(8,128)(2,1)}), bf16[32,2,16,256]{3,2,1,0:T(8,128)(2,1)S(1)}, u32[]{:S(2)}, u32[]{:S(2)}) async-start(bf16[32,2,16,256]{3,2,1,0:T(8,128)(2,1)} %get-tuple-element.24), calls=%async_computation | async-start | bytes 1048576 | tf_op jit(solution)/shard_map/all_to_all | solution.py:342
  31.4 106.2 %all-gather.5.cloned.1.call-start = ((), (), s32[]{:S(2)}) async-start(), calls=%async_computation.5 | async-start | bytes 12255232 | tf_op jit(solution)/shard_map/all_gather | solution.py:347
  31.5 15.7 %collective-permute-start.1 = (bf16[44,4096]{1,0:T(8,128)(2,1)S(1)}, bf16[44,4096]{1,0:T(8,128)(2,1)S(1)}, u32[]{:S(2)}, u32[]{:S(2)}) collective-permute-start(bf16[44,4096]{1,0:T(8,128)(2,1)S(1)} %copy-done.1), channel_id=1, source_target_pairs={{0,128},{128,0},{1,129},{129,1},{2,130},{130,2},{3,131},{131,3},{4... | collective-permute-start | bytes 1081352 | tf_op jit(solution)/shard_map/ppermute | solution.py:320
  57.2 20.6 %collective-permute-start.2 = (bf16[192,4096]{1,0:T(8,128)(2,1)}, bf16[192,4096]{1,0:T(8,128)(2,1)S(1)}, u32[]{:S(2)}, u32[]{:S(2)}) collective-permute-start(bf16[192,4096]{1,0:T(8,128)(2,1)} %all-gather.3.cloned.1.call-done.p0_ref), channel_id=1, source_target_pairs={{0,8},{8,0},{1,9},{9,1},{2,10},{10,2},{3,11},{11,3},{4,12},{12,4},... | collective-permute-start | bytes 4718600 | tf_op jit(solution)/shard_map/ppermute | solution.py:320
  61.0 42.4 %collective-permute-start.3 = (bf16[192,4096]{1,0:T(8,128)(2,1)}, bf16[192,4096]{1,0:T(8,128)(2,1)}, u32[]{:S(2)}, u32[]{:S(2)}) collective-permute-start(bf16[192,4096]{1,0:T(8,128)(2,1)} %all-gather.3.cloned.1.call-done.p0_ref), channel_id=1, source_target_pairs={{0,128},{128,0},{1,129},{129,1},{2,130},{130,2},{3,131},{131,3},{4... | collective-permute-start | bytes 4718600 | tf_op jit(solution)/shard_map/ppermute | solution.py:320
  77.8 25.6 %copy-start.4 = (bf16[192,4096]{1,0:T(8,128)(2,1)}, bf16[192,4096]{1,0:T(8,128)(2,1)S(1)}, u32[]{:S(2)}) copy-start(bf16[192,4096]{1,0:T(8,128)(2,1)S(1)} %collective-permute-done.2.p1_ref) | copy-start | bytes 4718596
  78.9 23.0 %all-to-all-start.1 = ((bf16[32,16,256]{2,1,0:T(8,128)(2,1)}), bf16[32,16,256]{2,1,0:T(8,128)(2,1)S(1)}, u32[]{:S(2)}, u32[]{:S(2)}) async-start(bf16[32,16,256]{2,1,0:T(8,128)(2,1)} %copy.20), calls=%async_computation.1 | async-start | bytes 524288 | tf_op jit(solution)/shard_map/all_to_all | solution.py:355
  103.4 34.2 %copy-start.3 = (bf16[192,4096]{1,0:T(8,128)(2,1)S(1)}, bf16[192,4096]{1,0:T(8,128)(2,1)}, u32[]{:S(2)}) copy-start(bf16[192,4096]{1,0:T(8,128)(2,1)} %all-gather.3.cloned.1.call-done.p0_ref) | copy-start | bytes 4718596
  103.4 32.0 %all-to-all-start.2 = ((bf16[8,528,256]{2,1,0:T(8,128)(2,1)}), bf16[8,528,256]{2,1,0:T(8,128)(2,1)}, u32[]{:S(2)}, u32[]{:S(2)}) async-start(bf16[8,528,256]{2,1,0:T(8,128)(2,1)} %get-tuple-element.32), calls=%async_computation.2 | async-start | bytes 4325376 | tf_op jit(solution)/shard_map/all_to_all | solution.py:364
  108.3 4.2 %collective-permute-start.4 = (bf16[192,4096]{1,0:T(8,128)(2,1)}, bf16[192,4096]{1,0:T(8,128)(2,1)}, u32[]{:S(2)}, u32[]{:S(2)}) collective-permute-start(bf16[192,4096]{1,0:T(8,128)(2,1)} %collective-permute-done.3.p2_ref), channel_id=1, source_target_pairs={{0,8},{8,0},{1,9},{9,1},{2,10},{10,2},{3,11},{11,3},{4,12},{12,4},... | collective-permute-start | bytes 4718600 | tf_op jit(solution)/shard_map/ppermute | solution.py:320
Sparse Core Ops, SparseCore 0:
  9.1 48.0 all-gather.2
  59.1 78.5 all-gather.4

commit v9 on v7

--- a/solution.py
+++ b/solution.py
@@ -46,37 +46,32 @@
     )(projected, jnp.pad(weights, ((0, 7), (0, 0))), edge)
 
 
-def pack_first_kernel(gate_ref, up_ref, down_ref, first_ref, pair_ref):
-    gate, up = gate_ref[...].astype(jnp.float32), up_ref[...].astype(jnp.float32)
-    down = down_ref[...].astype(jnp.float32)
-    blank = jnp.zeros((first_ref.shape[0] - down.shape[0], down.shape[1]), jnp.float32)
-    first_ref[...] = jnp.concatenate([down, blank], axis=0).astype(jnp.bfloat16)
-    pair_ref[...] = jnp.concatenate([gate, up], axis=0).astype(jnp.bfloat16)
-
-
-def pack_first(gate, up, down):
-    rows, width = gate.shape
-    return pl.pallas_call(
-        pack_first_kernel,
-        out_shape=(
-            jax.ShapeDtypeStruct((rows + -rows % 8, width), gate.dtype),
-            jax.ShapeDtypeStruct((2 * rows, width), gate.dtype),
-        ),
-        name="pack_first",
-    )(gate, up, down)
-
-
-def pack_second_kernel(pair_ref, other_ref, out_ref):
+def pad_kernel(rows_ref, out_ref):
+    rows = rows_ref[...].astype(jnp.float32)
+    blank = jnp.zeros((out_ref.shape[0] - rows.shape[0], rows.shape[1]), jnp.float32)
+    out_ref[...] = jnp.concatenate([rows, blank], axis=0).astype(jnp.bfloat16)
+
+
+def pad_rows(rows):
+    count, width = rows.shape
+    return pl.pallas_call(
+        pad_kernel,
+        out_shape=jax.ShapeDtypeStruct((count + -count % 8, width), rows.dtype),
+        name="pad_rows",
+    )(rows)
+
+
+def pack_kernel(pair_ref, other_ref, out_ref):
     pair, other = pair_ref[...].astype(jnp.float32), other_ref[...].astype(jnp.float32)
     out_ref[...] = jnp.concatenate([pair, other], axis=0).astype(jnp.bfloat16)
 
 
-def pack_second(pair, other):
-    return pl.pallas_call(
-        pack_second_kernel,
+def pack_rows(pair, other):
+    return pl.pallas_call(
+        pack_kernel,
         out_shape=jax.ShapeDtypeStruct((2 * pair.shape[0], pair.shape[1]), pair.dtype),
         compiler_params=SMALL,
-        name="pack_second",
+        name="pack_rows",
     )(pair, other)
 
 
@@ -324,8 +319,8 @@
     offset = lax.axis_index(SEQ) * per_group
     bias_part = lax.dynamic_slice_in_dim(skip_bias, offset, per_group, 0)
 
-    first, pair = pack_first(gate_weight, up_weight, down_weight)
-    own_near = lax.all_gather(first, "z", axis=0, tiled=True)
+    pair = pack_rows(gate_weight, up_weight)
+    own_near = lax.all_gather(pad_rows(down_weight), "z", axis=0, tiled=True)
     edge = projected[:, :, block_len - 2 :].transpose(0, 2, 1).reshape(6, local_width)
     edge = lax.ppermute(
         jnp.pad(edge, ((0, 2), (0, 0))), SEQ, [(i, i + 1) for i in range(groups - 1)]
@@ -339,7 +334,7 @@
     )
     gated, query = make_gated(projected, short_weight, edge)
     other_pair = swap(pair, "xh")
-    second = pack_second(pair, other_pair)
+    second = pack_rows(pair, other_pair)
     gated, taps, second, bias_part = lax.optimization_barrier((gated, taps, second, bias_part))
     here = lax.all_to_all(
         gated.reshape(groups, per_group, block_len), SEQ, split_axis=0, concat_axis=0, tiled=True

time: 185 us -> 185 us (level)
  no operation moved by 1% of the time
where the time goes in v9:
time: 185 us
  blocking collectives  53.7 us (29%)
  waiting for transfers between devices  50.2 us (27%)
  starting transfers between devices  31.2 us (17%)
  Pallas kernels  31.2 us (17%)
  between operations  13.5 us (7%)
  local copies, waits for them, and re-layouts  5.08 us (3%)
    all_to_all x1, blocking collectives, per_device(): lax.all_to_all(partial_sum, TP, split_axis=0, concat_axis=0, tiled=True)  30.5 us
    all_to_all x1, blocking collectives, per_device(): lax.all_to_all(gated.reshape(groups, per_group, block_len), SEQ, split_ax...  23.2 us
    all_to_all x1, waiting for transfers between devices, per_device(): sent = lax.all_to_all(payload, TP, split_axis=0, concat_axis=0, tiled=True)  23.1 us
    all_to_all x1, waiting for transfers between devices, per_device(): lax.all_to_all(mixed_term.transpose(1, 0, 2), SEQ, split_axis=0, concat_a...  18.7 us
    pallas_call x1, Pallas kernels, long_mixing(): pl.pallas_call(conv_kernel, out_shape=jax.ShapeDtypeStruct(gated.shape, j...  13.7 us
    all_to_all x1, starting transfers between devices, per_device(): lax.all_to_all(filter_taps.reshape(groups, per_group, block_len), SEQ, sp...  12.6 us
    pallas_call x1, Pallas kernels, feed_forward(): pl.pallas_call(functools.partial(feed_kernel, (units, block, per_step, fi...  10.4 us
    ppermute x4, waiting for transfers between devices, swap(): return lax.ppermute(values, axis, [(0, 1), (1, 0)])  8.4 us
  transfers between devices with their start and end apart: 10, of which 4 were waited for; matrix products, arithmetic and copies ran while one was open for 2% of the time, Pallas kernels for 10%

profile of v9, /device:TPU:1, one launch (start us, length us, event | category | flops | bytes accessed | tf_op | source)
XLA Modules:
  0.0 184.9 jit_solution(202967773272796301)
XLA Ops:
  6.5 1.7 pad_rows.1
  8.3 12.6 %all-to-all-start = ((bf16[32,16,256]{2,1,0:T(8,128)(2,1)}), bf16[32,16,256]{2,1,0:T(8,128)(2,1)S(1)}, u32[]{:S(2)}, u32[]{:S(2)}) async-start(bf16[32,16,256]{2,1,0:T(8,128)(2,1)} %bitcast.18), calls=%async_computation | async-start | bytes 524288 | tf_op jit(solution)/shard_map/all_to_all | solution.py:328
  20.9 0.9 copy-done.1
  21.8 0.9 copy-done.2
  22.8 3.0 %collective-permute-start.1 = (bf16[44,4096]{1,0:T(8,128)(2,1)S(1)}, bf16[44,4096]{1,0:T(8,128)(2,1)S(1)}, u32[]{:S(2)}, u32[]{:S(2)}) collective-permute-start(bf16[44,4096]{1,0:T(8,128)(2,1)S(1)} %pack_rows.2.pair_ref), channel_id=1, source_target_pairs={{0,128},{128,0},{1,129},{129,1},{2,130},{130,2},{3,131},{131,3},{4... | collective-permute-start | bytes 1081352 | tf_op jit(solution)/shard_map/ppermute | solution.py:308
  25.8 0.2 slice_bitcast_fusion
  26.0 0.2 copy.18
  26.2 3.6 %collective-permute-start = (bf16[8,512]{1,0:T(8,128)(2,1)S(1)}, bf16[8,512]{1,0:T(8,128)(2,1)S(1)}, u32[]{:S(2)}, u32[]{:S(2)}) collective-permute-start(bf16[8,512]{1,0:T(8,128)(2,1)S(1)} %pad.9), channel_id=1, source_target_pairs={{0,8},{8,16},{16,24},{24,32},{32,40},{40,48},{48,56},{56,64},{64,7... | collective-permute-start | bytes 24584 | tf_op jit(solution)/shard_map/ppermute | solution.py:325
  29.9 0.8 dynamic_slice.6.bias_ref
  30.7 1.8 make_gated.1
  32.4 5.0 %collective-permute-done.1.other_ref = bf16[44,4096]{1,0:T(8,128)(2,1)S(1)} collective-permute-done((bf16[44,4096]{1,0:T(8,128)(2,1)S(1)}, bf16[44,4096]{1,0:T(8,128)(2,1)S(1)}, u32[]{:S(2)}, u32[]{:S(2)}) %collective-permute-start.1) | collective-permute-done | bytes 360480 | tf_op jit(solution)/shard_map/ppermute | solution.py:308
  37.5 1.0 pack_rows.3
  38.5 23.2 %all_to_all.25 = bf16[32,16,256]{2,1,0:T(8,128)(2,1)S(1)} all-to-all(bf16[32,16,256]{2,1,0:T(8,128)(2,1)S(1)} %bitcast.14), channel_id=1, replica_groups=mesh['xh'=2,'z'=8,'core'=2,'y'=4,'xl'=2] {'xh','z','core'}, dimensions={0} | all-to-all | bytes 524288 | tf_op jit(solution)/shard_map/all_to_all | solution.py:339
  61.6 0.4 collective-permute-start.2
  62.0 0.3 collective-permute-start.3
  62.4 0.1 copy.20
  62.5 0.1 reshape_reshape.4.taps_ref
  62.6 0.1 copy.25
  62.7 13.7 %long_mixing.1 = bf16[16,32,256]{2,1,0:T(8,128)(2,1)S(1)} custom-call(f32[16]{0:T(128)S(1)} %dynamic_slice.6.bias_ref, bf16[16,32,256]{2,1,0:T(8,128)(2,1)S(1)} %bitcast.16, bf16[16,1,8192]{2,1,0:T(2,128)(2,1)S(1)} %reshape_reshape.4.taps_ref), custom_call_target="tpu_custom_call" | custom-call | flops 8589934592 | bytes 786432 | tf_op jit(solution)/shard_map/long_mixing/pallas_call | solution.py:145
  76.4 0.9 copy.22
  77.3 6.0 %all-to-all-start.2 = ((bf16[32,16,256]{2,1,0:T(8,128)(2,1)}), bf16[32,16,256]{2,1,0:T(8,128)(2,1)S(1)}, u32[]{:S(2)}, u32[]{:S(2)}) async-start(bf16[32,16,256]{2,1,0:T(8,128)(2,1)} %copy.22), calls=%async_computation.2 | async-start | bytes 524288 | tf_op jit(solution)/shard_map/all_to_all | solution.py:352
  83.3 0.8 dynamic_slice.7
  84.1 0.1 copy.23.gain_ref
  84.3 18.7 %all-to-all-done.2 = bf16[32,16,256]{2,1,0:T(8,128)(2,1)S(1)} async-done(((bf16[32,16,256]{2,1,0:T(8,128)(2,1)}), bf16[32,16,256]{2,1,0:T(8,128)(2,1)S(1)}, u32[]{:S(2)}, u32[]{:S(2)}) %all-to-all-start.2) | async-done | bytes 262176 | tf_op jit(solution)/shard_map/all_to_all | solution.py:352
  102.9 1.6 make_payload.1
  104.5 4.5 %all-to-all-start.3 = ((bf16[8,528,256]{2,1,0:T(8,128)(2,1)}), bf16[8,528,256]{2,1,0:T(8,128)(2,1)}, u32[]{:S(2)}, u32[]{:S(2)}) async-start(bf16[8,528,256]{2,1,0:T(8,128)(2,1)} %get-tuple-element.28), calls=%async_computation.3 | async-start | bytes 4325376 | tf_op jit(solution)/shard_map/all_to_all | solution.py:361
  109.0 0.7 collective-permute-start.4
  109.7 3.4 %collective-permute-done.4.p3_ref = bf16[192,4096]{1,0:T(8,128)(2,1)} collective-permute-done((bf16[192,4096]{1,0:T(8,128)(2,1)}, bf16[192,4096]{1,0:T(8,128)(2,1)}, u32[]{:S(2)}, u32[]{:S(2)}) %collective-permute-start.4) | collective-permute-done | bytes 1572896 | tf_op jit(solution)/shard_map/ppermute | solution.py:308
  113.1 23.1 %all-to-all-done.3.sent_ref = bf16[8,528,256]{2,1,0:T(8,128)(2,1)} async-done(((bf16[8,528,256]{2,1,0:T(8,128)(2,1)}), bf16[8,528,256]{2,1,0:T(8,128)(2,1)}, u32[]{:S(2)}, u32[]{:S(2)}) %all-to-all-start.3) | async-done | bytes 2162720 | tf_op jit(solution)/shard_map/all_to_all | solution.py:361
  136.2 10.4 %feed_forward.1 = bf16[8,256,512]{2,1,0:T(8,128)(2,1)} custom-call(s32[1]{0:T(128)} %bitcast.core_ref, bf16[8,528,256]{2,1,0:T(8,128)(2,1)} %all-to-all-done.3.sent_ref, bf16[1408,4096]{1,0:T(8,128)(2,1)} %all-gather.5.cloned.1.call-done.weight_ref, bf16[192,4096]{1,0:T(8,128)(2,1)S(1)} %copy-done.3, bf16[192,4096]{1,0:T(8,128)(2,1)} %collective-permute-done.2.p1_ref, ...), custom_call_target="tpu_custom_call" | custom-call | flops 10000000000 | bytes 30000000 | tf_op jit(solution)/shard_map/feed_forward/pallas_call | solution.py:258
  146.5 30.5 %all_to_all.26.shares_ref = bf16[8,256,512]{2,1,0:T(8,128)(2,1)S(1)} all-to-all(bf16[8,256,512]{2,1,0:T(8,128)(2,1)} %feed_forward.1), channel_id=1, replica_groups=mesh['xh'=2,'z'=8,'core'=2,'y'=4,'xl'=2] {'y','xl'}, dimensions={0} | all-to-all | bytes 4194304 | tf_op jit(solution)/shard_map/all_to_all | solution.py:363
  177.1 1.0 finish.1
  (23 shorter events, 0.2 us)
Async XLA Ops:
  6.5 19.3 %copy-start = (bf16[3,512,256]{2,1,0:T(8,128)(2,1)S(1)}, bf16[3,512,256]{2,1,0:T(8,128)(2,1)}, u32[]{:S(2)}) copy-start(bf16[3,512,256]{2,1,0:T(8,128)(2,1)} %projected_ref.1) | copy-start | bytes 2359300
  6.5 23.3 %copy-start.4 = (f32[3,512,3]{1,2,0:T(4,128)S(1)}, f32[3,512,3]{1,2,0:T(4,128)}, u32[]{:S(2)}) copy-start(f32[3,512,3]{1,2,0:T(4,128)} %param.10) | copy-start | bytes 55300
  6.5 55.1 %all-gather.3.cloned.1.call-start = ((), (), s32[]{:S(2)}) async-start(), calls=%async_computation.5 | async-start | bytes 1769472 | tf_op jit(solution)/shard_map/all_gather | solution.py:323
  8.3 30.2 %all-to-all-start = ((bf16[32,16,256]{2,1,0:T(8,128)(2,1)}), bf16[32,16,256]{2,1,0:T(8,128)(2,1)S(1)}, u32[]{:S(2)}, u32[]{:S(2)}) async-start(bf16[32,16,256]{2,1,0:T(8,128)(2,1)} %bitcast.18), calls=%async_computation | async-start | bytes 524288 | tf_op jit(solution)/shard_map/all_to_all | solution.py:328
  20.9 115.3 %all-gather.5.cloned.1.call-start = ((), (), s32[]{:S(2)}) async-start(), calls=%async_computation.6 | async-start | bytes 12255232 | tf_op jit(solution)/shard_map/all_gather | solution.py:344
  20.9 0.9 copy-start.1
  21.8 0.9 copy-start.2
  22.8 14.6 %collective-permute-start.1 = (bf16[44,4096]{1,0:T(8,128)(2,1)S(1)}, bf16[44,4096]{1,0:T(8,128)(2,1)S(1)}, u32[]{:S(2)}, u32[]{:S(2)}) collective-permute-start(bf16[44,4096]{1,0:T(8,128)(2,1)S(1)} %pack_rows.2.pair_ref), channel_id=1, source_target_pairs={{0,128},{128,0},{1,129},{129,1},{2,130},{130,2},{3,131},{131,3},{4... | collective-permute-start | bytes 1081352 | tf_op jit(solution)/shard_map/ppermute | solution.py:308
  26.2 4.4 %collective-permute-start = (bf16[8,512]{1,0:T(8,128)(2,1)S(1)}, bf16[8,512]{1,0:T(8,128)(2,1)S(1)}, u32[]{:S(2)}, u32[]{:S(2)}) collective-permute-start(bf16[8,512]{1,0:T(8,128)(2,1)S(1)} %pad.9), channel_id=1, source_target_pairs={{0,8},{8,16},{16,24},{24,32},{32,40},{40,48},{48,56},{56,64},{64,7... | collective-permute-start | bytes 24584 | tf_op jit(solution)/shard_map/ppermute | solution.py:325
  61.6 14.8 %collective-permute-start.2 = (bf16[192,4096]{1,0:T(8,128)(2,1)}, bf16[192,4096]{1,0:T(8,128)(2,1)}, u32[]{:S(2)}, u32[]{:S(2)}) collective-permute-start(bf16[192,4096]{1,0:T(8,128)(2,1)} %all-gather.3.cloned.1.call-done.p0_ref), channel_id=1, source_target_pairs={{0,8},{8,0},{1,9},{9,1},{2,10},{10,2},{3,11},{11,3},{4,12},{12,4},... | collective-permute-start | bytes 4718600 | tf_op jit(solution)/shard_map/ppermute | solution.py:308
  62.0 42.5 %collective-permute-start.3 = (bf16[192,4096]{1,0:T(8,128)(2,1)}, bf16[192,4096]{1,0:T(8,128)(2,1)}, u32[]{:S(2)}, u32[]{:S(2)}) collective-permute-start(bf16[192,4096]{1,0:T(8,128)(2,1)} %all-gather.3.cloned.1.call-done.p0_ref), channel_id=1, source_target_pairs={{0,128},{128,0},{1,129},{129,1},{2,130},{130,2},{3,131},{131,3},{4... | collective-permute-start | bytes 4718600 | tf_op jit(solution)/shard_map/ppermute | solution.py:308
  77.3 25.6 %all-to-all-start.2 = ((bf16[32,16,256]{2,1,0:T(8,128)(2,1)}), bf16[32,16,256]{2,1,0:T(8,128)(2,1)S(1)}, u32[]{:S(2)}, u32[]{:S(2)}) async-start(bf16[32,16,256]{2,1,0:T(8,128)(2,1)} %copy.22), calls=%async_computation.2 | async-start | bytes 524288 | tf_op jit(solution)/shard_map/all_to_all | solution.py:352
  104.5 31.7 %copy-start.3 = (bf16[192,4096]{1,0:T(8,128)(2,1)S(1)}, bf16[192,4096]{1,0:T(8,128)(2,1)}, u32[]{:S(2)}) copy-start(bf16[192,4096]{1,0:T(8,128)(2,1)} %all-gather.3.cloned.1.call-done.p0_ref) | copy-start | bytes 4718596
  104.5 31.6 %all-to-all-start.3 = ((bf16[8,528,256]{2,1,0:T(8,128)(2,1)}), bf16[8,528,256]{2,1,0:T(8,128)(2,1)}, u32[]{:S(2)}, u32[]{:S(2)}) async-start(bf16[8,528,256]{2,1,0:T(8,128)(2,1)} %get-tuple-element.28), calls=%async_computation.3 | async-start | bytes 4325376 | tf_op jit(solution)/shard_map/all_to_all | solution.py:361
  109.0 4.1 %collective-permute-start.4 = (bf16[192,4096]{1,0:T(8,128)(2,1)}, bf16[192,4096]{1,0:T(8,128)(2,1)}, u32[]{:S(2)}, u32[]{:S(2)}) collective-permute-start(bf16[192,4096]{1,0:T(8,128)(2,1)} %collective-permute-done.3.p2_ref), channel_id=1, source_target_pairs={{0,8},{8,0},{1,9},{9,1},{2,10},{10,2},{3,11},{11,3},{4,12},{12,4},... | collective-permute-start | bytes 4718600 | tf_op jit(solution)/shard_map/ppermute | solution.py:308
Sparse Core Ops, SparseCore 0:
  9.1 45.0 all-gather.2
  56.1 79.3 all-gather.4

commit v10 on v7

--- a/solution.py
+++ b/solution.py
@@ -349,11 +349,9 @@
     gate_up = lax.all_gather(second, ("z", "core"), axis=0, tiled=True)
 
     here, own_near = lax.optimization_barrier((here, own_near))
-    own_far = swap(own_near, "core")
     near = swap(own_near, "xh")
     taps = taps.transpose(1, 0, 2).reshape(per_group, seq_len)
     mixed_term = long_mixing(here.transpose(1, 0, 2), taps, bias_part)
-    mixed_term, own_far = lax.optimization_barrier((mixed_term, own_far))
     returned = lax.all_to_all(
         mixed_term.transpose(1, 0, 2), SEQ, split_axis=0, concat_axis=0, tiled=True
     )
@@ -361,8 +359,8 @@
         norm_gain, lax.axis_index(TP) * local_width, local_width, 0
     )
     hyena, payload = make_payload(query, returned.reshape(local_width, block_len), gain, members)
-    payload, near = lax.optimization_barrier((payload, near))
-    pieces = (own_near, own_far, near, swap(near, "core"))
+    payload, near, own_near = lax.optimization_barrier((payload, near, own_near))
+    pieces = (own_near, swap(own_near, "core"), near, swap(near, "core"))
     sent = lax.all_to_all(payload, TP, split_axis=0, concat_axis=0, tiled=True)
     partial_sum = feed_forward(sent, gate_up, pieces, core.reshape(1), gate_weight.shape[0])
     shares = lax.all_to_all(partial_sum, TP, split_axis=0, concat_axis=0, tiled=True)

time: 185 us -> 185 us (level)
    all_to_all x1, waiting for transfers between devices: 22.9 us -> 20.3 us  [per_device(): sent = lax.all_to_all(payload, TP, split_axis=0, concat_axis=0, tiled=True)]
  transfers between devices with their start and end apart: 10 -> 10, of which waited for: 4 -> 5; matrix products, arithmetic and copies ran while one was open for 2% -> 2% of each run, Pallas kernels for 10% -> 10%
where the time goes in v10:
time: 185 us
  blocking collectives  54.7 us (30%)
  waiting for transfers between devices  48 us (26%)
  starting transfers between devices  31.6 us (17%)
  Pallas kernels  31.5 us (17%)
  between operations  13.6 us (7%)
  local copies, waits for them, and re-layouts  5.43 us (3%)
    all_to_all x1, blocking collectives, per_device(): lax.all_to_all(partial_sum, TP, split_axis=0, concat_axis=0, tiled=True)  31.1 us
    all_to_all x1, blocking collectives, per_device(): lax.all_to_all(gated.reshape(groups, per_group, block_len), SEQ, split_ax...  23.6 us
    all_to_all x1, waiting for transfers between devices, per_device(): sent = lax.all_to_all(payload, TP, split_axis=0, concat_axis=0, tiled=True)  20.3 us
    all_to_all x1, waiting for transfers between devices, per_device(): lax.all_to_all(mixed_term.transpose(1, 0, 2), SEQ, split_axis=0, concat_a...  17.9 us
    pallas_call x1, Pallas kernels, long_mixing(): pl.pallas_call(conv_kernel, out_shape=jax.ShapeDtypeStruct(gated.shape, j...  13.7 us
    all_to_all x1, starting transfers between devices, per_device(): lax.all_to_all(filter_taps.reshape(groups, per_group, block_len), SEQ, sp...  12.7 us
    pallas_call x1, Pallas kernels, feed_forward(): pl.pallas_call(functools.partial(feed_kernel, (units, block, per_step, fi...  10.4 us
    ppermute x4, waiting for transfers between devices, swap(): return lax.ppermute(values, axis, [(0, 1), (1, 0)])  9.59 us
  transfers between devices with their start and end apart: 10, of which 5 were waited for; matrix products, arithmetic and copies ran while one was open for 2% of the time, Pallas kernels for 10%

profile of v10, /device:TPU:1, one launch (start us, length us, event | category | flops | bytes accessed | tf_op | source)
XLA Modules:
  0.0 184.8 jit_solution(17455784493115817554)
XLA Ops:
  6.5 2.0 %pack_first.1 = (bf16[24,4096]{1,0:T(8,128)(2,1)}, bf16[44,4096]{1,0:T(8,128)(2,1)}) custom-call(bf16[22,4096]{1,0:T(8,128)(2,1)} %gate_ref.1, bf16[22,4096]{1,0:T(8,128)(2,1)} %up_ref.1, bf16[22,4096]{1,0:T(8,128)(2,1)} %down_ref.1), custom_call_target="tpu_custom_call" | custom-call | tf_op jit(solution)/shard_map/pack_first/pallas_call | solution.py:59
  8.6 12.7 %all-to-all-start = ((bf16[32,16,256]{2,1,0:T(8,128)(2,1)}), bf16[32,16,256]{2,1,0:T(8,128)(2,1)S(1)}, u32[]{:S(2)}, u32[]{:S(2)}) async-start(bf16[32,16,256]{2,1,0:T(8,128)(2,1)} %bitcast.18), calls=%async_computation | async-start | bytes 524288 | tf_op jit(solution)/shard_map/all_to_all | solution.py:333
  21.4 3.0 %collective-permute-start.1 = (bf16[44,4096]{1,0:T(8,128)(2,1)}, bf16[44,4096]{1,0:T(8,128)(2,1)S(1)}, u32[]{:S(2)}, u32[]{:S(2)}) collective-permute-start(bf16[44,4096]{1,0:T(8,128)(2,1)} %get-tuple-element.22.pair_ref), channel_id=1, source_target_pairs={{0,128},{128,0},{1,129},{129,1},{2,130},{130,2},{3,131},{131,3},{4... | collective-permute-start | bytes 1081352 | tf_op jit(solution)/shard_map/ppermute | solution.py:313
  24.4 1.2 slice_bitcast_fusion
  25.5 0.2 copy.18
  25.8 3.6 %collective-permute-start = (bf16[8,512]{1,0:T(8,128)(2,1)S(1)}, bf16[8,512]{1,0:T(8,128)(2,1)S(1)}, u32[]{:S(2)}, u32[]{:S(2)}) collective-permute-start(bf16[8,512]{1,0:T(8,128)(2,1)S(1)} %pad.9), channel_id=1, source_target_pairs={{0,8},{8,16},{16,24},{24,32},{32,40},{40,48},{48,56},{56,64},{64,7... | collective-permute-start | bytes 24584 | tf_op jit(solution)/shard_map/ppermute | solution.py:330
  29.4 0.8 dynamic_slice.6.bias_ref
  30.2 1.8 make_gated.1
  32.0 4.4 %collective-permute-done.1.other_ref = bf16[44,4096]{1,0:T(8,128)(2,1)S(1)} collective-permute-done((bf16[44,4096]{1,0:T(8,128)(2,1)}, bf16[44,4096]{1,0:T(8,128)(2,1)S(1)}, u32[]{:S(2)}, u32[]{:S(2)}) %collective-permute-start.1) | collective-permute-done | bytes 360480 | tf_op jit(solution)/shard_map/ppermute | solution.py:313
  36.4 1.0 pack_second.1
  37.4 23.6 %all_to_all.25 = bf16[32,16,256]{2,1,0:T(8,128)(2,1)S(1)} all-to-all(bf16[32,16,256]{2,1,0:T(8,128)(2,1)S(1)} %bitcast.14), channel_id=1, replica_groups=mesh['xh'=2,'z'=8,'core'=2,'y'=4,'xl'=2] {'xh','z','core'}, dimensions={0} | all-to-all | bytes 524288 | tf_op jit(solution)/shard_map/all_to_all | solution.py:344
  61.0 0.2 collective-permute-start.2
  61.2 0.1 copy.20
  61.3 0.1 reshape_reshape.4.taps_ref
  61.5 0.1 copy.25
  61.6 13.7 %long_mixing.1 = bf16[16,32,256]{2,1,0:T(8,128)(2,1)S(1)} custom-call(f32[16]{0:T(128)S(1)} %dynamic_slice.6.bias_ref, bf16[16,32,256]{2,1,0:T(8,128)(2,1)S(1)} %bitcast.15, bf16[16,1,8192]{2,1,0:T(2,128)(2,1)S(1)} %reshape_reshape.4.taps_ref), custom_call_target="tpu_custom_call" | custom-call | flops 8589934592 | bytes 786432 | tf_op jit(solution)/shard_map/long_mixing/pallas_call | solution.py:150
  75.3 0.9 copy.22
  76.1 6.9 %all-to-all-start.2 = ((bf16[32,16,256]{2,1,0:T(8,128)(2,1)}), bf16[32,16,256]{2,1,0:T(8,128)(2,1)S(1)}, u32[]{:S(2)}, u32[]{:S(2)}) async-start(bf16[32,16,256]{2,1,0:T(8,128)(2,1)} %copy.22), calls=%async_computation.2 | async-start | bytes 524288 | tf_op jit(solution)/shard_map/all_to_all | solution.py:355
  83.0 0.8 dynamic_slice.7
  83.8 0.1 copy.23.gain_ref
  83.9 17.9 %all-to-all-done.2 = bf16[32,16,256]{2,1,0:T(8,128)(2,1)S(1)} async-done(((bf16[32,16,256]{2,1,0:T(8,128)(2,1)}), bf16[32,16,256]{2,1,0:T(8,128)(2,1)S(1)}, u32[]{:S(2)}, u32[]{:S(2)}) %all-to-all-start.2) | async-done | bytes 262176 | tf_op jit(solution)/shard_map/all_to_all | solution.py:355
  101.9 1.6 make_payload.1
  103.5 4.5 %all-to-all-start.3 = ((bf16[8,528,256]{2,1,0:T(8,128)(2,1)}), bf16[8,528,256]{2,1,0:T(8,128)(2,1)}, u32[]{:S(2)}, u32[]{:S(2)}) async-start(bf16[8,528,256]{2,1,0:T(8,128)(2,1)} %get-tuple-element.30), calls=%async_computation.3 | async-start | bytes 4325376 | tf_op jit(solution)/shard_map/all_to_all | solution.py:364
  108.0 0.6 collective-permute-start.3
  108.5 0.1 collective-permute-start.4
  108.6 5.2 %collective-permute-done.3.p1_ref = bf16[192,4096]{1,0:T(8,128)(2,1)S(1)} collective-permute-done((bf16[192,4096]{1,0:T(8,128)(2,1)S(1)}, bf16[192,4096]{1,0:T(8,128)(2,1)S(1)}, u32[]{:S(2)}, u32[]{:S(2)}) %collective-permute-start.3) | collective-permute-done | bytes 1572896 | tf_op jit(solution)/shard_map/ppermute | solution.py:313
  113.8 1.2 copy-done.4
  115.0 20.3 %all-to-all-done.3.sent_ref = bf16[8,528,256]{2,1,0:T(8,128)(2,1)} async-done(((bf16[8,528,256]{2,1,0:T(8,128)(2,1)}), bf16[8,528,256]{2,1,0:T(8,128)(2,1)}, u32[]{:S(2)}, u32[]{:S(2)}) %all-to-all-start.3) | async-done | bytes 2162720 | tf_op jit(solution)/shard_map/all_to_all | solution.py:364
  135.3 0.1 all-gather.5.cloned.1.call-done.weight_ref
  135.4 10.4 %feed_forward.1 = bf16[8,256,512]{2,1,0:T(8,128)(2,1)} custom-call(s32[1]{0:T(128)} %bitcast.core_ref, bf16[8,528,256]{2,1,0:T(8,128)(2,1)} %all-to-all-done.3.sent_ref, bf16[1408,4096]{1,0:T(8,128)(2,1)} %all-gather.5.cloned.1.call-done.weight_ref, bf16[192,4096]{1,0:T(8,128)(2,1)S(1)} %copy-done.2, bf16[192,4096]{1,0:T(8,128)(2,1)} %copy-done.4, ...), custom_call_target="tpu_custom_call" | custom-call | flops 10000000000 | bytes 30000000 | tf_op jit(solution)/shard_map/feed_forward/pallas_call | solution.py:263
  145.8 31.1 %all_to_all.26.shares_ref = bf16[8,256,512]{2,1,0:T(8,128)(2,1)S(1)} all-to-all(bf16[8,256,512]{2,1,0:T(8,128)(2,1)} %feed_forward.1), channel_id=1, replica_groups=mesh['xh'=2,'z'=8,'core'=2,'y'=4,'xl'=2] {'y','xl'}, dimensions={0} | all-to-all | bytes 4194304 | tf_op jit(solution)/shard_map/all_to_all | solution.py:366
  176.9 1.0 finish.1
  (22 shorter events, 0.1 us)
Async XLA Ops:
  6.5 23.7 %copy-start = (bf16[3,512,256]{2,1,0:T(8,128)(2,1)S(1)}, bf16[3,512,256]{2,1,0:T(8,128)(2,1)}, u32[]{:S(2)}) copy-start(bf16[3,512,256]{2,1,0:T(8,128)(2,1)} %projected_ref.1) | copy-start | bytes 2359300
  6.5 22.9 %copy-start.3 = (f32[3,512,3]{1,2,0:T(4,128)S(1)}, f32[3,512,3]{1,2,0:T(4,128)}, u32[]{:S(2)}) copy-start(f32[3,512,3]{1,2,0:T(4,128)} %param.10) | copy-start | bytes 55300
  6.5 54.5 %all-gather.3.cloned.1.call-start = ((), (), s32[]{:S(2)}) async-start(), calls=%async_computation.5 | async-start | bytes 1769472 | tf_op jit(solution)/shard_map/all_gather | solution.py:328
  8.6 27.8 %copy-start.1 = (bf16[44,4096]{1,0:T(8,128)(2,1)S(1)}, bf16[44,4096]{1,0:T(8,128)(2,1)}, u32[]{:S(2)}) copy-start(bf16[44,4096]{1,0:T(8,128)(2,1)} %get-tuple-element.22.pair_ref) | copy-start | bytes 1081348
  8.6 28.8 %all-to-all-start = ((bf16[32,16,256]{2,1,0:T(8,128)(2,1)}), bf16[32,16,256]{2,1,0:T(8,128)(2,1)S(1)}, u32[]{:S(2)}, u32[]{:S(2)}) async-start(bf16[32,16,256]{2,1,0:T(8,128)(2,1)} %bitcast.18), calls=%async_computation | async-start | bytes 524288 | tf_op jit(solution)/shard_map/all_to_all | solution.py:333
  21.3 114.1 %all-gather.5.cloned.1.call-start = ((), (), s32[]{:S(2)}) async-start(), calls=%async_computation.6 | async-start | bytes 12255232 | tf_op jit(solution)/shard_map/all_gather | solution.py:349
  21.4 15.0 %collective-permute-start.1 = (bf16[44,4096]{1,0:T(8,128)(2,1)}, bf16[44,4096]{1,0:T(8,128)(2,1)S(1)}, u32[]{:S(2)}, u32[]{:S(2)}) collective-permute-start(bf16[44,4096]{1,0:T(8,128)(2,1)} %get-tuple-element.22.pair_ref), channel_id=1, source_target_pairs={{0,128},{128,0},{1,129},{129,1},{2,130},{130,2},{3,131},{131,3},{4... | collective-permute-start | bytes 1081352 | tf_op jit(solution)/shard_map/ppermute | solution.py:313
  25.8 4.4 %collective-permute-start = (bf16[8,512]{1,0:T(8,128)(2,1)S(1)}, bf16[8,512]{1,0:T(8,128)(2,1)S(1)}, u32[]{:S(2)}, u32[]{:S(2)}) collective-permute-start(bf16[8,512]{1,0:T(8,128)(2,1)S(1)} %pad.9), channel_id=1, source_target_pairs={{0,8},{8,16},{16,24},{24,32},{32,40},{40,48},{48,56},{56,64},{64,7... | collective-permute-start | bytes 24584 | tf_op jit(solution)/shard_map/ppermute | solution.py:330
  61.0 42.4 %collective-permute-start.2 = (bf16[192,4096]{1,0:T(8,128)(2,1)}, bf16[192,4096]{1,0:T(8,128)(2,1)}, u32[]{:S(2)}, u32[]{:S(2)}) collective-permute-start(bf16[192,4096]{1,0:T(8,128)(2,1)} %all-gather.3.cloned.1.call-done.p0_ref), channel_id=1, source_target_pairs={{0,128},{128,0},{1,129},{129,1},{2,130},{130,2},{3,131},{131,3},{4... | collective-permute-start | bytes 4718600 | tf_op jit(solution)/shard_map/ppermute | solution.py:313
  76.1 25.7 %all-to-all-start.2 = ((bf16[32,16,256]{2,1,0:T(8,128)(2,1)}), bf16[32,16,256]{2,1,0:T(8,128)(2,1)S(1)}, u32[]{:S(2)}, u32[]{:S(2)}) async-start(bf16[32,16,256]{2,1,0:T(8,128)(2,1)} %copy.22), calls=%async_computation.2 | async-start | bytes 524288 | tf_op jit(solution)/shard_map/all_to_all | solution.py:355
  103.5 4.5 %copy-start.2 = (bf16[192,4096]{1,0:T(8,128)(2,1)S(1)}, bf16[192,4096]{1,0:T(8,128)(2,1)}, u32[]{:S(2)}) copy-start(bf16[192,4096]{1,0:T(8,128)(2,1)} %all-gather.3.cloned.1.call-done.p0_ref) | copy-start | bytes 4718596
  103.5 31.8 %all-to-all-start.3 = ((bf16[8,528,256]{2,1,0:T(8,128)(2,1)}), bf16[8,528,256]{2,1,0:T(8,128)(2,1)}, u32[]{:S(2)}, u32[]{:S(2)}) async-start(bf16[8,528,256]{2,1,0:T(8,128)(2,1)} %get-tuple-element.30), calls=%async_computation.3 | async-start | bytes 4325376 | tf_op jit(solution)/shard_map/all_to_all | solution.py:364
  108.0 5.8 %collective-permute-start.3 = (bf16[192,4096]{1,0:T(8,128)(2,1)S(1)}, bf16[192,4096]{1,0:T(8,128)(2,1)S(1)}, u32[]{:S(2)}, u32[]{:S(2)}) collective-permute-start(bf16[192,4096]{1,0:T(8,128)(2,1)S(1)} %copy-done.2), channel_id=1, source_target_pairs={{0,8},{8,0},{1,9},{9,1},{2,10},{10,2},{3,11},{11,3},{4,12},{12,4},... | collective-permute-start | bytes 4718600 | tf_op jit(solution)/shard_map/ppermute | solution.py:313
  108.5 6.5 %collective-permute-start.4 = (bf16[192,4096]{1,0:T(8,128)(2,1)}, bf16[192,4096]{1,0:T(8,128)(2,1)}, u32[]{:S(2)}, u32[]{:S(2)}) collective-permute-start(bf16[192,4096]{1,0:T(8,128)(2,1)} %collective-permute-done.2.p2_ref), channel_id=1, source_target_pairs={{0,8},{8,0},{1,9},{9,1},{2,10},{10,2},{3,11},{11,3},{4,12},{12,4},... | collective-permute-start | bytes 4718600 | tf_op jit(solution)/shard_map/ppermute | solution.py:313
  113.8 1.2 copy-start.4
Sparse Core Ops, SparseCore 0:
  9.1 45.2 all-gather.2
  56.3 79.1 all-gather.4
